TPU v7x, 32 devices: a whole 2x2x4 slice. The times are simulated.
32 devices in a mesh: section: 8 (over y, x, core), expert: 4 (over z).
Axes of the slice: x: 2, y: 2, z: 4, core: 2. Of those that a mesh axis runs over, the one named last changes fastest.
Arguments:
- forward_input: bfloat16 [8, 512, 2048], P('section', 'expert'), may hold values from -6 to 6
- forward_routes: int32 [8, 512, 8], P('section', 'expert'), may hold values from 0 to 127, as said below
- forward_shares: float32 [8, 512, 8], P('section', 'expert'), may hold values from 0.1 to 1
- backward_input: bfloat16 [8, 512, 2048], P('section', 'expert'), may hold values from -6 to 6
- backward_routes: int32 [8, 512, 8], P('section', 'expert'), may hold values from 0 to 127, as said below
- backward_shares: float32 [8, 512, 8], P('section', 'expert'), may hold values from 0.1 to 1
- output_grad: bfloat16 [8, 512, 2048], P('section', 'expert'), may hold values from -6 to 6
- norm_gain: float32 [8, 2048], P('section'), may hold values from 0.5 to 1.5
- gate_weight: bfloat16 [8, 3072, 2048], P('section', 'expert'), may hold values from -0.125 to 0.125
- up_weight: bfloat16 [8, 3072, 2048], P('section', 'expert'), may hold values from -0.125 to 0.125
- down_weight: bfloat16 [8, 3072, 2048], P('section', 'expert'), may hold values from -0.15625 to 0.15625
Outputs:
- next_input: bfloat16 [8, 512, 2048], P('section', 'expert')
- previous_gradient: bfloat16 [8, 512, 2048], P('section', 'expert')
Inputs may be any that keep to these rules, and one draw needn't show every extreme that they name: `forward_routes`: each token names 8 different experts. Among the 128 tokens of one device, at most 16 name any one expert below 2; in every draw some section has every device sending exactly 16 tokens to one expert below 2. `backward_routes`: as for forward_routes.
All inputs are finite; a program needn't handle non-finite values.
Results may differ from a plain program's by a relative error of at most 0.007.
Values may be sent and summed in bfloat16 or wider, within the bound.
No kernel may reach another device: no remote copies, remote signals or barrier semaphores. Data moves between devices by JAX's collectives and lax.ppermute only.
A program may use at most 64 MiB of HBM per device.

v0:
```python
import jax
import jax.numpy as jnp
from jax import lax
from jax.sharding import PartitionSpec as P

EF = 2
CAP = 16


EPSILON = 1e-06


def passed_along(block, axis, distance):
    devices = range(lax.axis_size(axis))
    route = [((i - distance) % len(devices), i) for i in devices]
    return lax.ppermute(block, axis, route)


def route_tables(route_ids, shares):
    hosted = jnp.arange(EF, dtype=jnp.int32)
    match = route_ids[:, :, None] == hosted
    member = jnp.any(match, axis=1)
    weight = jnp.sum(jnp.where(match, shares[:, :, None], 0.0), axis=1)
    member_int = member.astype(jnp.int32)
    rank = jnp.cumsum(member_int, axis=0) - member_int
    slots = jnp.arange(CAP, dtype=jnp.int32)
    placed = member.T[:, None, :] & (rank.T[:, None, :] == slots[None, :, None])
    table = placed.astype(jnp.float32)
    return (table, table * weight.T[:, None, :])


def normalize(rows, gain):
    values = rows.astype(jnp.float32)
    scale = lax.rsqrt(jnp.mean(values * values, axis=-1, keepdims=True) + EPSILON)
    unit = values * scale
    return (unit, scale, (unit * gain).astype(jnp.bfloat16))


def project(left, right):
    return lax.dot_general(
        left, right, (((1,), (1,)), ((), ())), preferred_element_type=jnp.float32
    )


def slice_forward(slots_in, gate_rows, up_rows, down_rows):
    gate = project(slots_in, gate_rows)
    upper = project(slots_in, up_rows)
    hidden = (jax.nn.silu(gate) * upper).astype(jnp.bfloat16)
    return jnp.dot(hidden, down_rows, preferred_element_type=jnp.float32).astype(jnp.bfloat16)


def slice_backward(slots_in, slot_grad, gate_rows, up_rows, down_rows):
    gate = project(slots_in, gate_rows)
    upper = project(slots_in, up_rows)
    sigma = jax.nn.sigmoid(gate)
    hidden_grad = project(slot_grad, down_rows)
    gate_grad = (hidden_grad * upper * sigma * (1.0 + gate * (1.0 - sigma))).astype(jnp.bfloat16)
    upper_grad = (hidden_grad * gate * sigma).astype(jnp.bfloat16)
    total = jnp.dot(gate_grad, gate_rows, preferred_element_type=jnp.float32)
    total = total + jnp.dot(upper_grad, up_rows, preferred_element_type=jnp.float32)
    return total.astype(jnp.bfloat16)


def on_device(
    forward_input,
    forward_routes,
    forward_shares,
    backward_input,
    backward_routes,
    backward_shares,
    output_grad,
    norm_gain,
    gate_weight,
    up_weight,
    down_weight,
):
    devices = lax.axis_size("expert")
    group = devices // EF
    owner = lax.axis_index("expert") // group
    forward_rows = forward_input[0]
    backward_rows = backward_input[0]
    grad_rows = output_grad[0]
    gain = norm_gain[0]
    gate_rows = gate_weight[0]
    up_rows = up_weight[0]
    down_rows = down_weight[0]
    width = forward_rows.shape[1]
    forward_unit, forward_scale, forward_normed = normalize(forward_rows, gain)
    backward_unit, backward_scale, backward_normed = normalize(backward_rows, gain)
    forward_table, forward_weighted = route_tables(forward_routes[0], forward_shares[0])
    backward_table, backward_weighted = route_tables(backward_routes[0], backward_shares[0])
    forward_slots = jnp.einsum(
        "ect,td->ecd",
        forward_table.astype(jnp.bfloat16),
        forward_normed,
        preferred_element_type=jnp.float32,
    ).astype(jnp.bfloat16)
    backward_slots = jnp.einsum(
        "ect,td->ecd",
        backward_table.astype(jnp.bfloat16),
        backward_normed,
        preferred_element_type=jnp.float32,
    ).astype(jnp.bfloat16)
    grad_slots = jnp.einsum(
        "ect,td->ecd",
        backward_weighted,
        grad_rows.astype(jnp.float32),
        precision=lax.Precision.HIGHEST,
    ).astype(jnp.bfloat16)
    gathered = (
        lax.all_gather(forward_slots[None], "expert", axis=0, tiled=True),
        lax.all_gather(backward_slots[None], "expert", axis=0, tiled=True),
        lax.all_gather(grad_slots[None], "expert", axis=0, tiled=True),
    )
    received = tuple(
        (lax.dynamic_index_in_dim(piece, owner, 1, keepdims=False) for piece in gathered)
    )
    rows_in = devices * CAP
    slots_f = received[0].reshape(rows_in, width)
    slots_b = received[1].reshape(rows_in, width)
    slots_g = received[2].reshape(rows_in, width)
    forward_part = slice_forward(slots_f, gate_rows, up_rows, down_rows).reshape(
        devices, CAP, width
    )
    backward_part = slice_backward(slots_b, slots_g, gate_rows, up_rows, down_rows).reshape(
        devices, CAP, width
    )
    select = (jnp.arange(EF) == owner).astype(jnp.bfloat16)[None, :, None, None]
    totals = (
        lax.psum_scatter(
            forward_part[:, None] * select, "expert", scatter_dimension=0, tiled=True
        ).astype(jnp.float32),
        lax.psum_scatter(
            backward_part[:, None] * select, "expert", scatter_dimension=0, tiled=True
        ).astype(jnp.float32),
    )
    forward_total = totals[0][0]
    backward_total = totals[1][0]
    mixed = jnp.einsum(
        "ect,ecd->td", forward_weighted, forward_total, precision=lax.Precision.HIGHEST
    )
    next_rows = (forward_rows.astype(jnp.float32) + mixed).astype(jnp.bfloat16)
    normed_grad = jnp.einsum(
        "ect,ecd->td", backward_table, backward_total, precision=lax.Precision.HIGHEST
    )
    scaled = normed_grad * gain
    input_grad = backward_scale * (
        scaled - backward_unit * jnp.mean(scaled * backward_unit, axis=-1, keepdims=True)
    )
    previous_rows = (grad_rows.astype(jnp.float32) + input_grad).astype(jnp.bfloat16)
    next_input = passed_along(next_rows[None], "section", 1)
    previous_gradient = passed_along(previous_rows[None], "section", -1)
    return (next_input, previous_gradient)


def solution(mesh):
    in_specs = (
        P("section", "expert", None),
        P("section", "expert", None),
        P("section", "expert", None),
        P("section", "expert", None),
        P("section", "expert", None),
        P("section", "expert", None),
        P("section", "expert", None),
        P("section", None),
        P("section", "expert", None),
        P("section", "expert", None),
        P("section", "expert", None),
    )
    out_specs = (P("section", "expert", None), P("section", "expert", None))
    return jax.shard_map(
        on_device, mesh=mesh, in_specs=in_specs, out_specs=out_specs, check_vma=False
    )
```

profile of v0, /device:TPU:0, one launch (start us, length us, event | category | flops | bytes accessed | tf_op | source)
XLA Modules:
  0.0 156.3 jit_solution(15306840720465346925)
XLA Ops:
  7.2 0.0 copy-start
  7.2 0.0 copy-start.8
  7.2 0.0 reduce-scatter.3.cloned.1.call-start
  7.3 0.9 fusion.106
  8.1 0.7 fusion.100
  8.9 1.2 fusion.57
  10.1 1.2 fusion.56
  11.4 0.7 select_reduce_fusion
  12.1 0.1 copy.37
  12.2 0.2 reduce_window_sum.21
  12.4 0.1 copy.38
  12.4 0.1 copy.39
  12.6 0.2 reduce_window_sum.23
  12.7 0.1 copy.40
  12.8 0.0 copy-start.5
  12.8 1.5 convolution_convert_fusion
  14.3 18.0 %all-gather.2 = bf16[8,16,2048]{2,1,0:T(8,128)(2,1)} all-gather(bf16[2,16,2048]{2,1,0:T(8,128)(2,1)S(1)} %convolution_convert_fusion), channel_id=4, replica_groups=mesh['section'=8,'expert'=4] {'expert'}, dimensions={0}, use_global_device_ids=true | all-gather | bytes 655360 | tf_op jit(solution)/shard_map/all_gather | solution.py:112
  32.3 0.0 copy-done.8
  32.3 1.4 convolution_convert_fusion.2
  33.6 17.1 %all-gather = bf16[8,16,2048]{2,1,0:T(8,128)(2,1)} all-gather(bf16[2,16,2048]{2,1,0:T(8,128)(2,1)S(1)} %convolution_convert_fusion.2), channel_id=2, replica_groups=mesh['section'=8,'expert'=4] {'expert'}, dimensions={0}, use_global_device_ids=true | all-gather | bytes 655360 | tf_op jit(solution)/shard_map/all_gather | solution.py:111
  50.8 0.0 copy-done.5
  50.8 0.3 convolution_convert_fusion.1
  51.1 16.6 %all-gather.1 = bf16[8,16,2048]{2,1,0:T(8,128)(2,1)} all-gather(bf16[2,16,2048]{2,1,0:T(8,128)(2,1)S(1)} %convolution_convert_fusion.1), channel_id=3, replica_groups=mesh['section'=8,'expert'=4] {'expert'}, dimensions={0}, use_global_device_ids=true | all-gather | bytes 655360 | tf_op jit(solution)/shard_map/all_gather | solution.py:113
  67.7 0.0 copy-start.6
  67.7 0.0 copy-start.1
  67.7 1.1 constant_dynamic-slice_fusion.2
  68.9 3.7 %fusion.14 = f32[64,768]{1,0:T(8,128)} fusion(bf16[64,2048]{1,0:T(8,128)(2,1)S(1)} %bitcast.121, bf16[1,768,2048]{2,1,0:T(8,128)(2,1)} %param.19), kind=kOutput, calls=%fused_computation.14 | convolution fusion | flops 201326592 | bytes 3604480 | tf_op jit(solution)/shard_map/dot_general | solution.py:40
  72.5 0.0 copy-start.2
  72.6 0.0 copy-done.6
  72.6 1.1 constant_dynamic-slice_fusion
  73.7 0.0 copy-start.3
  73.7 0.0 copy-done.1
  73.7 1.8 %fusion.12 = f32[64,768]{1,0:T(8,128)} fusion(bf16[64,2048]{1,0:T(8,128)(2,1)S(1)} %bitcast.123, bf16[1,768,2048]{2,1,0:T(8,128)(2,1)S(1)} %copy-done.1), kind=kOutput, calls=%fused_computation.12 | convolution fusion | flops 201326592 | bytes 3604480 | tf_op jit(solution)/shard_map/dot_general | solution.py:40
  75.5 0.0 copy-done.3
  75.5 0.0 copy-done.2
  75.5 1.7 %fusion = f32[64,768]{1,0:T(8,128)} fusion(bf16[64,2048]{1,0:T(8,128)(2,1)S(1)} %bitcast.128, bf16[1,768,2048]{2,1,0:T(8,128)(2,1)S(1)} %copy-done.2), kind=kOutput, calls=%fused_computation | convolution fusion | flops 201326592 | bytes 3604480 | tf_op jit(solution)/shard_map/dot_general | solution.py:40
  77.2 0.0 copy-done
  77.2 4.8 %fusion.26 = bf16[64,2048]{1,0:T(8,128)(2,1)} fusion(bf16[1,768,2048]{2,1,0:T(8,128)(2,1)} %param.21, bf16[64,2048]{1,0:T(8,128)(2,1)S(1)} %bitcast.122, bf16[1,768,2048]{2,1,0:T(8,128)(2,1)S(1)} %copy-done, f32[64,768]{1,0:T(8,128)} %fusion.14), kind=kOutput, calls=%fused_computation.24 | convolution fusion | flops 403079168 | bytes 7012352 | tf_op jit(solution)/shard_map/dot_general | solution.py:49
  82.0 0.0 copy-start.4
  82.0 2.5 %fusion.4 = f32[64,2048]{1,0:T(8,128)} fusion(bf16[1,768,2048]{2,1,0:T(8,128)(2,1)S(1)} %copy-done, f32[64,768]{1,0:T(8,128)} %fusion, f32[64,768]{1,0:T(8,128)} %fusion.12), kind=kOutput, calls=%fused_computation.4 | convolution fusion | flops 201621504 | bytes 4063232 | tf_op jit(solution)/shard_map/dot_general | solution.py:60
  84.5 0.0 copy-done.4
  84.5 0.0 copy-start.7
  84.5 0.0 copy-start.9
  84.5 5.0 %fusion.23 = bf16[64,2048]{1,0:T(8,128)(2,1)} fusion(f32[64,2048]{1,0:T(8,128)} %fusion.4, bf16[1,768,2048]{2,1,0:T(8,128)(2,1)} %param.19, f32[64,768]{1,0:T(8,128)} %fusion, bf16[64,2048]{1,0:T(8,128)(2,1)S(1)} %bitcast.124, bf16[1,768,2048]{2,1,0:T(8,128)(2,1)S(1)} %copy-done, f32[64,768]{1,0:T(8,128)} %fusion.12), kind=kOutput, calls=%fused_computation.23 | convolution fusion | flops 403406848 | bytes 7733248 | tf_op jit(solution)/shard_map/dot_general | solution.py:59
  89.6 2.1 %broadcast_multiply_fusion = (bf16[4,2,16,2048]{3,2,1,0:T(8,128)(2,1)}, bf16[4,2,16,2048]{3,2,1,0:T(8,128)(2,1)}) fusion(bf16[4,16,2048]{2,1,0:T(8,128)(2,1)} %bitcast.130, bf16[2]{0:T(256)(128)(2,1)S(1)} %compare_convert_fusion, bf16[4,16,2048]{2,1,0:T(8,128)(2,1)} %bitcast.129), kind=kLoop, calls=%fused_computation.61 | loop fusion | flops 524288 | bytes 1572868 | tf_op jit(solution)/shard_map/mul | solution.py:134
  91.7 0.0 reduce-scatter.3.cloned.1.call-update
  91.7 0.0 reduce-scatter.5.cloned.1.call-start
  91.8 0.7 reduce-scatter.5.cloned.1.call-update
  92.5 0.0 copy-done.7
  92.5 0.0 copy-done.9
  92.5 21.5 %reduce-scatter.3.cloned.1.call-done = bf16[1,2,16,2048]{3,2,1,0:T(8,128)(2,1)} async-done(((bf16[4,2,16,2048]{3,2,1,0:T(8,128)(2,1)}), bf16[1,2,16,2048]{3,2,1,0:T(8,128)(2,1)}) %reduce-scatter.3.cloned.1.call-update) | async-done | bytes 131088 | tf_op jit(solution)/shard_map/reduce_scatter | solution.py:130
  114.0 2.6 %fusion.22 = bf16[1,128,2048]{2,1,0:T(8,128)(2,1)} fusion(bf16[1,128,2048]{2,1,0:T(8,128)(2,1)} %param.11, bf16[1,2,16,2048]{3,2,1,0:T(8,128)(2,1)} %reduce-scatter.3.cloned.1.call-done, f32[2,128]{1,0:T(2,128)S(1)} %bitcast.146, s32[2,128]{1,0:T(2,128)S(1)} %bitcast_subtract_fusion.1, pred[2,128]{1,0:T(4,128)(4,1)S(1)} %bitcast.142), kind=kOutput, calls=%fused_computation.22 | convolution fusion | flops 101462016 | bytes 1181952 | tf_op jit(solution)/shard_map/ect,ecd->td/dot_general | solution.py:139
  116.5 0.0 collective-permute-start
  116.5 20.2 %reduce-scatter.5.cloned.1.call-done = bf16[1,2,16,2048]{3,2,1,0:T(8,128)(2,1)} async-done(((bf16[4,2,16,2048]{3,2,1,0:T(8,128)(2,1)}), bf16[1,2,16,2048]{3,2,1,0:T(8,128)(2,1)}) %reduce-scatter.5.cloned.1.call-update) | async-done | bytes 131088 | tf_op jit(solution)/shard_map/reduce_scatter | solution.py:133
  136.8 1.5 fusion.51
  138.3 1.6 %fusion.66 = bf16[1,128,2048]{2,1,0:T(8,128)(2,1)S(1)} fusion(f32[128,2048]{1,0:T(8,128)S(1)} %get-tuple-element.5, bf16[1,128,2048]{2,1,0:T(8,128)(2,1)} %param.14, bf16[1,128,2048]{2,1,0:T(8,128)(2,1)} %param.17, f32[128]{0:T(128)S(1)} %broadcast_multiply_fusion.2, f32[128]{0:T(128)S(1)} %add_rsqrt_fusion), kind=kLoop, calls=%fused_computation.52 | loop fusion | flops 2097152 | bytes 2622464 | tf_op jit(solution)/shard_map/broadcast_in_dim | solution.py:152
  139.9 0.1 collective-permute-start.1
  140.1 0.0 collective-permute-done
  140.1 6.7 %collective-permute-done.1 = bf16[1,128,2048]{2,1,0:T(8,128)(2,1)S(1)} collective-permute-done((bf16[1,128,2048]{2,1,0:T(8,128)(2,1)S(1)}, bf16[1,128,2048]{2,1,0:T(8,128)(2,1)S(1)}, u32[]{:S(2)}, u32[]{:S(2)}) %collective-permute-start.1) | collective-permute-done | bytes 524320 | tf_op jit(solution)/shard_map/ppermute | solution.py:16
  146.8 1.9 %copy.43 = bf16[1,128,2048]{2,1,0:T(8,128)(2,1)} copy(bf16[1,128,2048]{2,1,0:T(8,128)(2,1)} %collective-permute-done) | data formatting | bytes 1048576
  148.7 0.8 copy.44
  (9 shorter events, 0.1 us)
Async XLA Ops:
  7.2 70.1 %copy-start = (bf16[1,768,2048]{2,1,0:T(8,128)(2,1)S(1)}, bf16[1,768,2048]{2,1,0:T(8,128)(2,1)}, u32[]{:S(2)}) copy-start(bf16[1,768,2048]{2,1,0:T(8,128)(2,1)} %param.20) | copy-start | bytes 9437188
  7.2 25.1 %copy-start.8 = (f32[1,2048]{1,0:T(1,128)S(1)}, f32[1,2048]{1,0:T(1,128)}, u32[]{:S(2)}) copy-start(f32[1,2048]{1,0:T(1,128)} %param.18) | copy-start | bytes 24580
  7.2 106.8 %reduce-scatter.3.cloned.1.call-start = ((), (), s32[]{:S(2)}) async-start(), calls=%async_computation.2 | async-start | bytes 655360 | tf_op jit(solution)/shard_map/reduce_scatter | solution.py:130
  12.8 38.0 %copy-start.5 = (bf16[1,128,2048]{2,1,0:T(8,128)(2,1)S(1)}, bf16[1,128,2048]{2,1,0:T(8,128)(2,1)}, u32[]{:S(2)}) copy-start(bf16[1,128,2048]{2,1,0:T(8,128)(2,1)} %param.17) | copy-start | bytes 1572868
  67.7 4.8 %copy-start.6 = (bf16[8,16,2048]{2,1,0:T(8,128)(2,1)S(1)}, bf16[8,16,2048]{2,1,0:T(8,128)(2,1)}, u32[]{:S(2)}) copy-start(bf16[8,16,2048]{2,1,0:T(8,128)(2,1)} %all-gather.2) | copy-start | bytes 1572868
  67.7 6.0 %copy-start.1 = (bf16[1,768,2048]{2,1,0:T(8,128)(2,1)S(1)}, bf16[1,768,2048]{2,1,0:T(8,128)(2,1)}, u32[]{:S(2)}) copy-start(bf16[1,768,2048]{2,1,0:T(8,128)(2,1)} %param.19) | copy-start | bytes 9437188
  72.5 2.9 %copy-start.2 = (bf16[1,768,2048]{2,1,0:T(8,128)(2,1)S(1)}, bf16[1,768,2048]{2,1,0:T(8,128)(2,1)}, u32[]{:S(2)}) copy-start(bf16[1,768,2048]{2,1,0:T(8,128)(2,1)} %param.21) | copy-start | bytes 9437188
  73.7 1.8 %copy-start.3 = (bf16[4,1,16,2048]{3,2,1,0:T(8,128)(2,1)}, bf16[4,1,16,2048]{3,2,1,0:T(8,128)(2,1)S(1)}, u32[]{:S(2)}) copy-start(bf16[4,1,16,2048]{3,2,1,0:T(8,128)(2,1)S(1)} %get-tuple-element.6) | copy-start | bytes 786436
  82.0 2.5 %copy-start.4 = (bf16[4,1,16,2048]{3,2,1,0:T(8,128)(2,1)S(1)}, bf16[4,1,16,2048]{3,2,1,0:T(8,128)(2,1)}, u32[]{:S(2)}) copy-start(bf16[4,1,16,2048]{3,2,1,0:T(8,128)(2,1)} %copy-done.3) | copy-start | bytes 786436
  84.5 7.9 %copy-start.7 = (s32[1,128,8]{1,2,0:T(8,128)S(1)}, s32[1,128,8]{1,2,0:T(8,128)}, u32[]{:S(2)}) copy-start(s32[1,128,8]{1,2,0:T(8,128)} %param.12) | copy-start | bytes 12292
  84.5 7.9 %copy-start.9 = (f32[1,128,8]{1,2,0:T(8,128)S(1)}, f32[1,128,8]{1,2,0:T(8,128)}, u32[]{:S(2)}) copy-start(f32[1,128,8]{1,2,0:T(8,128)} %param.13) | copy-start | bytes 12292
  91.7 45.0 %reduce-scatter.5.cloned.1.call-start = ((), (), s32[]{:S(2)}) async-start(), calls=%async_computation.3 | async-start | bytes 655360 | tf_op jit(solution)/shard_map/reduce_scatter | solution.py:133
  116.5 23.6 %collective-permute-start = (bf16[1,128,2048]{2,1,0:T(8,128)(2,1)}, bf16[1,128,2048]{2,1,0:T(8,128)(2,1)}, u32[]{:S(2)}, u32[]{:S(2)}) collective-permute-start(bf16[1,128,2048]{2,1,0:T(8,128)(2,1)} %fusion.22), channel_id=1, source_target_pairs={{28,0},{0,4},{4,8},{8,12},{12,16},{16,20},{20,24},{24,28},{29,1},{... | collective-permute-start | bytes 1572872 | tf_op jit(solution)/shard_map/ppermute | solution.py:16
  139.9 6.8 %collective-permute-start.1 = (bf16[1,128,2048]{2,1,0:T(8,128)(2,1)S(1)}, bf16[1,128,2048]{2,1,0:T(8,128)(2,1)S(1)}, u32[]{:S(2)}, u32[]{:S(2)}) collective-permute-start(bf16[1,128,2048]{2,1,0:T(8,128)(2,1)S(1)} %fusion.66), channel_id=1, source_target_pairs={{4,0},{8,4},{12,8},{16,12},{20,16},{24,20},{28,24},{0,28},{5,1},{9... | collective-permute-start | bytes 1572872 | tf_op jit(solution)/shard_map/ppermute | solution.py:16
Sparse Core Ops, SparseCore 0:
  91.8 22.0 reduce-scatter.2
  116.8 19.9 reduce-scatter.4
where the time goes:
time: 158 us; the launch traced here: 156 us
  blocking collectives  51.8 us (33%)
  waiting for transfers between devices  49.1 us (31%)
  matrix products  26.8 us (17%)
  between operations  14.2 us (9%)
  other arithmetic  8.93 us (6%)
  local copies, waits for them, and re-layouts  5.33 us (3%)
    reduce_scatter x1, waiting for transfers between devices, on_device(): lax.psum_scatter(forward_part[:, None] * select, 'expert', scatter_dimens...  21.5 us
    reduce_scatter x1, waiting for transfers between devices, on_device(): lax.psum_scatter(backward_part[:, None] * select, 'expert', scatter_dimen...  20.2 us
    all_gather x1, blocking collectives, on_device(): lax.all_gather(backward_slots[None], 'expert', axis=0, tiled=True)  18 us
    all_gather x1, blocking collectives, on_device(): lax.all_gather(forward_slots[None], 'expert', axis=0, tiled=True)  17.1 us
    all_gather x1, blocking collectives, on_device(): lax.all_gather(grad_slots[None], 'expert', axis=0, tiled=True)  16.6 us
    dot_general x3, matrix products, project(): lax.dot_general(left, right, (((1,), (1,)), ((), ())), preferred_element_...  7.2 us
    ppermute x2, waiting for transfers between devices, passed_along(): return lax.ppermute(block, axis, route)  6.7 us
    dot_general x1, matrix products, slice_backward(): total = jnp.dot(gate_grad, gate_rows, preferred_element_type=jnp.float32)  5.02 us
  transfers between devices with their start and end apart: 4, of which 3 were waited for; matrix products, arithmetic and copies ran while one was open for 4% of the time, Pallas kernels for 0%

commit v1 on v0

v1 whole, which is shorter than its diff:
```python
import functools

import jax
import jax.numpy as jnp
from jax import lax
from jax.experimental import pallas as pl
from jax.experimental.pallas import tpu as pltpu
from jax.sharding import PartitionSpec as P

EF = 2
CAP = 16
EPSILON = 1e-06
LANES = 128
MIB = 1 << 20

VMEM = pl.BlockSpec(memory_space=pltpu.VMEM)
SMEM = pl.BlockSpec(memory_space=pltpu.SMEM)


def call(body, outs, specs, flops, nbytes, limit):
    return pl.pallas_call(
        body,
        out_shape=outs,
        in_specs=specs,
        out_specs=[VMEM] * len(outs),
        compiler_params=pltpu.CompilerParams(vmem_limit_bytes=limit * MIB),
        cost_estimate=pl.CostEstimate(flops=flops, bytes_accessed=nbytes, transcendentals=0),
    )


def bf16(shape):
    return jax.ShapeDtypeStruct(shape, jnp.bfloat16)


def slot_tables(owner, routes, shares):
    tokens = routes.shape[0]
    lane = lax.broadcasted_iota(jnp.int32, (tokens, LANES), 1)
    weights = []
    members = []
    for expert in (owner, 1 - owner):
        hit = routes == expert
        members.append(jnp.sum(jnp.where(hit, 1.0, 0.0), axis=1, keepdims=True))
        weights.append(jnp.sum(jnp.where(hit, shares, 0.0), axis=1, keepdims=True))
    first = lane < CAP
    used = lane < EF * CAP
    member = jnp.where(used, jnp.where(first, members[0], members[1]), 0.0)
    row = lax.broadcasted_iota(jnp.int32, (tokens, tokens), 0)
    col = lax.broadcasted_iota(jnp.int32, (tokens, tokens), 1)
    earlier = jnp.where(col < row, 1.0, 0.0).astype(jnp.bfloat16)
    rank = jnp.dot(earlier, member.astype(jnp.bfloat16), preferred_element_type=jnp.float32)
    slot = (lane % CAP).astype(jnp.float32)
    placed = jnp.where((member > 0.5) & (rank == slot), 1.0, 0.0)
    return lane, first, weights, placed


def dispatch_forward(owner_ref, routes_ref, shares_ref, rows_ref, own_ref, other_ref, early_ref):
    lane, first, weights, placed = slot_tables(owner_ref[0], routes_ref[0], shares_ref[0])
    rows = rows_ref[0]
    width = rows.shape[1]
    table = placed
    for e, weight in enumerate(weights):
        left = weight
        for piece in range(3):
            part = left.astype(jnp.bfloat16).astype(jnp.float32)
            left = left - part
            table = jnp.where(lane == EF * CAP + 3 * e + piece, part, table)
    early_ref[:, width:] = table.astype(jnp.bfloat16)
    early_ref[:, :width] = rows
    pick = jnp.transpose(placed)[: EF * CAP].astype(jnp.bfloat16)
    slots = jnp.dot(pick, rows, preferred_element_type=jnp.float32).astype(jnp.bfloat16)
    own_ref[...] = slots[:CAP]
    other_ref[...] = slots[CAP:]


def dispatch_backward(
    owner_ref, routes_ref, shares_ref, rows_ref, grad_ref, own_ref, other_ref, early_ref
):
    lane, first, weights, placed = slot_tables(owner_ref[0], routes_ref[0], shares_ref[0])
    rows = rows_ref[0]
    grads = grad_ref[0]
    width = rows.shape[1]
    turned = jnp.transpose(placed)[: EF * CAP]
    shared = jnp.transpose(placed * jnp.where(first, weights[0], weights[1]))[: EF * CAP]
    share = jnp.sum(shared, axis=1, keepdims=True)
    pick = turned.astype(jnp.bfloat16)
    slots = jnp.dot(pick, rows, preferred_element_type=jnp.float32).astype(jnp.bfloat16)
    picked = jnp.dot(pick, grads, preferred_element_type=jnp.float32)
    grad_slots = (share * picked).astype(jnp.bfloat16)
    own_ref[:CAP] = slots[:CAP]
    own_ref[CAP:] = grad_slots[:CAP]
    other_ref[:CAP] = slots[CAP:]
    other_ref[CAP:] = grad_slots[CAP:]
    early_ref[:, width:] = placed.astype(jnp.bfloat16)
    early_ref[:, :width] = grads


def project(left, right):
    return lax.dot_general(
        left, right, (((1,), (1,)), ((), ())), preferred_element_type=jnp.float32
    )


def unit_rows(rows):
    values = rows.astype(jnp.float32)
    scale = lax.rsqrt(jnp.mean(values * values, axis=-1, keepdims=True) + EPSILON)
    return values * scale, scale


def expert_forward(blocks, *refs):
    rows = jnp.concatenate([ref[...] for ref in refs[:blocks]], axis=0)
    gain_ref, gate_ref, up_ref, down_ref = refs[blocks : blocks + 4]
    outs = refs[blocks + 4 :]
    unit, _ = unit_rows(rows)
    normed = (unit * gain_ref[...]).astype(jnp.bfloat16)
    gate = project(normed, gate_ref[0])
    upper = project(normed, up_ref[0])
    hidden = (gate * jax.nn.sigmoid(gate) * upper).astype(jnp.bfloat16)
    result = jnp.dot(hidden, down_ref[0], preferred_element_type=jnp.float32)
    result = result.astype(jnp.bfloat16)
    for k in range(blocks):
        outs[k][...] = result[k * CAP : (k + 1) * CAP]


def expert_backward(blocks, *refs):
    rows = jnp.concatenate([ref[:CAP] for ref in refs[:blocks]], axis=0)
    grads = jnp.concatenate([ref[CAP:] for ref in refs[:blocks]], axis=0)
    gain_ref, gate_ref, up_ref, down_ref = refs[blocks : blocks + 4]
    outs = refs[blocks + 4 :]
    gain = gain_ref[...]
    unit, scale = unit_rows(rows)
    normed = (unit * gain).astype(jnp.bfloat16)
    hidden_grad = project(grads, down_ref[0])
    gate = project(normed, gate_ref[0])
    upper = project(normed, up_ref[0])
    sigma = jax.nn.sigmoid(gate)
    gate_grad = (hidden_grad * upper * sigma * (1.0 + gate * (1.0 - sigma))).astype(jnp.bfloat16)
    upper_grad = (hidden_grad * gate * sigma).astype(jnp.bfloat16)
    total = jnp.dot(gate_grad, gate_ref[0], preferred_element_type=jnp.float32)
    total = total + jnp.dot(upper_grad, up_ref[0], preferred_element_type=jnp.float32)
    scaled = total * gain
    inner = jnp.mean(scaled * unit, axis=-1, keepdims=True)
    result = (scale * (scaled - unit * inner)).astype(jnp.bfloat16)
    for k in range(blocks):
        outs[k][...] = result[k * CAP : (k + 1) * CAP]


def combine_forward(half, early_ref, *refs):
    out_ref = refs[-1]
    width = out_ref.shape[2]
    total = early_ref[:, :width].astype(jnp.float32)
    table = early_ref[:, width:]
    for e in range(EF):
        parts = jnp.concatenate([ref[...] for ref in refs[e * half : (e + 1) * half]], axis=0)
        pick = jnp.concatenate([table[:, e * CAP : (e + 1) * CAP]] * half, axis=1)
        column = EF * CAP + 3 * e
        weight = jnp.sum(
            table[:, column : column + 3].astype(jnp.float32), axis=1, keepdims=True
        )
        total = total + weight * jnp.dot(pick, parts, preferred_element_type=jnp.float32)
    out_ref[0] = total.astype(jnp.bfloat16)


def combine_backward(half, early_ref, *refs):
    out_ref = refs[-1]
    width = out_ref.shape[2]
    table = early_ref[:, width:]
    parts = jnp.concatenate([ref[...] for ref in refs[:-1]], axis=0)
    pick = jnp.concatenate(
        [table[:, e * CAP : (e + 1) * CAP] for e in range(EF) for _ in range(half)], axis=1
    )
    total = early_ref[:, :width].astype(jnp.float32)
    total = total + jnp.dot(pick, parts, preferred_element_type=jnp.float32)
    out_ref[0] = total.astype(jnp.bfloat16)


def on_device(
    sections,
    devices,
    forward_input,
    forward_routes,
    forward_shares,
    backward_input,
    backward_routes,
    backward_shares,
    output_grad,
    norm_gain,
    gate_weight,
    up_weight,
    down_weight,
):
    half = devices // EF
    tokens, width = forward_input.shape[1:]
    hidden = gate_weight.shape[1]
    owner = (lax.axis_index("expert") // half).astype(jnp.int32)[None]

    def swapped(block, k):
        return lax.ppermute(block, "expert", [(i, i ^ k) for i in range(devices)])

    def moved(block, distance):
        route = [(i, (i + distance) % sections) for i in range(sections)]
        return lax.ppermute(block, "section", route)

    def returned(block, distance, k):
        route = [
            (s * devices + z, (s + distance) % sections * devices + (z ^ k))
            for s in range(sections)
            for z in range(devices)
        ]
        return lax.ppermute(block, ("section", "expert"), route)

    def gathered(own, other):
        blocks = [own]
        far = [swapped(other, half)]
        step = 1
        while step < half:
            blocks = blocks + [swapped(b, step) for b in blocks]
            far = far + [swapped(b, step) for b in far]
            step *= 2
        return blocks + far

    dispatch_bytes = 3 * tokens * width * 2
    own_b, other_b, early_b = call(
        dispatch_backward,
        [bf16((2 * CAP, width)), bf16((2 * CAP, width)), bf16((tokens, width + LANES))],
        [SMEM, VMEM, VMEM, VMEM, VMEM],
        4 * EF * CAP * tokens * width,
        dispatch_bytes,
        24,
    )(owner, backward_routes, backward_shares, backward_input, output_grad)
    own_f, other_f, early_f = call(
        dispatch_forward,
        [bf16((CAP, width)), bf16((CAP, width)), bf16((tokens, width + LANES))],
        [SMEM, VMEM, VMEM, VMEM],
        2 * EF * CAP * tokens * width,
        dispatch_bytes,
        24,
    )(owner, forward_routes, forward_shares, forward_input)

    blocks_b = gathered(own_b, other_b)
    blocks_f = gathered(own_f, other_f)
    early_b = moved(early_b, -1)
    early_f = moved(early_f, 1)

    weights = [
        pltpu.with_memory_space_constraint(w, pltpu.VMEM)
        for w in (gate_weight, up_weight, down_weight)
    ]
    rows = devices * CAP
    weight_bytes = 3 * hidden * width * 2
    outs = [bf16((CAP, width))] * devices
    parts_b = call(
        functools.partial(expert_backward, devices),
        outs,
        [VMEM] * (devices + 4),
        10 * rows * hidden * width,
        weight_bytes,
        24,
    )(*blocks_b, norm_gain, *weights)
    parts_f = call(
        functools.partial(expert_forward, devices),
        outs,
        [VMEM] * (devices + 4),
        6 * rows * hidden * width,
        weight_bytes,
        24,
    )(*blocks_f, norm_gain, *weights)

    parts_b = [returned(part, -1, k) for k, part in enumerate(parts_b)]
    parts_f = [returned(part, 1, k) for k, part in enumerate(parts_f)]
    result = [bf16((1, tokens, width))]
    (previous_gradient,) = call(
        functools.partial(combine_backward, half),
        result,
        [VMEM] * (devices + 1),
        2 * tokens * devices * CAP * width,
        dispatch_bytes,
        24,
    )(early_b, *parts_b)
    (next_input,) = call(
        functools.partial(combine_forward, half),
        result,
        [VMEM] * (devices + 1),
        2 * tokens * devices * CAP * width,
        dispatch_bytes,
        24,
    )(early_f, *parts_f)
    return next_input, previous_gradient


def solution(mesh):
    rows = P("section", "expert", None)
    return jax.shard_map(
        functools.partial(on_device, mesh.shape["section"], mesh.shape["expert"]),
        mesh=mesh,
        in_specs=(rows,) * 7 + (P("section", None),) + (rows,) * 3,
        out_specs=(rows, rows),
        check_vma=False,
    )
```

time: 158 us -> 62.2 us (0.39)
  blocking collectives: 51.8 us -> 0 us
  waiting for transfers between devices: 49.1 us -> 15.2 us
  matrix products: 26.8 us -> 0 us
  starting transfers between devices: 0.21 us -> 21.9 us
  between operations: 14.2 us -> 0.72 us
  Pallas kernels: 0 us -> 10.6 us
  other arithmetic: 8.93 us -> 0 us
  local copies, waits for them, and re-layouts: 5.33 us -> 12.6 us
    all_gather x3 -> x0, blocking collectives: 51.8 us -> none  [the longest x1 18 us: on_device(): lax.all_gather(backward_slots[None], 'expert', axis=0, tiled=True)]
    reduce_scatter x2 -> x0, waiting for transfers between devices: 41.7 us -> none  [the longest x1 21.5 us: on_device(): lax.psum_scatter(forward_part[:, None] * select, 'expert', scatter_dimens...]
    dot_general x11 -> x0, matrix products: 26.8 us -> none  [the longest x3 7.2 us: project(): lax.dot_general(left, right, (((1,), (1,)), ((), ())), preferred_element_...]
    ppermute x2 -> x16, starting transfers between devices: 0.13 us -> 21.9 us  [the longest x8 10.5 us: returned(): return lax.ppermute(block, ('section', 'expert'), route)]
    pallas_call x0 -> x6, Pallas kernels: none -> 10.6 us  [the longest x1 4.51 us: on_device(): call(functools.partial(expert_backward, devices), outs, [VMEM] * (devices...]
    unnamed x22 -> x26, local copies, waits for them, and re-layouts: 2.72 us -> 12.6 us
    ppermute x2 -> x16, waiting for transfers between devices: 6.7 us -> 15.2 us  [the longest x6 8.66 us: swapped(): return lax.ppermute(block, 'expert', [(i, i ^ k) for i in range(devices)])]
    reduce_sum x4 -> x0, other arithmetic: 3.2 us -> none  [the longest x2 2.46 us: normalize(): jnp.mean(values * values, axis=-1, keepdims=True) + EPSILON]
  transfers between devices with their start and end apart: 4 -> 16, of which waited for: 3 -> 6; matrix products, arithmetic and copies ran while one was open for 4% -> 3% of each run, Pallas kernels for 0% -> 15%
where the time goes in v1:
time: 62.2 us; the launch traced here: 61.1 us
  starting transfers between devices  21.9 us (35%)
  waiting for transfers between devices  15.2 us (24%)
  local copies, waits for them, and re-layouts  12.6 us (20%)
  Pallas kernels  10.6 us (17%)
  between operations  0.72 us (1%)
    unnamed x26, local copies, waits for them, and re-layouts  12.6 us
    ppermute x8, starting transfers between devices, returned(): return lax.ppermute(block, ('section', 'expert'), route)  10.5 us
    ppermute x6, waiting for transfers between devices, swapped(): return lax.ppermute(block, 'expert', [(i, i ^ k) for i in range(devices)])  8.66 us
    ppermute x6, starting transfers between devices, swapped(): return lax.ppermute(block, 'expert', [(i, i ^ k) for i in range(devices)])  7.94 us
    ppermute x8, waiting for transfers between devices, returned(): return lax.ppermute(block, ('section', 'expert'), route)  6.58 us
    pallas_call x1, Pallas kernels, on_device(): call(functools.partial(expert_backward, devices), outs, [VMEM] * (devices...  4.51 us
    ppermute x2, starting transfers between devices, moved(): return lax.ppermute(block, 'section', route)  3.45 us
    pallas_call x1, Pallas kernels, on_device(): call(functools.partial(expert_forward, devices), outs, [VMEM] * (devices...  2.64 us
  transfers between devices with their start and end apart: 16, of which 6 were waited for; matrix products, arithmetic and copies ran while one was open for 3% of the time, Pallas kernels for 15%

profile of v1, /device:TPU:0, one launch (start us, length us, event | category | flops | bytes accessed | tf_op | source)
XLA Modules:
  0.0 61.1 jit_solution(16652358347571015917)
XLA Ops:
  0.6 0.8 %copy.13.routes_ref = s32[1,128,8]{2,1,0:T(8,128)S(1)} copy(s32[1,128,8]{1,2,0:T(8,128)} %param.12) | data formatting | bytes 8192 | tf_op args[1]
  1.4 0.8 %copy.14.shares_ref = f32[1,128,8]{2,1,0:T(8,128)S(1)} copy(f32[1,128,8]{1,2,0:T(8,128)} %param.13) | data formatting | bytes 8192 | tf_op args[2]
  2.2 0.0 copy-start.6
  2.2 1.0 %copy-done.6 = bf16[1,128,2048]{2,1,0:T(8,128)(2,1)S(1)} copy-done((bf16[1,128,2048]{2,1,0:T(8,128)(2,1)S(1)}, bf16[1,128,2048]{2,1,0:T(8,128)(2,1)}, u32[]{:S(2)}) %copy-start.6) | copy-done | bytes 524312
  3.3 0.5 shard_map.122
  3.8 0.5 collective-permute-start
  4.3 0.8 %copy.15.routes_ref = s32[1,128,8]{2,1,0:T(8,128)S(1)} copy(s32[1,128,8]{1,2,0:T(8,128)} %param.15) | data formatting | bytes 8192 | tf_op args[4]
  5.0 0.8 %copy.16.shares_ref = f32[1,128,8]{2,1,0:T(8,128)S(1)} copy(f32[1,128,8]{1,2,0:T(8,128)} %param.16) | data formatting | bytes 8192 | tf_op args[5]
  5.8 0.0 copy-start.7
  5.8 1.0 %copy-done.7 = bf16[1,128,2048]{2,1,0:T(8,128)(2,1)S(1)} copy-done((bf16[1,128,2048]{2,1,0:T(8,128)(2,1)S(1)}, bf16[1,128,2048]{2,1,0:T(8,128)(2,1)}, u32[]{:S(2)}) %copy-start.7) | copy-done | bytes 524312
  6.9 0.0 copy-start.8
  6.9 1.0 %copy-done.8 = bf16[1,128,2048]{2,1,0:T(8,128)(2,1)S(1)} copy-done((bf16[1,128,2048]{2,1,0:T(8,128)(2,1)S(1)}, bf16[1,128,2048]{2,1,0:T(8,128)(2,1)}, u32[]{:S(2)}) %copy-start.8) | copy-done | bytes 524312
  7.9 0.6 shard_map.125
  8.5 2.9 %collective-permute-start.8 = (bf16[128,2176]{1,0:T(8,128)(2,1)S(1)}, bf16[128,2176]{1,0:T(8,128)(2,1)S(1)}, u32[]{:S(2)}, u32[]{:S(2)}) collective-permute-start(bf16[128,2176]{1,0:T(8,128)(2,1)S(1)} %get-tuple-element.23), channel_id=1, source_target_pairs={{0,28},{4,0},{8,4},{12,8},{16,12},{20,16},{24,20},{28,24},{1,29},{... | collective-permute-start | bytes 1671176 | tf_op jit(solution)/shard_map/ppermute | solution.py:201
  11.4 3.3 %collective-permute-start.10 = (bf16[32,2048]{1,0:T(8,128)(2,1)S(1)}, bf16[32,2048]{1,0:T(8,128)(2,1)S(1)}, u32[]{:S(2)}, u32[]{:S(2)}) collective-permute-start(bf16[32,2048]{1,0:T(8,128)(2,1)S(1)} %get-tuple-element.25), channel_id=1, source_target_pairs={{0,2},{1,3},{2,0},{3,1},{4,6},{5,7},{6,4},{7,5},{8,10},{9,11},{10,... | collective-permute-start | bytes 393224 | tf_op jit(solution)/shard_map/ppermute | solution.py:197
  14.8 0.0 collective-permute-start.2
  14.8 1.9 %collective-permute-start.1 = (bf16[16,2048]{1,0:T(8,128)(2,1)S(1)}, bf16[16,2048]{1,0:T(8,128)(2,1)S(1)}, u32[]{:S(2)}, u32[]{:S(2)}) collective-permute-start(bf16[16,2048]{1,0:T(8,128)(2,1)S(1)} %get-tuple-element.17.refs_0_), channel_id=1, source_target_pairs={{0,1},{1,0},{2,3},{3,2},{4,5},{5,4},{6,7},{7,6},{8,9},{9,8},{10,11... | collective-permute-start | bytes 196616 | tf_op jit(solution)/shard_map/ppermute | solution.py:197
  16.7 6.5 %collective-permute-done.2.refs_2_ = bf16[16,2048]{1,0:T(8,128)(2,1)S(1)} collective-permute-done((bf16[16,2048]{1,0:T(8,128)(2,1)S(1)}, bf16[16,2048]{1,0:T(8,128)(2,1)S(1)}, u32[]{:S(2)}, u32[]{:S(2)}) %collective-permute-start.2) | collective-permute-done | bytes 65568 | tf_op jit(solution)/shard_map/ppermute | solution.py:197
  23.1 0.7 %collective-permute-start.3 = (bf16[16,2048]{1,0:T(8,128)(2,1)S(1)}, bf16[16,2048]{1,0:T(8,128)(2,1)S(1)}, u32[]{:S(2)}, u32[]{:S(2)}) collective-permute-start(bf16[16,2048]{1,0:T(8,128)(2,1)S(1)} %collective-permute-done.2.refs_2_), channel_id=1, source_target_pairs={{0,1},{1,0},{2,3},{3,2},{4,5},{5,4},{6,7},{7,6},{8,9},{9,8},{10,11... | collective-permute-start | bytes 196616 | tf_op jit(solution)/shard_map/ppermute | solution.py:197
  23.8 0.0 collective-permute-done.1.refs_1_
  23.8 1.4 %collective-permute-start.9 = (bf16[32,2048]{1,0:T(8,128)(2,1)S(1)}, bf16[32,2048]{1,0:T(8,128)(2,1)S(1)}, u32[]{:S(2)}, u32[]{:S(2)}) collective-permute-start(bf16[32,2048]{1,0:T(8,128)(2,1)S(1)} %get-tuple-element.24.refs_0_), channel_id=1, source_target_pairs={{0,1},{1,0},{2,3},{3,2},{4,5},{5,4},{6,7},{7,6},{8,9},{9,8},{10,11... | collective-permute-start | bytes 393224 | tf_op jit(solution)/shard_map/ppermute | solution.py:197
  25.2 0.0 collective-permute-done.10.refs_2_
  25.2 0.7 %collective-permute-start.11 = (bf16[32,2048]{1,0:T(8,128)(2,1)S(1)}, bf16[32,2048]{1,0:T(8,128)(2,1)S(1)}, u32[]{:S(2)}, u32[]{:S(2)}) collective-permute-start(bf16[32,2048]{1,0:T(8,128)(2,1)S(1)} %collective-permute-done.10.refs_2_), channel_id=1, source_target_pairs={{0,1},{1,0},{2,3},{3,2},{4,5},{5,4},{6,7},{7,6},{8,9},{9,8},{10,11... | collective-permute-start | bytes 393224 | tf_op jit(solution)/shard_map/ppermute | solution.py:197
  25.8 2.2 %collective-permute-done.3.refs_3_ = bf16[16,2048]{1,0:T(8,128)(2,1)S(1)} collective-permute-done((bf16[16,2048]{1,0:T(8,128)(2,1)S(1)}, bf16[16,2048]{1,0:T(8,128)(2,1)S(1)}, u32[]{:S(2)}, u32[]{:S(2)}) %collective-permute-start.3) | collective-permute-done | bytes 65568 | tf_op jit(solution)/shard_map/ppermute | solution.py:197
  28.0 0.0 copy-start
  28.0 1.9 %copy-done = bf16[1,768,2048]{2,1,0:T(8,128)(2,1)S(1)} copy-done((bf16[1,768,2048]{2,1,0:T(8,128)(2,1)S(1)}, bf16[1,768,2048]{2,1,0:T(8,128)(2,1)}, u32[]{:S(2)}) %copy-start) | copy-done | bytes 3145752
  29.9 0.0 copy-start.2
  29.9 1.9 %copy-done.2 = bf16[1,768,2048]{2,1,0:T(8,128)(2,1)S(1)} copy-done((bf16[1,768,2048]{2,1,0:T(8,128)(2,1)S(1)}, bf16[1,768,2048]{2,1,0:T(8,128)(2,1)}, u32[]{:S(2)}) %copy-start.2) | copy-done | bytes 3145752
  31.8 0.0 copy-start.4
  31.8 1.9 %copy-done.4 = bf16[1,768,2048]{2,1,0:T(8,128)(2,1)S(1)} copy-done((bf16[1,768,2048]{2,1,0:T(8,128)(2,1)S(1)}, bf16[1,768,2048]{2,1,0:T(8,128)(2,1)}, u32[]{:S(2)}) %copy-start.4) | copy-done | bytes 3145752
  33.7 0.0 copy-start.9
  33.7 0.7 %copy-done.9 = f32[1,2048]{1,0:T(1,128)S(1)} copy-done((f32[1,2048]{1,0:T(1,128)S(1)}, f32[1,2048]{1,0:T(1,128)}, u32[]{:S(2)}) %copy-start.9) | copy-done | bytes 8216
  34.4 0.0 copy-start.1
  34.4 0.0 copy-start.3
  34.4 0.0 copy-start.5
  34.4 0.0 copy-start.10
  34.4 2.6 %shard_map.123 = (bf16[16,2048]{1,0:T(8,128)(2,1)S(1)}, bf16[16,2048]{1,0:T(8,128)(2,1)S(1)}, bf16[16,2048]{1,0:T(8,128)(2,1)S(1)}, bf16[16,2048]{1,0:T(8,128)(2,1)S(1)}) custom-call(bf16[16,2048]{1,0:T(8,128)(2,1)S(1)} %get-tuple-element.17.refs_0_, bf16[16,2048]{1,0:T(8,128)(2,1)S(1)} %collective-permute-done.1.refs_1_, ...), custom_call_target="tpu_custom_call" | custom-call | flops 603979776 | bytes 9437184 | tf_op jit(solution)/shard_map/pallas_call | solution.py:259
  37.1 0.1 collective-permute-start.4
  37.1 0.0 collective-permute-done.9.refs_1_
  37.1 1.9 %collective-permute-start.5 = (bf16[16,2048]{1,0:T(8,128)(2,1)S(1)}, bf16[16,2048]{1,0:T(8,128)(2,1)S(1)}, u32[]{:S(2)}, u32[]{:S(2)}) collective-permute-start(bf16[16,2048]{1,0:T(8,128)(2,1)S(1)} %get-tuple-element.20), channel_id=1, source_target_pairs={{0,5},{1,4},{2,7},{3,6},{4,9},{5,8},{6,11},{7,10},{8,13},{9,12},{1... | collective-permute-start | bytes 196616 | tf_op jit(solution)/shard_map/ppermute | solution.py:209
  39.1 2.6 %collective-permute-done.4.refs_0_ = bf16[16,2048]{1,0:T(8,128)(2,1)S(1)} collective-permute-done((bf16[16,2048]{1,0:T(8,128)(2,1)S(1)}, bf16[16,2048]{1,0:T(8,128)(2,1)S(1)}, u32[]{:S(2)}, u32[]{:S(2)}) %collective-permute-start.4) | collective-permute-done | bytes 65568 | tf_op jit(solution)/shard_map/ppermute | solution.py:209
  41.7 0.2 collective-permute-start.6
  41.9 0.0 collective-permute-done.11.refs_3_
  41.9 2.6 %collective-permute-start.7 = (bf16[16,2048]{1,0:T(8,128)(2,1)S(1)}, bf16[16,2048]{1,0:T(8,128)(2,1)S(1)}, u32[]{:S(2)}, u32[]{:S(2)}) collective-permute-start(bf16[16,2048]{1,0:T(8,128)(2,1)S(1)} %get-tuple-element.22), channel_id=1, source_target_pairs={{0,7},{1,6},{2,5},{3,4},{4,11},{5,10},{6,9},{7,8},{8,15},{9,14},{1... | collective-permute-start | bytes 196616 | tf_op jit(solution)/shard_map/ppermute | solution.py:209
  44.5 0.0 copy-done.1
  44.5 0.0 copy-done.3
  44.5 0.0 copy-done.5
  44.5 0.0 copy-done.10
  44.6 4.5 %shard_map.126 = (bf16[16,2048]{1,0:T(8,128)(2,1)S(1)}, bf16[16,2048]{1,0:T(8,128)(2,1)S(1)}, bf16[16,2048]{1,0:T(8,128)(2,1)S(1)}, bf16[16,2048]{1,0:T(8,128)(2,1)S(1)}) custom-call(bf16[32,2048]{1,0:T(8,128)(2,1)S(1)} %get-tuple-element.24.refs_0_, bf16[32,2048]{1,0:T(8,128)(2,1)S(1)} %collective-permute-done.9.refs_1_, ...), custom_call_target="tpu_custom_call" | custom-call | flops 1006632960 | bytes 9437184 | tf_op jit(solution)/shard_map/pallas_call | solution.py:251
  49.1 0.0 collective-permute-done.5.refs_1_
  49.1 2.8 %collective-permute-start.12 = (bf16[16,2048]{1,0:T(8,128)(2,1)S(1)}, bf16[16,2048]{1,0:T(8,128)(2,1)S(1)}, u32[]{:S(2)}, u32[]{:S(2)}) collective-permute-start(bf16[16,2048]{1,0:T(8,128)(2,1)S(1)} %get-tuple-element.26), channel_id=1, source_target_pairs={{0,28},{1,29},{2,30},{3,31},{4,0},{5,1},{6,2},{7,3},{8,4},{9,5},{1... | collective-permute-start | bytes 196616 | tf_op jit(solution)/shard_map/ppermute | solution.py:209
  51.9 0.0 collective-permute-done.6.refs_2_
  51.9 0.1 collective-permute-start.13
  52.0 0.0 collective-permute-done.7.refs_3_
  52.0 1.6 %collective-permute-start.14 = (bf16[16,2048]{1,0:T(8,128)(2,1)S(1)}, bf16[16,2048]{1,0:T(8,128)(2,1)S(1)}, u32[]{:S(2)}, u32[]{:S(2)}) collective-permute-start(bf16[16,2048]{1,0:T(8,128)(2,1)S(1)} %get-tuple-element.28), channel_id=1, source_target_pairs={{0,30},{1,31},{2,28},{3,29},{4,2},{5,3},{6,0},{7,1},{8,6},{9,7},{1... | collective-permute-start | bytes 196616 | tf_op jit(solution)/shard_map/ppermute | solution.py:209
  53.6 0.0 collective-permute-done.early_ref
  53.6 1.1 %collective-permute-start.15 = (bf16[16,2048]{1,0:T(8,128)(2,1)S(1)}, bf16[16,2048]{1,0:T(8,128)(2,1)S(1)}, u32[]{:S(2)}, u32[]{:S(2)}) collective-permute-start(bf16[16,2048]{1,0:T(8,128)(2,1)S(1)} %get-tuple-element.29), channel_id=1, source_target_pairs={{0,31},{1,30},{2,29},{3,28},{4,3},{5,2},{6,1},{7,0},{8,7},{9,6},{1... | collective-permute-start | bytes 196616 | tf_op jit(solution)/shard_map/ppermute | solution.py:209
  54.7 1.3 %shard_map.124 = bf16[1,128,2048]{2,1,0:T(8,128)(2,1)} custom-call(bf16[128,2176]{1,0:T(8,128)(2,1)S(1)} %collective-permute-done.early_ref, bf16[16,2048]{1,0:T(8,128)(2,1)S(1)} %collective-permute-done.4.refs_0_, bf16[16,2048]{1,0:T(8,128)(2,1)S(1)} %collective-permute-done.5.refs_1_, bf16[16,2048]{1,0:T(8,128)(2,1)S(1)} %collective-permute-done.6.refs_2_, ...), custom_call_target="tpu_custom_call" | custom-call | flops 33554432 | bytes 1572864 | tf_op jit(solution)/shard_map/pallas_call | solution.py:279
  56.1 0.0 collective-permute-done.12.refs_0_
  56.1 1.4 %collective-permute-done.13.refs_1_ = bf16[16,2048]{1,0:T(8,128)(2,1)S(1)} collective-permute-done((bf16[16,2048]{1,0:T(8,128)(2,1)S(1)}, bf16[16,2048]{1,0:T(8,128)(2,1)S(1)}, u32[]{:S(2)}, u32[]{:S(2)}) %collective-permute-start.13) | collective-permute-done | bytes 65568 | tf_op jit(solution)/shard_map/ppermute | solution.py:209
  57.4 0.2 collective-permute-done.14.refs_2_
  57.7 2.3 %collective-permute-done.15.refs_3_ = bf16[16,2048]{1,0:T(8,128)(2,1)S(1)} collective-permute-done((bf16[16,2048]{1,0:T(8,128)(2,1)S(1)}, bf16[16,2048]{1,0:T(8,128)(2,1)S(1)}, u32[]{:S(2)}, u32[]{:S(2)}) %collective-permute-start.15) | collective-permute-done | bytes 65568 | tf_op jit(solution)/shard_map/ppermute | solution.py:209
  60.0 0.0 collective-permute-done.8.early_ref
  60.0 1.1 %shard_map.127 = bf16[1,128,2048]{2,1,0:T(8,128)(2,1)} custom-call(bf16[128,2176]{1,0:T(8,128)(2,1)S(1)} %collective-permute-done.8.early_ref, bf16[16,2048]{1,0:T(8,128)(2,1)S(1)} %collective-permute-done.12.refs_0_, bf16[16,2048]{1,0:T(8,128)(2,1)S(1)} %collective-permute-done.13.refs_1_, bf16[16,2048]{1,0:T(8,128)(2,1)S(1)} %collective-permute-done.14.refs_2_, ...), custom_call_target="tpu_custom_call" | custom-call | flops 33554432 | bytes 1572864 | tf_op jit(solution)/shard_map/pallas_call | solution.py:271
Async XLA Ops:
  2.2 1.0 %copy-start.6 = (bf16[1,128,2048]{2,1,0:T(8,128)(2,1)S(1)}, bf16[1,128,2048]{2,1,0:T(8,128)(2,1)}, u32[]{:S(2)}) copy-start(bf16[1,128,2048]{2,1,0:T(8,128)(2,1)} %rows_ref.2) | copy-start | bytes 1572868
  3.8 49.9 %collective-permute-start = (bf16[128,2176]{1,0:T(8,128)(2,1)S(1)}, bf16[128,2176]{1,0:T(8,128)(2,1)S(1)}, u32[]{:S(2)}, u32[]{:S(2)}) collective-permute-start(bf16[128,2176]{1,0:T(8,128)(2,1)S(1)} %get-tuple-element.16), channel_id=1, source_target_pairs={{0,4},{4,8},{8,12},{12,16},{16,20},{20,24},{24,28},{28,0},{1,5},{5... | collective-permute-start | bytes 1671176 | tf_op jit(solution)/shard_map/ppermute | solution.py:201
  5.8 1.0 %copy-start.7 = (bf16[1,128,2048]{2,1,0:T(8,128)(2,1)S(1)}, bf16[1,128,2048]{2,1,0:T(8,128)(2,1)}, u32[]{:S(2)}) copy-start(bf16[1,128,2048]{2,1,0:T(8,128)(2,1)} %rows_ref.3) | copy-start | bytes 1572868
  6.9 1.0 %copy-start.8 = (bf16[1,128,2048]{2,1,0:T(8,128)(2,1)S(1)}, bf16[1,128,2048]{2,1,0:T(8,128)(2,1)}, u32[]{:S(2)}) copy-start(bf16[1,128,2048]{2,1,0:T(8,128)(2,1)} %grad_ref.1) | copy-start | bytes 1572868
  8.5 51.5 %collective-permute-start.8 = (bf16[128,2176]{1,0:T(8,128)(2,1)S(1)}, bf16[128,2176]{1,0:T(8,128)(2,1)S(1)}, u32[]{:S(2)}, u32[]{:S(2)}) collective-permute-start(bf16[128,2176]{1,0:T(8,128)(2,1)S(1)} %get-tuple-element.23), channel_id=1, source_target_pairs={{0,28},{4,0},{8,4},{12,8},{16,12},{20,16},{24,20},{28,24},{1,29},{... | collective-permute-start | bytes 1671176 | tf_op jit(solution)/shard_map/ppermute | solution.py:201
  11.4 13.7 %collective-permute-start.10 = (bf16[32,2048]{1,0:T(8,128)(2,1)S(1)}, bf16[32,2048]{1,0:T(8,128)(2,1)S(1)}, u32[]{:S(2)}, u32[]{:S(2)}) collective-permute-start(bf16[32,2048]{1,0:T(8,128)(2,1)S(1)} %get-tuple-element.25), channel_id=1, source_target_pairs={{0,2},{1,3},{2,0},{3,1},{4,6},{5,7},{6,4},{7,5},{8,10},{9,11},{10,... | collective-permute-start | bytes 393224 | tf_op jit(solution)/shard_map/ppermute | solution.py:197
  14.8 8.4 %collective-permute-start.2 = (bf16[16,2048]{1,0:T(8,128)(2,1)S(1)}, bf16[16,2048]{1,0:T(8,128)(2,1)S(1)}, u32[]{:S(2)}, u32[]{:S(2)}) collective-permute-start(bf16[16,2048]{1,0:T(8,128)(2,1)S(1)} %get-tuple-element.18), channel_id=1, source_target_pairs={{0,2},{1,3},{2,0},{3,1},{4,6},{5,7},{6,4},{7,5},{8,10},{9,11},{10,... | collective-permute-start | bytes 196616 | tf_op jit(solution)/shard_map/ppermute | solution.py:197
  14.8 9.0 %collective-permute-start.1 = (bf16[16,2048]{1,0:T(8,128)(2,1)S(1)}, bf16[16,2048]{1,0:T(8,128)(2,1)S(1)}, u32[]{:S(2)}, u32[]{:S(2)}) collective-permute-start(bf16[16,2048]{1,0:T(8,128)(2,1)S(1)} %get-tuple-element.17.refs_0_), channel_id=1, source_target_pairs={{0,1},{1,0},{2,3},{3,2},{4,5},{5,4},{6,7},{7,6},{8,9},{9,8},{10,11... | collective-permute-start | bytes 196616 | tf_op jit(solution)/shard_map/ppermute | solution.py:197
  23.1 4.9 %collective-permute-start.3 = (bf16[16,2048]{1,0:T(8,128)(2,1)S(1)}, bf16[16,2048]{1,0:T(8,128)(2,1)S(1)}, u32[]{:S(2)}, u32[]{:S(2)}) collective-permute-start(bf16[16,2048]{1,0:T(8,128)(2,1)S(1)} %collective-permute-done.2.refs_2_), channel_id=1, source_target_pairs={{0,1},{1,0},{2,3},{3,2},{4,5},{5,4},{6,7},{7,6},{8,9},{9,8},{10,11... | collective-permute-start | bytes 196616 | tf_op jit(solution)/shard_map/ppermute | solution.py:197
  23.8 13.3 %collective-permute-start.9 = (bf16[32,2048]{1,0:T(8,128)(2,1)S(1)}, bf16[32,2048]{1,0:T(8,128)(2,1)S(1)}, u32[]{:S(2)}, u32[]{:S(2)}) collective-permute-start(bf16[32,2048]{1,0:T(8,128)(2,1)S(1)} %get-tuple-element.24.refs_0_), channel_id=1, source_target_pairs={{0,1},{1,0},{2,3},{3,2},{4,5},{5,4},{6,7},{7,6},{8,9},{9,8},{10,11... | collective-permute-start | bytes 393224 | tf_op jit(solution)/shard_map/ppermute | solution.py:197
  25.2 16.8 %collective-permute-start.11 = (bf16[32,2048]{1,0:T(8,128)(2,1)S(1)}, bf16[32,2048]{1,0:T(8,128)(2,1)S(1)}, u32[]{:S(2)}, u32[]{:S(2)}) collective-permute-start(bf16[32,2048]{1,0:T(8,128)(2,1)S(1)} %collective-permute-done.10.refs_2_), channel_id=1, source_target_pairs={{0,1},{1,0},{2,3},{3,2},{4,5},{5,4},{6,7},{7,6},{8,9},{9,8},{10,11... | collective-permute-start | bytes 393224 | tf_op jit(solution)/shard_map/ppermute | solution.py:197
  28.0 1.9 %copy-start = (bf16[1,768,2048]{2,1,0:T(8,128)(2,1)S(1)}, bf16[1,768,2048]{2,1,0:T(8,128)(2,1)}, u32[]{:S(2)}) copy-start(bf16[1,768,2048]{2,1,0:T(8,128)(2,1)} %refs_5_.3) | copy-start | bytes 9437188
  29.9 1.9 %copy-start.2 = (bf16[1,768,2048]{2,1,0:T(8,128)(2,1)S(1)}, bf16[1,768,2048]{2,1,0:T(8,128)(2,1)}, u32[]{:S(2)}) copy-start(bf16[1,768,2048]{2,1,0:T(8,128)(2,1)} %refs_6_.3) | copy-start | bytes 9437188
  31.8 1.9 %copy-start.4 = (bf16[1,768,2048]{2,1,0:T(8,128)(2,1)S(1)}, bf16[1,768,2048]{2,1,0:T(8,128)(2,1)}, u32[]{:S(2)}) copy-start(bf16[1,768,2048]{2,1,0:T(8,128)(2,1)} %refs_7_.3) | copy-start | bytes 9437188
  33.7 0.7 %copy-start.9 = (f32[1,2048]{1,0:T(1,128)S(1)}, f32[1,2048]{1,0:T(1,128)}, u32[]{:S(2)}) copy-start(f32[1,2048]{1,0:T(1,128)} %refs_4_.3) | copy-start | bytes 24580
  34.4 10.1 %copy-start.1 = (bf16[1,768,2048]{2,1,0:T(8,128)(2,1)S(1)}, bf16[1,768,2048]{2,1,0:T(8,128)(2,1)}, u32[]{:S(2)}) copy-start(bf16[1,768,2048]{2,1,0:T(8,128)(2,1)} %refs_5_.3) | copy-start | bytes 9437188
  34.4 10.1 %copy-start.3 = (bf16[1,768,2048]{2,1,0:T(8,128)(2,1)S(1)}, bf16[1,768,2048]{2,1,0:T(8,128)(2,1)}, u32[]{:S(2)}) copy-start(bf16[1,768,2048]{2,1,0:T(8,128)(2,1)} %refs_6_.3) | copy-start | bytes 9437188
  34.4 10.1 %copy-start.5 = (bf16[1,768,2048]{2,1,0:T(8,128)(2,1)S(1)}, bf16[1,768,2048]{2,1,0:T(8,128)(2,1)}, u32[]{:S(2)}) copy-start(bf16[1,768,2048]{2,1,0:T(8,128)(2,1)} %refs_7_.3) | copy-start | bytes 9437188
  34.4 10.1 %copy-start.10 = (f32[1,2048]{1,0:T(1,128)S(1)}, f32[1,2048]{1,0:T(1,128)}, u32[]{:S(2)}) copy-start(f32[1,2048]{1,0:T(1,128)} %refs_4_.3) | copy-start | bytes 24580
  37.1 4.6 %collective-permute-start.4 = (bf16[16,2048]{1,0:T(8,128)(2,1)S(1)}, bf16[16,2048]{1,0:T(8,128)(2,1)S(1)}, u32[]{:S(2)}, u32[]{:S(2)}) collective-permute-start(bf16[16,2048]{1,0:T(8,128)(2,1)S(1)} %get-tuple-element.19), channel_id=1, source_target_pairs={{0,4},{1,5},{2,6},{3,7},{4,8},{5,9},{6,10},{7,11},{8,12},{9,13},{1... | collective-permute-start | bytes 196616 | tf_op jit(solution)/shard_map/ppermute | solution.py:209
  37.1 11.9 %collective-permute-start.5 = (bf16[16,2048]{1,0:T(8,128)(2,1)S(1)}, bf16[16,2048]{1,0:T(8,128)(2,1)S(1)}, u32[]{:S(2)}, u32[]{:S(2)}) collective-permute-start(bf16[16,2048]{1,0:T(8,128)(2,1)S(1)} %get-tuple-element.20), channel_id=1, source_target_pairs={{0,5},{1,4},{2,7},{3,6},{4,9},{5,8},{6,11},{7,10},{8,13},{9,12},{1... | collective-permute-start | bytes 196616 | tf_op jit(solution)/shard_map/ppermute | solution.py:209
  41.7 10.2 %collective-permute-start.6 = (bf16[16,2048]{1,0:T(8,128)(2,1)S(1)}, bf16[16,2048]{1,0:T(8,128)(2,1)S(1)}, u32[]{:S(2)}, u32[]{:S(2)}) collective-permute-start(bf16[16,2048]{1,0:T(8,128)(2,1)S(1)} %get-tuple-element.21), channel_id=1, source_target_pairs={{0,6},{1,7},{2,4},{3,5},{4,10},{5,11},{6,8},{7,9},{8,14},{9,15},{1... | collective-permute-start | bytes 196616 | tf_op jit(solution)/shard_map/ppermute | solution.py:209
  41.9 10.1 %collective-permute-start.7 = (bf16[16,2048]{1,0:T(8,128)(2,1)S(1)}, bf16[16,2048]{1,0:T(8,128)(2,1)S(1)}, u32[]{:S(2)}, u32[]{:S(2)}) collective-permute-start(bf16[16,2048]{1,0:T(8,128)(2,1)S(1)} %get-tuple-element.22), channel_id=1, source_target_pairs={{0,7},{1,6},{2,5},{3,4},{4,11},{5,10},{6,9},{7,8},{8,15},{9,14},{1... | collective-permute-start | bytes 196616 | tf_op jit(solution)/shard_map/ppermute | solution.py:209
  49.1 7.0 %collective-permute-start.12 = (bf16[16,2048]{1,0:T(8,128)(2,1)S(1)}, bf16[16,2048]{1,0:T(8,128)(2,1)S(1)}, u32[]{:S(2)}, u32[]{:S(2)}) collective-permute-start(bf16[16,2048]{1,0:T(8,128)(2,1)S(1)} %get-tuple-element.26), channel_id=1, source_target_pairs={{0,28},{1,29},{2,30},{3,31},{4,0},{5,1},{6,2},{7,3},{8,4},{9,5},{1... | collective-permute-start | bytes 196616 | tf_op jit(solution)/shard_map/ppermute | solution.py:209
  51.9 5.5 %collective-permute-start.13 = (bf16[16,2048]{1,0:T(8,128)(2,1)S(1)}, bf16[16,2048]{1,0:T(8,128)(2,1)S(1)}, u32[]{:S(2)}, u32[]{:S(2)}) collective-permute-start(bf16[16,2048]{1,0:T(8,128)(2,1)S(1)} %get-tuple-element.27), channel_id=1, source_target_pairs={{0,29},{1,28},{2,31},{3,30},{4,1},{5,0},{6,3},{7,2},{8,5},{9,4},{1... | collective-permute-start | bytes 196616 | tf_op jit(solution)/shard_map/ppermute | solution.py:209
  52.0 5.6 %collective-permute-start.14 = (bf16[16,2048]{1,0:T(8,128)(2,1)S(1)}, bf16[16,2048]{1,0:T(8,128)(2,1)S(1)}, u32[]{:S(2)}, u32[]{:S(2)}) collective-permute-start(bf16[16,2048]{1,0:T(8,128)(2,1)S(1)} %get-tuple-element.28), channel_id=1, source_target_pairs={{0,30},{1,31},{2,28},{3,29},{4,2},{5,3},{6,0},{7,1},{8,6},{9,7},{1... | collective-permute-start | bytes 196616 | tf_op jit(solution)/shard_map/ppermute | solution.py:209
  53.6 6.4 %collective-permute-start.15 = (bf16[16,2048]{1,0:T(8,128)(2,1)S(1)}, bf16[16,2048]{1,0:T(8,128)(2,1)S(1)}, u32[]{:S(2)}, u32[]{:S(2)}) collective-permute-start(bf16[16,2048]{1,0:T(8,128)(2,1)S(1)} %get-tuple-element.29), channel_id=1, source_target_pairs={{0,31},{1,30},{2,29},{3,28},{4,3},{5,2},{6,1},{7,0},{8,7},{9,6},{1... | collective-permute-start | bytes 196616 | tf_op jit(solution)/shard_map/ppermute | solution.py:209

commit v2 on v1

v2 whole, which is shorter than its diff:
```python
import functools

import jax
import jax.numpy as jnp
from jax import lax
from jax.experimental import pallas as pl
from jax.experimental.pallas import tpu as pltpu
from jax.sharding import PartitionSpec as P

EF = 2
CAP = 16
EPSILON = 1e-06
LANES = 128
MIB = 1 << 20

VMEM = pl.BlockSpec(memory_space=pltpu.VMEM)
SMEM = pl.BlockSpec(memory_space=pltpu.SMEM)


ANY = pl.BlockSpec(memory_space=pl.ANY)


def call(body, outs, specs, flops, nbytes, limit, scratch=()):
    return pl.pallas_call(
        body,
        out_shape=outs,
        in_specs=specs,
        out_specs=[VMEM] * len(outs),
        scratch_shapes=scratch,
        compiler_params=pltpu.CompilerParams(vmem_limit_bytes=limit * MIB),
        cost_estimate=pl.CostEstimate(flops=flops, bytes_accessed=nbytes, transcendentals=0),
    )


def bf16(shape):
    return jax.ShapeDtypeStruct(shape, jnp.bfloat16)


def in_hbm(array):
    return pltpu.with_memory_space_constraint(array, pltpu.HBM)


def slot_tables(owner, routes, shares):
    tokens = routes.shape[1]
    slot = lax.broadcasted_iota(jnp.int32, (EF * CAP, tokens), 0)
    first = slot < CAP
    weights = []
    members = []
    for expert in (owner, 1 - owner):
        hit = routes == expert
        members.append(jnp.sum(jnp.where(hit, 1.0, 0.0), axis=0, keepdims=True))
        weights.append(jnp.sum(jnp.where(hit, shares, 0.0), axis=0, keepdims=True))
    member = jnp.where(first, members[0], members[1])
    row = lax.broadcasted_iota(jnp.int32, (tokens, tokens), 0)
    col = lax.broadcasted_iota(jnp.int32, (tokens, tokens), 1)
    earlier = jnp.where(row < col, 1.0, 0.0).astype(jnp.bfloat16)
    rank = jnp.dot(member.astype(jnp.bfloat16), earlier, preferred_element_type=jnp.float32)
    place = (slot % CAP).astype(jnp.float32)
    placed = jnp.where((member > 0.5) & (rank == place), 1.0, 0.0)
    return placed, weights


def turned(table):
    rows, tokens = table.shape
    return jnp.transpose(jnp.concatenate([table, jnp.zeros((LANES - rows, tokens), jnp.float32)], axis=0))


def started(pairs, sem):
    loads = [pltpu.make_async_copy(src, dst, sem.at[i]) for i, (src, dst) in enumerate(pairs)]
    for load in loads:
        load.start()
    return loads


def dispatch(owner_ref, *refs):
    loads = started(list(zip(refs[:7], refs[11:18])), refs[18])
    own_ref, other_ref, forward_ref, backward_ref = refs[7:11]
    routes_f, shares_f, routes_b, shares_b, rows_f, rows_b, grads = refs[11:18]
    owner = owner_ref[0]
    for load in loads[:4]:
        load.wait()
    placed, weights = slot_tables(owner, routes_f[0], shares_f[0])
    pieces = []
    for weight in weights:
        left = weight
        for _ in range(3):
            part = left.astype(jnp.bfloat16).astype(jnp.float32)
            left = left - part
            pieces.append(part)
    pieces.append(jnp.zeros((2, placed.shape[1]), jnp.float32))
    table = jnp.concatenate([placed, *pieces], axis=0)
    forward_ref[...] = turned(table).astype(jnp.bfloat16)
    pick = placed.astype(jnp.bfloat16)
    loads[4].wait()
    slots = jnp.dot(pick, rows_f[0], preferred_element_type=jnp.float32)
    own_ref[:CAP] = slots[:CAP].astype(jnp.bfloat16)
    other_ref[:CAP] = slots[CAP:].astype(jnp.bfloat16)

    placed, weights = slot_tables(owner, routes_b[0], shares_b[0])
    backward_ref[...] = turned(placed).astype(jnp.bfloat16)
    slot = lax.broadcasted_iota(jnp.int32, placed.shape, 0)
    share = placed * jnp.where(slot < CAP, weights[0], weights[1])
    share = jnp.sum(share, axis=1, keepdims=True)
    pick = placed.astype(jnp.bfloat16)
    loads[5].wait()
    slots = jnp.dot(pick, rows_b[0], preferred_element_type=jnp.float32)
    own_ref[CAP : 2 * CAP] = slots[:CAP].astype(jnp.bfloat16)
    other_ref[CAP : 2 * CAP] = slots[CAP:].astype(jnp.bfloat16)
    loads[6].wait()
    slots = share * jnp.dot(pick, grads[0], preferred_element_type=jnp.float32)
    own_ref[2 * CAP :] = slots[:CAP].astype(jnp.bfloat16)
    other_ref[2 * CAP :] = slots[CAP:].astype(jnp.bfloat16)


def load(*refs):
    rows_f, rows_b, table_f, table_b = refs[3:7]
    early_f, early_b, sem = refs[10:]
    width = rows_f.shape[2]
    pairs = [(rows_f.at[0], early_f.at[:, :width]), (rows_b.at[0], early_b.at[:, :width])]
    loads = started(pairs + list(zip(refs[:3], refs[7:10])), sem)
    early_f[:, width:] = table_f[...]
    early_b[:, width:] = table_b[...]
    for each in loads:
        each.wait()


def project(left, right):
    return lax.dot_general(
        left, right, (((1,), (1,)), ((), ())), preferred_element_type=jnp.float32
    )


def unit_rows(rows):
    values = rows.astype(jnp.float32)
    scale = lax.rsqrt(jnp.mean(values * values, axis=-1, keepdims=True) + EPSILON)
    return values * scale, scale


def halving(blocks):
    bits = blocks.bit_length() - 1
    return sorted(range(blocks), key=lambda k: [k >> b & 1 for b in range(bits)])


def give(outs, rows):
    order = halving(rows.shape[0] // CAP)
    rows = jnp.concatenate([rows[k * CAP : (k + 1) * CAP] for k in order], axis=0)
    split = rows.shape[0] // 2
    outs[0][...] = rows[:split]
    outs[1][...] = rows[split:]


def add_received(kept_ref, received_ref, *outs):
    total = kept_ref[...].astype(jnp.float32) + received_ref[...].astype(jnp.float32)
    total = total.astype(jnp.bfloat16)
    split = total.shape[0] // 2
    outs[0][...] = total[:split]
    outs[1][...] = total[split:]


def expert_forward(blocks, *refs):
    rows = jnp.concatenate([ref[:CAP] for ref in refs[:blocks]], axis=0)
    gain_ref, gate_ref, up_ref, down_ref = refs[blocks : blocks + 4]
    outs = refs[blocks + 4 :]
    unit, _ = unit_rows(rows)
    normed = (unit * gain_ref[...]).astype(jnp.bfloat16)
    gate = project(normed, gate_ref[0])
    upper = project(normed, up_ref[0])
    hidden = (gate * jax.nn.sigmoid(gate) * upper).astype(jnp.bfloat16)
    result = jnp.dot(hidden, down_ref[0], preferred_element_type=jnp.float32)
    result = result.astype(jnp.bfloat16)
    give(outs, result)


def expert_backward(blocks, *refs):
    gain_ref, gate_ref, up_ref, down_ref = refs[blocks : blocks + 4]
    outs = refs[blocks + 4 :]
    rows = jnp.concatenate([ref[CAP : 2 * CAP] for ref in refs[:blocks]], axis=0)
    grads = jnp.concatenate([ref[2 * CAP :] for ref in refs[:blocks]], axis=0)
    gain = gain_ref[...]
    unit, scale = unit_rows(rows)
    normed = (unit * gain).astype(jnp.bfloat16)
    hidden_grad = project(grads, down_ref[0])
    gate = project(normed, gate_ref[0])
    upper = project(normed, up_ref[0])
    sigma = jax.nn.sigmoid(gate)
    gate_grad = (hidden_grad * upper * sigma * (1.0 + gate * (1.0 - sigma))).astype(jnp.bfloat16)
    upper_grad = (hidden_grad * gate * sigma).astype(jnp.bfloat16)
    total = jnp.dot(gate_grad, gate_ref[0], preferred_element_type=jnp.float32)
    total = total + jnp.dot(upper_grad, up_ref[0], preferred_element_type=jnp.float32)
    scaled = total * gain
    inner = jnp.mean(scaled * unit, axis=-1, keepdims=True)
    result = (scale * (scaled - unit * inner)).astype(jnp.bfloat16)
    give(outs, result)


def combine_forward(early_ref, own_ref, other_ref, out_ref):
    width = out_ref.shape[2]
    total = early_ref[:, :width].astype(jnp.float32)
    table = early_ref[:, width:]
    for e, part_ref in enumerate((own_ref, other_ref)):
        pick = table[:, e * CAP : (e + 1) * CAP]
        column = EF * CAP + 3 * e
        weight = jnp.sum(
            table[:, column : column + 3].astype(jnp.float32), axis=1, keepdims=True
        )
        total = total + weight * jnp.dot(pick, part_ref[...], preferred_element_type=jnp.float32)
    out_ref[0] = total.astype(jnp.bfloat16)


def combine_backward(early_ref, own_ref, other_ref, out_ref):
    width = out_ref.shape[2]
    pick = early_ref[:, width : width + EF * CAP]
    parts = jnp.concatenate([own_ref[...], other_ref[...]], axis=0)
    total = early_ref[:, :width].astype(jnp.float32)
    total = total + jnp.dot(pick, parts, preferred_element_type=jnp.float32)
    out_ref[0] = total.astype(jnp.bfloat16)


def on_device(
    sections,
    devices,
    forward_input,
    forward_routes,
    forward_shares,
    backward_input,
    backward_routes,
    backward_shares,
    output_grad,
    norm_gain,
    gate_weight,
    up_weight,
    down_weight,
):
    half = devices // EF
    tokens, width = forward_input.shape[1:]
    hidden = gate_weight.shape[1]
    owner = (lax.axis_index("expert") // half).astype(jnp.int32)[None]

    def swapped(block, k):
        return lax.ppermute(block, "expert", [(i, i ^ k) for i in range(devices)])

    def moved(block, distance):
        route = [(i, (i + distance) % sections) for i in range(sections)]
        return lax.ppermute(block, "section", route)

    def returned(block, distance, k):
        route = [
            (s * devices + z, (s + distance) % sections * devices + (z ^ k))
            for s in range(sections)
            for z in range(devices)
        ]
        return lax.ppermute(block, ("section", "expert"), route)

    def gathered(own, other, held):
        blocks = [own]
        far = [swapped(other, half)]
        step = 1
        while step < half:
            blocks = blocks + [swapped(b, step) for b in blocks]
            far, blocks, *held = lax.optimization_barrier((far, blocks, *held))
            far = far + [swapped(b, step) for b in far]
            step *= 2
        return blocks + far, held

    dispatch_bytes = 3 * tokens * width * 2
    lists = forward_routes.shape[:0:-1]
    groups = (forward_routes, forward_shares, backward_routes, backward_shares)
    layers = (forward_input, backward_input, output_grad)
    own, other, table_f, table_b = call(
        dispatch,
        [bf16((3 * CAP, width))] * 2 + [bf16((tokens, LANES))] * 2,
        [SMEM] + [ANY] * 7,
        6 * EF * CAP * tokens * width,
        dispatch_bytes,
        24,
        [pltpu.VMEM((1, *lists), a.dtype) for a in groups]
        + [pltpu.VMEM((1, tokens, width), jnp.bfloat16)] * 3
        + [pltpu.SemaphoreType.DMA((7,))],
    )(owner, *(in_hbm(jnp.swapaxes(a, 1, 2)) for a in groups), *(in_hbm(a) for a in layers))

    weights = (gate_weight, up_weight, down_weight)
    *held, early_f, early_b = call(
        load,
        [pltpu.VMEM(w.shape, w.dtype) for w in weights] + [bf16((tokens, width + LANES))] * 2,
        [ANY] * 5 + [VMEM] * 2,
        0,
        6 * hidden * width * 2,
        8,
        [pltpu.SemaphoreType.DMA((5,))],
    )(*(in_hbm(w) for w in weights), in_hbm(forward_input), in_hbm(output_grad), table_f, table_b)
    early_b = moved(early_b, -1)
    early_f = moved(early_f, 1)
    blocks, held = gathered(own, other, held)

    rows = devices * CAP
    weight_bytes = 3 * hidden * width * 2
    outs = [bf16((rows // 2, width))] * 2
    parts_f = call(
        functools.partial(expert_forward, devices),
        outs,
        [VMEM] * (devices + 4),
        6 * rows * hidden * width,
        weight_bytes,
        24,
    )(*blocks, norm_gain, *held)
    parts_b = call(
        functools.partial(expert_backward, devices),
        outs,
        [VMEM] * (devices + 4),
        10 * rows * hidden * width,
        weight_bytes,
        24,
    )(*blocks, norm_gain, *held)

    def handed_back(kept, given, distance):
        step = 1
        while step < half:
            quarter = kept.shape[0] // 2
            kept, given = call(
                add_received,
                [bf16((quarter, width))] * 2,
                [VMEM] * 2,
                0,
                6 * kept.shape[0] * width,
                8,
            )(kept, swapped(given, step))
            step *= 2
        return returned(kept, distance, 0), returned(given, distance, half)

    parts_f = handed_back(*parts_f, 1)
    parts_b = handed_back(*parts_b, -1)
    result = [bf16((1, tokens, width))]
    combine_flops = 2 * tokens * EF * CAP * width
    (next_input,) = call(
        combine_forward, result, [VMEM] * 3, combine_flops, dispatch_bytes, 24
    )(early_f, *parts_f)
    (previous_gradient,) = call(
        combine_backward, result, [VMEM] * 3, combine_flops, dispatch_bytes, 24
    )(early_b, *parts_b)
    return next_input, previous_gradient


def solution(mesh):
    rows = P("section", "expert", None)
    return jax.shard_map(
        functools.partial(on_device, mesh.shape["section"], mesh.shape["expert"]),
        mesh=mesh,
        in_specs=(rows,) * 7 + (P("section", None),) + (rows,) * 3,
        out_specs=(rows, rows),
        check_vma=False,
    )
```

time: 62.2 us -> 45.2 us (0.73)
  local copies, waits for them, and re-layouts: 12.6 us -> 0.01 us
  waiting for transfers between devices: 15.2 us -> 6 us
  Pallas kernels: 10.6 us -> 15.6 us
    unnamed x26 -> x2, local copies, waits for them, and re-layouts: 12.6 us -> 0.01 us
    ppermute x8 -> x4, waiting for transfers between devices: 6.58 us -> 0.65 us  [returned(): return lax.ppermute(block, ('section', 'expert'), route)]
    pallas_call x4 -> x6, Pallas kernels: 3.5 us -> 8.43 us  [the longest x1 4.13 us: on_device(): call(load, [pltpu.VMEM(w.shape, w.dtype) for w in weights] + [bf16((token...]
    ppermute x6 -> x5, waiting for transfers between devices: 8.66 us -> 5.35 us  [swapped(): return lax.ppermute(block, 'expert', [(i, i ^ k) for i in range(devices)])]
    ppermute x6 -> x5, starting transfers between devices: 7.94 us -> 9.31 us  [swapped(): return lax.ppermute(block, 'expert', [(i, i ^ k) for i in range(devices)])]
    ppermute x2, starting transfers between devices: 3.45 us -> 2.69 us  [moved(): return lax.ppermute(block, 'section', route)]
    ppermute x8 -> x4, starting transfers between devices: 10.5 us -> 10.4 us  [returned(): return lax.ppermute(block, ('section', 'expert'), route)]
  transfers between devices with their start and end apart: 16 -> 11, of which waited for: 6 -> 4; matrix products, arithmetic and copies ran while one was open for 3% -> 0% of each run, Pallas kernels for 15% -> 28%
where the time goes in v2:
time: 45.2 us; the launch traced here: 44.7 us
  starting transfers between devices  22.4 us (50%)
  Pallas kernels  15.6 us (35%)
  waiting for transfers between devices  6 us (13%)
  between operations  0.7 us (2%)
    ppermute x4, starting transfers between devices, returned(): return lax.ppermute(block, ('section', 'expert'), route)  10.4 us
    ppermute x5, starting transfers between devices, swapped(): return lax.ppermute(block, 'expert', [(i, i ^ k) for i in range(devices)])  9.31 us
    ppermute x5, waiting for transfers between devices, swapped(): return lax.ppermute(block, 'expert', [(i, i ^ k) for i in range(devices)])  5.35 us
    pallas_call x1, Pallas kernels, on_device(): call(functools.partial(expert_backward, devices), outs, [VMEM] * (devices...  4.51 us
    pallas_call x1, Pallas kernels, on_device(): call(load, [pltpu.VMEM(w.shape, w.dtype) for w in weights] + [bf16((token...  4.13 us
    ppermute x2, starting transfers between devices, moved(): return lax.ppermute(block, 'section', route)  2.69 us
    pallas_call x1, Pallas kernels, on_device(): call(functools.partial(expert_forward, devices), outs, [VMEM] * (devices...  2.64 us
    pallas_call x1, Pallas kernels, on_device(): call(dispatch, [bf16((3 * CAP, width))] * 2 + [bf16((tokens, LANES))] * 2...  1.92 us
  transfers between devices with their start and end apart: 11, of which 4 were waited for; matrix products, arithmetic and copies ran while one was open for 0% of the time, Pallas kernels for 28%

profile of v2, /device:TPU:0, one launch (start us, length us, event | category | flops | bytes accessed | tf_op | source)
XLA Modules:
  0.0 44.7 jit_solution(15108929141510408275)
XLA Ops:
  0.6 1.9 %shard_map.122 = (bf16[48,2048]{1,0:T(8,128)(2,1)S(1)}, bf16[48,2048]{1,0:T(8,128)(2,1)S(1)}, bf16[128,128]{1,0:T(8,128)(2,1)S(1)}, bf16[128,128]{1,0:T(8,128)(2,1)S(1)}) custom-call(s32[1]{0:T(128)} %bitcast.owner_ref, s32[1,8,128]{2,1,0:T(8,128)} %bitcast.5, f32[1,8,128]{2,1,0:T(8,128)} %bitcast.6, s32[1,8,128]{2,1,0:T(8,128)} %bitcast.7, ...), custom_call_target="tpu_custom_call" | custom-call | flops 50331648 | bytes 1572864 | tf_op jit(solution)/shard_map/pallas_call | solution.py:269
  2.6 4.1 %collective-permute-start.1 = (bf16[48,2048]{1,0:T(8,128)(2,1)S(1)}, bf16[48,2048]{1,0:T(8,128)(2,1)S(1)}, u32[]{:S(2)}, u32[]{:S(2)}) collective-permute-start(bf16[48,2048]{1,0:T(8,128)(2,1)S(1)} %get-tuple-element.28), channel_id=1, source_target_pairs={{0,2},{1,3},{2,0},{3,1},{4,6},{5,7},{6,4},{7,5},{8,10},{9,11},{10,... | collective-permute-start | bytes 589832 | tf_op jit(solution)/shard_map/ppermute | solution.py:240
  6.7 1.6 %collective-permute-start.2 = (bf16[48,2048]{1,0:T(8,128)(2,1)S(1)}, bf16[48,2048]{1,0:T(8,128)(2,1)S(1)}, u32[]{:S(2)}, u32[]{:S(2)}) collective-permute-start(bf16[48,2048]{1,0:T(8,128)(2,1)S(1)} %get-tuple-element.33.refs_0_), channel_id=1, source_target_pairs={{0,1},{1,0},{2,3},{3,2},{4,5},{5,4},{6,7},{7,6},{8,9},{9,8},{10,11... | collective-permute-start | bytes 589832 | tf_op jit(solution)/shard_map/ppermute | solution.py:240
  8.2 0.0 copy-start
  8.2 4.1 %shard_map.123 = (bf16[1,768,2048]{2,1,0:T(8,128)(2,1)S(1)}, bf16[1,768,2048]{2,1,0:T(8,128)(2,1)S(1)}, bf16[1,768,2048]{2,1,0:T(8,128)(2,1)S(1)}, bf16[128,2176]{1,0:T(8,128)(2,1)S(1)}, bf16[128,2176]{1,0:T(8,128)(2,1)S(1)}) custom-call(bf16[1,768,2048]{2,1,0:T(8,128)(2,1)} %refs_0_.1, bf16[1,768,2048]{2,1,0:T(8,128)(2,1)} %refs_1_.1, ...), custom_call_target="tpu_custom_call" | custom-call | bytes 18874368 | tf_op jit(solution)/shard_map/pallas_call | solution.py:282
  12.4 0.1 collective-permute-start
  12.4 2.6 %collective-permute-start.7 = (bf16[128,2176]{1,0:T(8,128)(2,1)S(1)}, bf16[128,2176]{1,0:T(8,128)(2,1)S(1)}, u32[]{:S(2)}, u32[]{:S(2)}) collective-permute-start(bf16[128,2176]{1,0:T(8,128)(2,1)S(1)} %get-tuple-element.43), channel_id=1, source_target_pairs={{0,28},{4,0},{8,4},{12,8},{16,12},{20,16},{24,20},{28,24},{1,29},{... | collective-permute-start | bytes 1671176 | tf_op jit(solution)/shard_map/ppermute | solution.py:244
  15.1 0.8 %collective-permute-done.1.refs_2_ = bf16[48,2048]{1,0:T(8,128)(2,1)S(1)} collective-permute-done((bf16[48,2048]{1,0:T(8,128)(2,1)S(1)}, bf16[48,2048]{1,0:T(8,128)(2,1)S(1)}, u32[]{:S(2)}, u32[]{:S(2)}) %collective-permute-start.1) | collective-permute-done | bytes 196640 | tf_op jit(solution)/shard_map/ppermute | solution.py:240
  15.9 0.2 collective-permute-done.2.refs_1_
  16.1 1.5 %collective-permute-start.3 = (bf16[48,2048]{1,0:T(8,128)(2,1)S(1)}, bf16[48,2048]{1,0:T(8,128)(2,1)S(1)}, u32[]{:S(2)}, u32[]{:S(2)}) collective-permute-start(bf16[48,2048]{1,0:T(8,128)(2,1)S(1)} %collective-permute-done.1.refs_2_), channel_id=1, source_target_pairs={{0,1},{1,0},{2,3},{3,2},{4,5},{5,4},{6,7},{7,6},{8,9},{9,8},{10,11... | collective-permute-start | bytes 589832 | tf_op jit(solution)/shard_map/ppermute | solution.py:240
  17.6 4.3 %collective-permute-done.3.refs_3_ = bf16[48,2048]{1,0:T(8,128)(2,1)S(1)} collective-permute-done((bf16[48,2048]{1,0:T(8,128)(2,1)S(1)}, bf16[48,2048]{1,0:T(8,128)(2,1)S(1)}, u32[]{:S(2)}, u32[]{:S(2)}) %collective-permute-start.3) | collective-permute-done | bytes 196640 | tf_op jit(solution)/shard_map/ppermute | solution.py:240
  21.9 0.0 copy-done
  21.9 2.6 %shard_map.124 = (bf16[32,2048]{1,0:T(8,128)(2,1)S(1)}, bf16[32,2048]{1,0:T(8,128)(2,1)S(1)}) custom-call(bf16[48,2048]{1,0:T(8,128)(2,1)S(1)} %get-tuple-element.33.refs_0_, bf16[48,2048]{1,0:T(8,128)(2,1)S(1)} %collective-permute-done.2.refs_1_, bf16[48,2048]{1,0:T(8,128)(2,1)S(1)} %collective-permute-done.1.refs_2_, ...), custom_call_target="tpu_custom_call" | custom-call | flops 603979776 | bytes 9437184 | tf_op jit(solution)/shard_map/pallas_call | solution.py:298
  24.6 1.5 %collective-permute-start.4 = (bf16[32,2048]{1,0:T(8,128)(2,1)S(1)}, bf16[32,2048]{1,0:T(8,128)(2,1)S(1)}, u32[]{:S(2)}, u32[]{:S(2)}) collective-permute-start(bf16[32,2048]{1,0:T(8,128)(2,1)S(1)} %get-tuple-element.40), channel_id=1, source_target_pairs={{0,1},{1,0},{2,3},{3,2},{4,5},{5,4},{6,7},{7,6},{8,9},{9,8},{10,11... | collective-permute-start | bytes 393224 | tf_op jit(solution)/shard_map/ppermute | solution.py:240
  26.0 4.5 %shard_map.127 = (bf16[32,2048]{1,0:T(8,128)(2,1)S(1)}, bf16[32,2048]{1,0:T(8,128)(2,1)S(1)}) custom-call(bf16[48,2048]{1,0:T(8,128)(2,1)S(1)} %get-tuple-element.33.refs_0_, bf16[48,2048]{1,0:T(8,128)(2,1)S(1)} %collective-permute-done.2.refs_1_, bf16[48,2048]{1,0:T(8,128)(2,1)S(1)} %collective-permute-done.1.refs_2_, ...), custom_call_target="tpu_custom_call" | custom-call | flops 1006632960 | bytes 9437184 | tf_op jit(solution)/shard_map/pallas_call | solution.py:306
  30.6 0.7 %collective-permute-start.8 = (bf16[32,2048]{1,0:T(8,128)(2,1)S(1)}, bf16[32,2048]{1,0:T(8,128)(2,1)S(1)}, u32[]{:S(2)}, u32[]{:S(2)}) collective-permute-start(bf16[32,2048]{1,0:T(8,128)(2,1)S(1)} %get-tuple-element.45), channel_id=1, source_target_pairs={{0,1},{1,0},{2,3},{3,2},{4,5},{5,4},{6,7},{7,6},{8,9},{9,8},{10,11... | collective-permute-start | bytes 393224 | tf_op jit(solution)/shard_map/ppermute | solution.py:240
  31.2 0.0 collective-permute-done.4.received_ref
  31.3 0.1 collective-permute-start.5
  31.3 4.3 %collective-permute-start.6 = (bf16[16,2048]{1,0:T(8,128)(2,1)S(1)}, bf16[16,2048]{1,0:T(8,128)(2,1)S(1)}, u32[]{:S(2)}, u32[]{:S(2)}) collective-permute-start(bf16[16,2048]{1,0:T(8,128)(2,1)S(1)} %get-tuple-element.42), channel_id=1, source_target_pairs={{0,6},{1,7},{2,4},{3,5},{4,10},{5,11},{6,8},{7,9},{8,14},{9,15},{1... | collective-permute-start | bytes 196616 | tf_op jit(solution)/shard_map/ppermute | solution.py:252
  35.6 0.0 collective-permute-done.8.received_ref
  35.6 1.0 %collective-permute-start.9 = (bf16[16,2048]{1,0:T(8,128)(2,1)S(1)}, bf16[16,2048]{1,0:T(8,128)(2,1)S(1)}, u32[]{:S(2)}, u32[]{:S(2)}) collective-permute-start(bf16[16,2048]{1,0:T(8,128)(2,1)S(1)} %get-tuple-element.46), channel_id=1, source_target_pairs={{0,28},{1,29},{2,30},{3,31},{4,0},{5,1},{6,2},{7,3},{8,4},{9,5},{1... | collective-permute-start | bytes 196616 | tf_op jit(solution)/shard_map/ppermute | solution.py:252
  36.6 0.0 collective-permute-done.early_ref
  36.6 5.1 %collective-permute-start.10 = (bf16[16,2048]{1,0:T(8,128)(2,1)S(1)}, bf16[16,2048]{1,0:T(8,128)(2,1)S(1)}, u32[]{:S(2)}, u32[]{:S(2)}) collective-permute-start(bf16[16,2048]{1,0:T(8,128)(2,1)S(1)} %get-tuple-element.47), channel_id=1, source_target_pairs={{0,30},{1,31},{2,28},{3,29},{4,2},{5,3},{6,0},{7,1},{8,6},{9,7},{1... | collective-permute-start | bytes 196616 | tf_op jit(solution)/shard_map/ppermute | solution.py:252
  41.8 0.0 collective-permute-done.5.own_ref
  41.8 0.0 collective-permute-done.6.other_ref
  41.8 1.2 %shard_map.126 = bf16[1,128,2048]{2,1,0:T(8,128)(2,1)} custom-call(bf16[128,2176]{1,0:T(8,128)(2,1)S(1)} %collective-permute-done.early_ref, bf16[16,2048]{1,0:T(8,128)(2,1)S(1)} %collective-permute-done.5.own_ref, bf16[16,2048]{1,0:T(8,128)(2,1)S(1)} %collective-permute-done.6.other_ref), custom_call_target="tpu_custom_call" | custom-call | flops 16777216 | bytes 1572864 | tf_op jit(solution)/shard_map/pallas_call | solution.py:334
  43.0 0.0 collective-permute-done.7.early_ref
  43.0 0.0 collective-permute-done.9.own_ref
  43.0 0.6 %collective-permute-done.10.other_ref = bf16[16,2048]{1,0:T(8,128)(2,1)S(1)} collective-permute-done((bf16[16,2048]{1,0:T(8,128)(2,1)S(1)}, bf16[16,2048]{1,0:T(8,128)(2,1)S(1)}, u32[]{:S(2)}, u32[]{:S(2)}) %collective-permute-start.10) | collective-permute-done | bytes 65568 | tf_op jit(solution)/shard_map/ppermute | solution.py:252
  43.7 1.1 %shard_map.129 = bf16[1,128,2048]{2,1,0:T(8,128)(2,1)} custom-call(bf16[128,2176]{1,0:T(8,128)(2,1)S(1)} %collective-permute-done.7.early_ref, bf16[16,2048]{1,0:T(8,128)(2,1)S(1)} %collective-permute-done.9.own_ref, bf16[16,2048]{1,0:T(8,128)(2,1)S(1)} %collective-permute-done.10.other_ref), custom_call_target="tpu_custom_call" | custom-call | flops 16777216 | bytes 1572864 | tf_op jit(solution)/shard_map/pallas_call | solution.py:337
  (2 shorter events, 0.1 us)
Async XLA Ops:
  2.6 13.3 %collective-permute-start.1 = (bf16[48,2048]{1,0:T(8,128)(2,1)S(1)}, bf16[48,2048]{1,0:T(8,128)(2,1)S(1)}, u32[]{:S(2)}, u32[]{:S(2)}) collective-permute-start(bf16[48,2048]{1,0:T(8,128)(2,1)S(1)} %get-tuple-element.28), channel_id=1, source_target_pairs={{0,2},{1,3},{2,0},{3,1},{4,6},{5,7},{6,4},{7,5},{8,10},{9,11},{10,... | collective-permute-start | bytes 589832 | tf_op jit(solution)/shard_map/ppermute | solution.py:240
  6.7 9.4 %collective-permute-start.2 = (bf16[48,2048]{1,0:T(8,128)(2,1)S(1)}, bf16[48,2048]{1,0:T(8,128)(2,1)S(1)}, u32[]{:S(2)}, u32[]{:S(2)}) collective-permute-start(bf16[48,2048]{1,0:T(8,128)(2,1)S(1)} %get-tuple-element.33.refs_0_), channel_id=1, source_target_pairs={{0,1},{1,0},{2,3},{3,2},{4,5},{5,4},{6,7},{7,6},{8,9},{9,8},{10,11... | collective-permute-start | bytes 589832 | tf_op jit(solution)/shard_map/ppermute | solution.py:240
  8.2 13.7 %copy-start = (f32[1,2048]{1,0:T(1,128)S(1)}, f32[1,2048]{1,0:T(1,128)}, u32[]{:S(2)}) copy-start(f32[1,2048]{1,0:T(1,128)} %refs_4_.7) | copy-start | bytes 24580
  12.4 24.2 %collective-permute-start = (bf16[128,2176]{1,0:T(8,128)(2,1)S(1)}, bf16[128,2176]{1,0:T(8,128)(2,1)S(1)}, u32[]{:S(2)}, u32[]{:S(2)}) collective-permute-start(bf16[128,2176]{1,0:T(8,128)(2,1)S(1)} %get-tuple-element.27), channel_id=1, source_target_pairs={{0,4},{4,8},{8,12},{12,16},{16,20},{20,24},{24,28},{28,0},{1,5},{5... | collective-permute-start | bytes 1671176 | tf_op jit(solution)/shard_map/ppermute | solution.py:244
  12.4 30.6 %collective-permute-start.7 = (bf16[128,2176]{1,0:T(8,128)(2,1)S(1)}, bf16[128,2176]{1,0:T(8,128)(2,1)S(1)}, u32[]{:S(2)}, u32[]{:S(2)}) collective-permute-start(bf16[128,2176]{1,0:T(8,128)(2,1)S(1)} %get-tuple-element.43), channel_id=1, source_target_pairs={{0,28},{4,0},{8,4},{12,8},{16,12},{20,16},{24,20},{28,24},{1,29},{... | collective-permute-start | bytes 1671176 | tf_op jit(solution)/shard_map/ppermute | solution.py:244
  16.1 5.8 %collective-permute-start.3 = (bf16[48,2048]{1,0:T(8,128)(2,1)S(1)}, bf16[48,2048]{1,0:T(8,128)(2,1)S(1)}, u32[]{:S(2)}, u32[]{:S(2)}) collective-permute-start(bf16[48,2048]{1,0:T(8,128)(2,1)S(1)} %collective-permute-done.1.refs_2_), channel_id=1, source_target_pairs={{0,1},{1,0},{2,3},{3,2},{4,5},{5,4},{6,7},{7,6},{8,9},{9,8},{10,11... | collective-permute-start | bytes 589832 | tf_op jit(solution)/shard_map/ppermute | solution.py:240
  24.6 6.7 %collective-permute-start.4 = (bf16[32,2048]{1,0:T(8,128)(2,1)S(1)}, bf16[32,2048]{1,0:T(8,128)(2,1)S(1)}, u32[]{:S(2)}, u32[]{:S(2)}) collective-permute-start(bf16[32,2048]{1,0:T(8,128)(2,1)S(1)} %get-tuple-element.40), channel_id=1, source_target_pairs={{0,1},{1,0},{2,3},{3,2},{4,5},{5,4},{6,7},{7,6},{8,9},{9,8},{10,11... | collective-permute-start | bytes 393224 | tf_op jit(solution)/shard_map/ppermute | solution.py:240
  30.6 5.0 %collective-permute-start.8 = (bf16[32,2048]{1,0:T(8,128)(2,1)S(1)}, bf16[32,2048]{1,0:T(8,128)(2,1)S(1)}, u32[]{:S(2)}, u32[]{:S(2)}) collective-permute-start(bf16[32,2048]{1,0:T(8,128)(2,1)S(1)} %get-tuple-element.45), channel_id=1, source_target_pairs={{0,1},{1,0},{2,3},{3,2},{4,5},{5,4},{6,7},{7,6},{8,9},{9,8},{10,11... | collective-permute-start | bytes 393224 | tf_op jit(solution)/shard_map/ppermute | solution.py:240
  31.3 10.5 %collective-permute-start.5 = (bf16[16,2048]{1,0:T(8,128)(2,1)S(1)}, bf16[16,2048]{1,0:T(8,128)(2,1)S(1)}, u32[]{:S(2)}, u32[]{:S(2)}) collective-permute-start(bf16[16,2048]{1,0:T(8,128)(2,1)S(1)} %get-tuple-element.41), channel_id=1, source_target_pairs={{0,4},{1,5},{2,6},{3,7},{4,8},{5,9},{6,10},{7,11},{8,12},{9,13},{1... | collective-permute-start | bytes 196616 | tf_op jit(solution)/shard_map/ppermute | solution.py:252
  31.3 10.4 %collective-permute-start.6 = (bf16[16,2048]{1,0:T(8,128)(2,1)S(1)}, bf16[16,2048]{1,0:T(8,128)(2,1)S(1)}, u32[]{:S(2)}, u32[]{:S(2)}) collective-permute-start(bf16[16,2048]{1,0:T(8,128)(2,1)S(1)} %get-tuple-element.42), channel_id=1, source_target_pairs={{0,6},{1,7},{2,4},{3,5},{4,10},{5,11},{6,8},{7,9},{8,14},{9,15},{1... | collective-permute-start | bytes 196616 | tf_op jit(solution)/shard_map/ppermute | solution.py:252
  35.6 7.4 %collective-permute-start.9 = (bf16[16,2048]{1,0:T(8,128)(2,1)S(1)}, bf16[16,2048]{1,0:T(8,128)(2,1)S(1)}, u32[]{:S(2)}, u32[]{:S(2)}) collective-permute-start(bf16[16,2048]{1,0:T(8,128)(2,1)S(1)} %get-tuple-element.46), channel_id=1, source_target_pairs={{0,28},{1,29},{2,30},{3,31},{4,0},{5,1},{6,2},{7,3},{8,4},{9,5},{1... | collective-permute-start | bytes 196616 | tf_op jit(solution)/shard_map/ppermute | solution.py:252
  36.6 7.0 %collective-permute-start.10 = (bf16[16,2048]{1,0:T(8,128)(2,1)S(1)}, bf16[16,2048]{1,0:T(8,128)(2,1)S(1)}, u32[]{:S(2)}, u32[]{:S(2)}) collective-permute-start(bf16[16,2048]{1,0:T(8,128)(2,1)S(1)} %get-tuple-element.47), channel_id=1, source_target_pairs={{0,30},{1,31},{2,28},{3,29},{4,2},{5,3},{6,0},{7,1},{8,6},{9,7},{1... | collective-permute-start | bytes 196616 | tf_op jit(solution)/shard_map/ppermute | solution.py:252

commit v3 on v2

--- a/solution.py
+++ b/solution.py
@@ -112,22 +112,31 @@
     other_ref[2 * CAP :] = slots[CAP:].astype(jnp.bfloat16)
 
 
-def load(*refs):
-    rows_f, rows_b, table_f, table_b = refs[3:7]
-    early_f, early_b, sem = refs[10:]
+def load(pieces, rows_f, rows_b, table_f, table_b, *refs):
+    *refs, early_sem, sem = refs
+    count = (len(refs) - 2) // 3
+    early_f, early_b = refs[count : count + 2]
+    source, held, turned_ref = refs[:count], refs[count + 2 : -count], refs[-count:]
     width = rows_f.shape[2]
-    pairs = [(rows_f.at[0], early_f.at[:, :width]), (rows_b.at[0], early_b.at[:, :width])]
-    loads = started(pairs + list(zip(refs[:3], refs[7:10])), sem)
+    size = held[0].shape[1] // pieces
+    spans = [pl.ds(piece * size, size) for piece in range(pieces)]
+    pairs = [(src.at[0, span], dst.at[0, span]) for span in spans for src, dst in zip(source, held)]
+    loads = started(pairs, sem)
+    early = started(
+        [(rows_f.at[0], early_f.at[:, :width]), (rows_b.at[0], early_b.at[:, :width])], early_sem
+    )
     early_f[:, width:] = table_f[...]
     early_b[:, width:] = table_b[...]
-    for each in loads:
+    for piece, span in enumerate(spans):
+        for i in range(count):
+            loads[piece * count + i].wait()
+            turned_ref[i][:, span] = held[i][0, span].T
+    for each in early:
         each.wait()
 
 
-def project(left, right):
-    return lax.dot_general(
-        left, right, (((1,), (1,)), ((), ())), preferred_element_type=jnp.float32
-    )
+def product(left, right_ref):
+    return jnp.dot(left, right_ref[...], preferred_element_type=jnp.float32)
 
 
 def unit_rows(rows):
@@ -158,39 +167,34 @@
 
 
 def expert_forward(blocks, *refs):
-    rows = jnp.concatenate([ref[:CAP] for ref in refs[:blocks]], axis=0)
-    gain_ref, gate_ref, up_ref, down_ref = refs[blocks : blocks + 4]
-    outs = refs[blocks + 4 :]
-    unit, _ = unit_rows(rows)
+    gain_ref, gate_turned, up_turned, down_ref = refs[blocks : blocks + 4]
+    kept_ref, given_ref, to_gate_ref, to_up_ref = refs[blocks + 4 :]
+    rows = [ref[:CAP] for ref in refs[:blocks]] + [ref[CAP : 2 * CAP] for ref in refs[:blocks]]
+    unit, _ = unit_rows(jnp.concatenate(rows, axis=0))
     normed = (unit * gain_ref[...]).astype(jnp.bfloat16)
-    gate = project(normed, gate_ref[0])
-    upper = project(normed, up_ref[0])
-    hidden = (gate * jax.nn.sigmoid(gate) * upper).astype(jnp.bfloat16)
-    result = jnp.dot(hidden, down_ref[0], preferred_element_type=jnp.float32)
-    result = result.astype(jnp.bfloat16)
-    give(outs, result)
+    gate = product(normed, gate_turned)
+    upper = product(normed, up_turned)
+    split = blocks * CAP
+    sigma = jax.nn.sigmoid(gate)
+    passed = gate * sigma
+    hidden = (passed[:split] * upper[:split]).astype(jnp.bfloat16)
+    to_up_ref[...] = passed[split:]
+    to_gate_ref[...] = (upper * sigma * (1.0 + gate * (1.0 - sigma)))[split:]
+    give((kept_ref, given_ref), product(hidden, down_ref.at[0]).astype(jnp.bfloat16))
 
 
 def expert_backward(blocks, *refs):
-    gain_ref, gate_ref, up_ref, down_ref = refs[blocks : blocks + 4]
-    outs = refs[blocks + 4 :]
+    gain_ref, to_gate_ref, to_up_ref, gate_ref, up_ref, down_turned = refs[blocks : blocks + 6]
+    grads = jnp.concatenate([ref[2 * CAP :] for ref in refs[:blocks]], axis=0)
+    hidden_grad = product(grads, down_turned)
+    gate_grad = (hidden_grad * to_gate_ref[...]).astype(jnp.bfloat16)
+    upper_grad = (hidden_grad * to_up_ref[...]).astype(jnp.bfloat16)
+    total = product(gate_grad, gate_ref.at[0]) + product(upper_grad, up_ref.at[0])
     rows = jnp.concatenate([ref[CAP : 2 * CAP] for ref in refs[:blocks]], axis=0)
-    grads = jnp.concatenate([ref[2 * CAP :] for ref in refs[:blocks]], axis=0)
-    gain = gain_ref[...]
     unit, scale = unit_rows(rows)
-    normed = (unit * gain).astype(jnp.bfloat16)
-    hidden_grad = project(grads, down_ref[0])
-    gate = project(normed, gate_ref[0])
-    upper = project(normed, up_ref[0])
-    sigma = jax.nn.sigmoid(gate)
-    gate_grad = (hidden_grad * upper * sigma * (1.0 + gate * (1.0 - sigma))).astype(jnp.bfloat16)
-    upper_grad = (hidden_grad * gate * sigma).astype(jnp.bfloat16)
-    total = jnp.dot(gate_grad, gate_ref[0], preferred_element_type=jnp.float32)
-    total = total + jnp.dot(upper_grad, up_ref[0], preferred_element_type=jnp.float32)
-    scaled = total * gain
+    scaled = total * gain_ref[...]
     inner = jnp.mean(scaled * unit, axis=-1, keepdims=True)
-    result = (scale * (scaled - unit * inner)).astype(jnp.bfloat16)
-    give(outs, result)
+    give(refs[blocks + 6 :], (scale * (scaled - unit * inner)).astype(jnp.bfloat16))
 
 
 def combine_forward(early_ref, own_ref, other_ref, out_ref):
@@ -279,38 +283,49 @@
     )(owner, *(in_hbm(jnp.swapaxes(a, 1, 2)) for a in groups), *(in_hbm(a) for a in layers))
 
     weights = (gate_weight, up_weight, down_weight)
-    *held, early_f, early_b = call(
-        load,
-        [pltpu.VMEM(w.shape, w.dtype) for w in weights] + [bf16((tokens, width + LANES))] * 2,
-        [ANY] * 5 + [VMEM] * 2,
+    pieces = 3 if hidden % (3 * LANES) == 0 else 1
+    early_f, early_b, *held = call(
+        functools.partial(load, pieces),
+        [bf16((tokens, width + LANES))] * 2
+        + [pltpu.VMEM(w.shape, w.dtype) for w in weights]
+        + [pltpu.VMEM((width, hidden), w.dtype) for w in weights],
+        [ANY] * 2 + [VMEM] * 2 + [ANY] * 3,
         0,
-        6 * hidden * width * 2,
+        12 * hidden * width * 2,
         8,
-        [pltpu.SemaphoreType.DMA((5,))],
-    )(*(in_hbm(w) for w in weights), in_hbm(forward_input), in_hbm(output_grad), table_f, table_b)
+        [pltpu.SemaphoreType.DMA((2,)), pltpu.SemaphoreType.DMA((3 * pieces,))],
+    )(
+        in_hbm(forward_input),
+        in_hbm(output_grad),
+        table_f,
+        table_b,
+        *(in_hbm(w) for w in weights),
+    )
     early_b = moved(early_b, -1)
     early_f = moved(early_f, 1)
     blocks, held = gathered(own, other, held)
+    gate, up, down, gate_turned, up_turned, down_turned = held
 
     rows = devices * CAP
     weight_bytes = 3 * hidden * width * 2
     outs = [bf16((rows // 2, width))] * 2
-    parts_f = call(
+    factor = jax.ShapeDtypeStruct((rows, hidden), jnp.float32)
+    *parts_f, to_gate, to_up = call(
         functools.partial(expert_forward, devices),
-        outs,
+        outs + [factor] * 2,
         [VMEM] * (devices + 4),
-        6 * rows * hidden * width,
+        10 * rows * hidden * width,
         weight_bytes,
-        24,
-    )(*blocks, norm_gain, *held)
+        16,
+    )(*blocks, norm_gain, gate_turned, up_turned, down)
     parts_b = call(
         functools.partial(expert_backward, devices),
         outs,
-        [VMEM] * (devices + 4),
-        10 * rows * hidden * width,
+        [VMEM] * (devices + 6),
+        6 * rows * hidden * width,
         weight_bytes,
-        24,
-    )(*blocks, norm_gain, *held)
+        16,
+    )(*blocks, norm_gain, to_gate, to_up, gate, up, down_turned)
 
     def handed_back(kept, given, distance):
         step = 1

time: 45.2 us -> 41 us (0.907)
  Pallas kernels: 15.6 us -> 12.5 us
  starting transfers between devices: 22.4 us -> 20.2 us
  waiting for transfers between devices: 6 us -> 7.47 us
    pallas_call x1, Pallas kernels: 4.51 us -> 2.2 us  [on_device(): call(functools.partial(expert_backward, devices), outs, [VMEM] * (devices...]
    ppermute x4, starting transfers between devices: 10.4 us -> 8.17 us  [returned(): return lax.ppermute(block, ('section', 'expert'), route)]
    ppermute x5, waiting for transfers between devices: 5.35 us -> 6.82 us  [swapped(): return lax.ppermute(block, 'expert', [(i, i ^ k) for i in range(devices)])]
    pallas_call x2, Pallas kernels: 6.77 us -> 6 us  [the longest x1 4.31 us: on_device(): call(functools.partial(load, pieces), [bf16((tokens, width + LANES))] * 2...]
  transfers between devices with their start and end apart: 11 -> 11, of which waited for: 4 -> 5; matrix products, arithmetic and copies ran while one was open for 0% -> 0% of each run, Pallas kernels for 28% -> 23%
where the time goes in v3:
time: 41 us; the launch traced here: 40.9 us
  starting transfers between devices  20.2 us (49%)
  Pallas kernels  12.5 us (30%)
  waiting for transfers between devices  7.47 us (18%)
  between operations  0.7 us (2%)
    ppermute x5, starting transfers between devices, swapped(): return lax.ppermute(block, 'expert', [(i, i ^ k) for i in range(devices)])  9.31 us
    ppermute x4, starting transfers between devices, returned(): return lax.ppermute(block, ('section', 'expert'), route)  8.17 us
    ppermute x5, waiting for transfers between devices, swapped(): return lax.ppermute(block, 'expert', [(i, i ^ k) for i in range(devices)])  6.82 us
    pallas_call x1, Pallas kernels, on_device(): call(functools.partial(load, pieces), [bf16((tokens, width + LANES))] * 2...  4.31 us
    ppermute x2, starting transfers between devices, moved(): return lax.ppermute(block, 'section', route)  2.69 us
    pallas_call x1, Pallas kernels, on_device(): call(functools.partial(expert_backward, devices), outs, [VMEM] * (devices...  2.2 us
    pallas_call x1, Pallas kernels, on_device(): call(dispatch, [bf16((3 * CAP, width))] * 2 + [bf16((tokens, LANES))] * 2...  1.92 us
    pallas_call x1, Pallas kernels, on_device(): call(functools.partial(expert_forward, devices), outs + [factor] * 2, [VM...  1.69 us
  transfers between devices with their start and end apart: 11, of which 5 were waited for; matrix products, arithmetic and copies ran while one was open for 0% of the time, Pallas kernels for 23%

profile of v3, /device:TPU:0, one launch (start us, length us, event | category | flops | bytes accessed | tf_op | source)
XLA Modules:
  0.0 40.9 jit_solution(17818473424224420603)
XLA Ops:
  0.6 1.9 %shard_map.122 = (bf16[48,2048]{1,0:T(8,128)(2,1)S(1)}, bf16[48,2048]{1,0:T(8,128)(2,1)S(1)}, bf16[128,128]{1,0:T(8,128)(2,1)S(1)}, bf16[128,128]{1,0:T(8,128)(2,1)S(1)}) custom-call(s32[1]{0:T(128)} %bitcast.owner_ref, s32[1,8,128]{2,1,0:T(8,128)} %bitcast.5, f32[1,8,128]{2,1,0:T(8,128)} %bitcast.6, s32[1,8,128]{2,1,0:T(8,128)} %bitcast.7, ...), custom_call_target="tpu_custom_call" | custom-call | flops 50331648 | bytes 1572864 | tf_op jit(solution)/shard_map/pallas_call | solution.py:273
  2.6 4.1 %collective-permute-start.1 = (bf16[48,2048]{1,0:T(8,128)(2,1)S(1)}, bf16[48,2048]{1,0:T(8,128)(2,1)S(1)}, u32[]{:S(2)}, u32[]{:S(2)}) collective-permute-start(bf16[48,2048]{1,0:T(8,128)(2,1)S(1)} %get-tuple-element.36), channel_id=1, source_target_pairs={{0,2},{1,3},{2,0},{3,1},{4,6},{5,7},{6,4},{7,5},{8,10},{9,11},{10,... | collective-permute-start | bytes 589832 | tf_op jit(solution)/shard_map/ppermute | solution.py:244
  6.7 1.6 %collective-permute-start.2 = (bf16[48,2048]{1,0:T(8,128)(2,1)S(1)}, bf16[48,2048]{1,0:T(8,128)(2,1)S(1)}, u32[]{:S(2)}, u32[]{:S(2)}) collective-permute-start(bf16[48,2048]{1,0:T(8,128)(2,1)S(1)} %get-tuple-element.44.refs_0_), channel_id=1, source_target_pairs={{0,1},{1,0},{2,3},{3,2},{4,5},{5,4},{6,7},{7,6},{8,9},{9,8},{10,11... | collective-permute-start | bytes 589832 | tf_op jit(solution)/shard_map/ppermute | solution.py:244
  8.2 0.0 copy-start
  8.2 4.3 %shard_map.123 = (bf16[128,2176]{1,0:T(8,128)(2,1)S(1)}, bf16[128,2176]{1,0:T(8,128)(2,1)S(1)}, bf16[1,768,2048]{2,1,0:T(8,128)(2,1)S(1)}, bf16[1,768,2048]{2,1,...) custom-call(bf16[1,128,2048]{2,1,0:T(8,128)(2,1)} %rows_f.1, ...), custom_call_target="tpu_custom_call" | custom-call | bytes 37748736 | tf_op jit(solution)/shard_map/pallas_call | solution.py:287
  12.6 0.1 collective-permute-start
  12.6 2.6 %collective-permute-start.7 = (bf16[128,2176]{1,0:T(8,128)(2,1)S(1)}, bf16[128,2176]{1,0:T(8,128)(2,1)S(1)}, u32[]{:S(2)}, u32[]{:S(2)}) collective-permute-start(bf16[128,2176]{1,0:T(8,128)(2,1)S(1)} %get-tuple-element.54), channel_id=1, source_target_pairs={{0,28},{4,0},{8,4},{12,8},{16,12},{20,16},{24,20},{28,24},{1,29},{... | collective-permute-start | bytes 1671176 | tf_op jit(solution)/shard_map/ppermute | solution.py:248
  15.3 0.6 %collective-permute-done.1.refs_2_ = bf16[48,2048]{1,0:T(8,128)(2,1)S(1)} collective-permute-done((bf16[48,2048]{1,0:T(8,128)(2,1)S(1)}, bf16[48,2048]{1,0:T(8,128)(2,1)S(1)}, u32[]{:S(2)}, u32[]{:S(2)}) %collective-permute-start.1) | collective-permute-done | bytes 196640 | tf_op jit(solution)/shard_map/ppermute | solution.py:244
  15.9 0.2 collective-permute-done.2.refs_1_
  16.1 1.5 %collective-permute-start.3 = (bf16[48,2048]{1,0:T(8,128)(2,1)S(1)}, bf16[48,2048]{1,0:T(8,128)(2,1)S(1)}, u32[]{:S(2)}, u32[]{:S(2)}) collective-permute-start(bf16[48,2048]{1,0:T(8,128)(2,1)S(1)} %collective-permute-done.1.refs_2_), channel_id=1, source_target_pairs={{0,1},{1,0},{2,3},{3,2},{4,5},{5,4},{6,7},{7,6},{8,9},{9,8},{10,11... | collective-permute-start | bytes 589832 | tf_op jit(solution)/shard_map/ppermute | solution.py:244
  17.6 4.3 %collective-permute-done.3.refs_3_ = bf16[48,2048]{1,0:T(8,128)(2,1)S(1)} collective-permute-done((bf16[48,2048]{1,0:T(8,128)(2,1)S(1)}, bf16[48,2048]{1,0:T(8,128)(2,1)S(1)}, u32[]{:S(2)}, u32[]{:S(2)}) %collective-permute-start.3) | collective-permute-done | bytes 196640 | tf_op jit(solution)/shard_map/ppermute | solution.py:244
  21.9 0.0 copy-done
  21.9 1.7 %shard_map.124 = (bf16[32,2048]{1,0:T(8,128)(2,1)S(1)}, bf16[32,2048]{1,0:T(8,128)(2,1)S(1)}, f32[64,768]{1,0:T(8,128)S(1)}, f32[64,768]{1,0:T(8,128)S(1)}) custom-call(bf16[48,2048]{1,0:T(8,128)(2,1)S(1)} %get-tuple-element.44.refs_0_, bf16[48,2048]{1,0:T(8,128)(2,1)S(1)} %collective-permute-done.2.refs_1_, ...), custom_call_target="tpu_custom_call" | custom-call | flops 1006632960 | bytes 9437184 | tf_op jit(solution)/shard_map/pallas_call | solution.py:313
  23.6 1.5 %collective-permute-start.4 = (bf16[32,2048]{1,0:T(8,128)(2,1)S(1)}, bf16[32,2048]{1,0:T(8,128)(2,1)S(1)}, u32[]{:S(2)}, u32[]{:S(2)}) collective-permute-start(bf16[32,2048]{1,0:T(8,128)(2,1)S(1)} %get-tuple-element.51), channel_id=1, source_target_pairs={{0,1},{1,0},{2,3},{3,2},{4,5},{5,4},{6,7},{7,6},{8,9},{9,8},{10,11... | collective-permute-start | bytes 393224 | tf_op jit(solution)/shard_map/ppermute | solution.py:244
  25.1 2.2 %shard_map.127 = (bf16[32,2048]{1,0:T(8,128)(2,1)S(1)}, bf16[32,2048]{1,0:T(8,128)(2,1)S(1)}) custom-call(bf16[48,2048]{1,0:T(8,128)(2,1)S(1)} %get-tuple-element.44.refs_0_, bf16[48,2048]{1,0:T(8,128)(2,1)S(1)} %collective-permute-done.2.refs_1_, bf16[48,2048]{1,0:T(8,128)(2,1)S(1)} %collective-permute-done.1.refs_2_, ...), custom_call_target="tpu_custom_call" | custom-call | flops 603979776 | bytes 9437184 | tf_op jit(solution)/shard_map/pallas_call | solution.py:321
  27.3 0.7 %collective-permute-start.8 = (bf16[32,2048]{1,0:T(8,128)(2,1)S(1)}, bf16[32,2048]{1,0:T(8,128)(2,1)S(1)}, u32[]{:S(2)}, u32[]{:S(2)}) collective-permute-start(bf16[32,2048]{1,0:T(8,128)(2,1)S(1)} %get-tuple-element.61), channel_id=1, source_target_pairs={{0,1},{1,0},{2,3},{3,2},{4,5},{5,4},{6,7},{7,6},{8,9},{9,8},{10,11... | collective-permute-start | bytes 393224 | tf_op jit(solution)/shard_map/ppermute | solution.py:244
  28.0 1.7 %collective-permute-done.4.received_ref = bf16[32,2048]{1,0:T(8,128)(2,1)S(1)} collective-permute-done((bf16[32,2048]{1,0:T(8,128)(2,1)S(1)}, bf16[32,2048]{1,0:T(8,128)(2,1)S(1)}, u32[]{:S(2)}, u32[]{:S(2)}) %collective-permute-start.4) | collective-permute-done | bytes 131104 | tf_op jit(solution)/shard_map/ppermute | solution.py:244
  29.7 0.1 collective-permute-start.5
  29.7 3.3 %collective-permute-start.6 = (bf16[16,2048]{1,0:T(8,128)(2,1)S(1)}, bf16[16,2048]{1,0:T(8,128)(2,1)S(1)}, u32[]{:S(2)}, u32[]{:S(2)}) collective-permute-start(bf16[16,2048]{1,0:T(8,128)(2,1)S(1)} %get-tuple-element.53), channel_id=1, source_target_pairs={{0,6},{1,7},{2,4},{3,5},{4,10},{5,11},{6,8},{7,9},{8,14},{9,15},{1... | collective-permute-start | bytes 196616 | tf_op jit(solution)/shard_map/ppermute | solution.py:256
  33.0 0.0 collective-permute-done.8.received_ref
  33.0 1.0 %collective-permute-start.9 = (bf16[16,2048]{1,0:T(8,128)(2,1)S(1)}, bf16[16,2048]{1,0:T(8,128)(2,1)S(1)}, u32[]{:S(2)}, u32[]{:S(2)}) collective-permute-start(bf16[16,2048]{1,0:T(8,128)(2,1)S(1)} %get-tuple-element.62), channel_id=1, source_target_pairs={{0,28},{1,29},{2,30},{3,31},{4,0},{5,1},{6,2},{7,3},{8,4},{9,5},{1... | collective-permute-start | bytes 196616 | tf_op jit(solution)/shard_map/ppermute | solution.py:256
  34.0 0.0 collective-permute-done.early_ref
  34.0 3.9 %collective-permute-start.10 = (bf16[16,2048]{1,0:T(8,128)(2,1)S(1)}, bf16[16,2048]{1,0:T(8,128)(2,1)S(1)}, u32[]{:S(2)}, u32[]{:S(2)}) collective-permute-start(bf16[16,2048]{1,0:T(8,128)(2,1)S(1)} %get-tuple-element.63), channel_id=1, source_target_pairs={{0,30},{1,31},{2,28},{3,29},{4,2},{5,3},{6,0},{7,1},{8,6},{9,7},{1... | collective-permute-start | bytes 196616 | tf_op jit(solution)/shard_map/ppermute | solution.py:256
  37.9 0.0 collective-permute-done.5.own_ref
  37.9 0.0 collective-permute-done.6.other_ref
  37.9 1.2 %shard_map.126 = bf16[1,128,2048]{2,1,0:T(8,128)(2,1)} custom-call(bf16[128,2176]{1,0:T(8,128)(2,1)S(1)} %collective-permute-done.early_ref, bf16[16,2048]{1,0:T(8,128)(2,1)S(1)} %collective-permute-done.5.own_ref, bf16[16,2048]{1,0:T(8,128)(2,1)S(1)} %collective-permute-done.6.other_ref), custom_call_target="tpu_custom_call" | custom-call | flops 16777216 | bytes 1572864 | tf_op jit(solution)/shard_map/pallas_call | solution.py:349
  39.1 0.0 collective-permute-done.7.early_ref
  39.1 0.0 collective-permute-done.9.own_ref
  39.1 0.6 %collective-permute-done.10.other_ref = bf16[16,2048]{1,0:T(8,128)(2,1)S(1)} collective-permute-done((bf16[16,2048]{1,0:T(8,128)(2,1)S(1)}, bf16[16,2048]{1,0:T(8,128)(2,1)S(1)}, u32[]{:S(2)}, u32[]{:S(2)}) %collective-permute-start.10) | collective-permute-done | bytes 65568 | tf_op jit(solution)/shard_map/ppermute | solution.py:256
  39.8 1.1 %shard_map.129 = bf16[1,128,2048]{2,1,0:T(8,128)(2,1)} custom-call(bf16[128,2176]{1,0:T(8,128)(2,1)S(1)} %collective-permute-done.7.early_ref, bf16[16,2048]{1,0:T(8,128)(2,1)S(1)} %collective-permute-done.9.own_ref, bf16[16,2048]{1,0:T(8,128)(2,1)S(1)} %collective-permute-done.10.other_ref), custom_call_target="tpu_custom_call" | custom-call | flops 16777216 | bytes 1572864 | tf_op jit(solution)/shard_map/pallas_call | solution.py:352
  (2 shorter events, 0.1 us)
Async XLA Ops:
  2.6 13.3 %collective-permute-start.1 = (bf16[48,2048]{1,0:T(8,128)(2,1)S(1)}, bf16[48,2048]{1,0:T(8,128)(2,1)S(1)}, u32[]{:S(2)}, u32[]{:S(2)}) collective-permute-start(bf16[48,2048]{1,0:T(8,128)(2,1)S(1)} %get-tuple-element.36), channel_id=1, source_target_pairs={{0,2},{1,3},{2,0},{3,1},{4,6},{5,7},{6,4},{7,5},{8,10},{9,11},{10,... | collective-permute-start | bytes 589832 | tf_op jit(solution)/shard_map/ppermute | solution.py:244
  6.7 9.4 %collective-permute-start.2 = (bf16[48,2048]{1,0:T(8,128)(2,1)S(1)}, bf16[48,2048]{1,0:T(8,128)(2,1)S(1)}, u32[]{:S(2)}, u32[]{:S(2)}) collective-permute-start(bf16[48,2048]{1,0:T(8,128)(2,1)S(1)} %get-tuple-element.44.refs_0_), channel_id=1, source_target_pairs={{0,1},{1,0},{2,3},{3,2},{4,5},{5,4},{6,7},{7,6},{8,9},{9,8},{10,11... | collective-permute-start | bytes 589832 | tf_op jit(solution)/shard_map/ppermute | solution.py:244
  8.2 13.7 %copy-start = (f32[1,2048]{1,0:T(1,128)S(1)}, f32[1,2048]{1,0:T(1,128)}, u32[]{:S(2)}) copy-start(f32[1,2048]{1,0:T(1,128)} %refs_4_.5) | copy-start | bytes 24580
  12.6 21.5 %collective-permute-start = (bf16[128,2176]{1,0:T(8,128)(2,1)S(1)}, bf16[128,2176]{1,0:T(8,128)(2,1)S(1)}, u32[]{:S(2)}, u32[]{:S(2)}) collective-permute-start(bf16[128,2176]{1,0:T(8,128)(2,1)S(1)} %get-tuple-element.35), channel_id=1, source_target_pairs={{0,4},{4,8},{8,12},{12,16},{16,20},{20,24},{24,28},{28,0},{1,5},{5... | collective-permute-start | bytes 1671176 | tf_op jit(solution)/shard_map/ppermute | solution.py:248
  12.6 26.5 %collective-permute-start.7 = (bf16[128,2176]{1,0:T(8,128)(2,1)S(1)}, bf16[128,2176]{1,0:T(8,128)(2,1)S(1)}, u32[]{:S(2)}, u32[]{:S(2)}) collective-permute-start(bf16[128,2176]{1,0:T(8,128)(2,1)S(1)} %get-tuple-element.54), channel_id=1, source_target_pairs={{0,28},{4,0},{8,4},{12,8},{16,12},{20,16},{24,20},{28,24},{1,29},{... | collective-permute-start | bytes 1671176 | tf_op jit(solution)/shard_map/ppermute | solution.py:248
  16.1 5.8 %collective-permute-start.3 = (bf16[48,2048]{1,0:T(8,128)(2,1)S(1)}, bf16[48,2048]{1,0:T(8,128)(2,1)S(1)}, u32[]{:S(2)}, u32[]{:S(2)}) collective-permute-start(bf16[48,2048]{1,0:T(8,128)(2,1)S(1)} %collective-permute-done.1.refs_2_), channel_id=1, source_target_pairs={{0,1},{1,0},{2,3},{3,2},{4,5},{5,4},{6,7},{7,6},{8,9},{9,8},{10,11... | collective-permute-start | bytes 589832 | tf_op jit(solution)/shard_map/ppermute | solution.py:244
  23.6 6.0 %collective-permute-start.4 = (bf16[32,2048]{1,0:T(8,128)(2,1)S(1)}, bf16[32,2048]{1,0:T(8,128)(2,1)S(1)}, u32[]{:S(2)}, u32[]{:S(2)}) collective-permute-start(bf16[32,2048]{1,0:T(8,128)(2,1)S(1)} %get-tuple-element.51), channel_id=1, source_target_pairs={{0,1},{1,0},{2,3},{3,2},{4,5},{5,4},{6,7},{7,6},{8,9},{9,8},{10,11... | collective-permute-start | bytes 393224 | tf_op jit(solution)/shard_map/ppermute | solution.py:244
  27.3 5.7 %collective-permute-start.8 = (bf16[32,2048]{1,0:T(8,128)(2,1)S(1)}, bf16[32,2048]{1,0:T(8,128)(2,1)S(1)}, u32[]{:S(2)}, u32[]{:S(2)}) collective-permute-start(bf16[32,2048]{1,0:T(8,128)(2,1)S(1)} %get-tuple-element.61), channel_id=1, source_target_pairs={{0,1},{1,0},{2,3},{3,2},{4,5},{5,4},{6,7},{7,6},{8,9},{9,8},{10,11... | collective-permute-start | bytes 393224 | tf_op jit(solution)/shard_map/ppermute | solution.py:244
  29.7 8.2 %collective-permute-start.5 = (bf16[16,2048]{1,0:T(8,128)(2,1)S(1)}, bf16[16,2048]{1,0:T(8,128)(2,1)S(1)}, u32[]{:S(2)}, u32[]{:S(2)}) collective-permute-start(bf16[16,2048]{1,0:T(8,128)(2,1)S(1)} %get-tuple-element.52), channel_id=1, source_target_pairs={{0,4},{1,5},{2,6},{3,7},{4,8},{5,9},{6,10},{7,11},{8,12},{9,13},{1... | collective-permute-start | bytes 196616 | tf_op jit(solution)/shard_map/ppermute | solution.py:256
  29.7 8.2 %collective-permute-start.6 = (bf16[16,2048]{1,0:T(8,128)(2,1)S(1)}, bf16[16,2048]{1,0:T(8,128)(2,1)S(1)}, u32[]{:S(2)}, u32[]{:S(2)}) collective-permute-start(bf16[16,2048]{1,0:T(8,128)(2,1)S(1)} %get-tuple-element.53), channel_id=1, source_target_pairs={{0,6},{1,7},{2,4},{3,5},{4,10},{5,11},{6,8},{7,9},{8,14},{9,15},{1... | collective-permute-start | bytes 196616 | tf_op jit(solution)/shard_map/ppermute | solution.py:256
  33.0 6.1 %collective-permute-start.9 = (bf16[16,2048]{1,0:T(8,128)(2,1)S(1)}, bf16[16,2048]{1,0:T(8,128)(2,1)S(1)}, u32[]{:S(2)}, u32[]{:S(2)}) collective-permute-start(bf16[16,2048]{1,0:T(8,128)(2,1)S(1)} %get-tuple-element.62), channel_id=1, source_target_pairs={{0,28},{1,29},{2,30},{3,31},{4,0},{5,1},{6,2},{7,3},{8,4},{9,5},{1... | collective-permute-start | bytes 196616 | tf_op jit(solution)/shard_map/ppermute | solution.py:256
  34.0 5.8 %collective-permute-start.10 = (bf16[16,2048]{1,0:T(8,128)(2,1)S(1)}, bf16[16,2048]{1,0:T(8,128)(2,1)S(1)}, u32[]{:S(2)}, u32[]{:S(2)}) collective-permute-start(bf16[16,2048]{1,0:T(8,128)(2,1)S(1)} %get-tuple-element.63), channel_id=1, source_target_pairs={{0,30},{1,31},{2,28},{3,29},{4,2},{5,3},{6,0},{7,1},{8,6},{9,7},{1... | collective-permute-start | bytes 196616 | tf_op jit(solution)/shard_map/ppermute | solution.py:256

commit v4 on v3

--- a/solution.py
+++ b/solution.py
@@ -10,6 +10,7 @@
 EF = 2
 CAP = 16
 EPSILON = 1e-06
+OUT_PIECES = 4
 LANES = 128
 MIB = 1 << 20
 
@@ -20,12 +21,12 @@
 ANY = pl.BlockSpec(memory_space=pl.ANY)
 
 
-def call(body, outs, specs, flops, nbytes, limit, scratch=()):
+def call(body, outs, specs, flops, nbytes, limit, scratch=(), out_spec=VMEM):
     return pl.pallas_call(
         body,
         out_shape=outs,
         in_specs=specs,
-        out_specs=[VMEM] * len(outs),
+        out_specs=[out_spec] * len(outs),
         scratch_shapes=scratch,
         compiler_params=pltpu.CompilerParams(vmem_limit_bytes=limit * MIB),
         cost_estimate=pl.CostEstimate(flops=flops, bytes_accessed=nbytes, transcendentals=0),
@@ -139,6 +140,14 @@
     return jnp.dot(left, right_ref[...], preferred_element_type=jnp.float32)
 
 
+def wide_product(left, right_ref):
+    rows, depth = left.shape
+    if rows >= LANES:
+        return product(left, right_ref)
+    below = jnp.zeros((LANES - rows, depth), left.dtype)
+    return product(jnp.concatenate([left, below], axis=0), right_ref)[:rows]
+
+
 def unit_rows(rows):
     values = rows.astype(jnp.float32)
     scale = lax.rsqrt(jnp.mean(values * values, axis=-1, keepdims=True) + EPSILON)
@@ -186,10 +195,10 @@
 def expert_backward(blocks, *refs):
     gain_ref, to_gate_ref, to_up_ref, gate_ref, up_ref, down_turned = refs[blocks : blocks + 6]
     grads = jnp.concatenate([ref[2 * CAP :] for ref in refs[:blocks]], axis=0)
-    hidden_grad = product(grads, down_turned)
+    hidden_grad = wide_product(grads, down_turned)
     gate_grad = (hidden_grad * to_gate_ref[...]).astype(jnp.bfloat16)
     upper_grad = (hidden_grad * to_up_ref[...]).astype(jnp.bfloat16)
-    total = product(gate_grad, gate_ref.at[0]) + product(upper_grad, up_ref.at[0])
+    total = wide_product(gate_grad, gate_ref.at[0]) + wide_product(upper_grad, up_ref.at[0])
     rows = jnp.concatenate([ref[CAP : 2 * CAP] for ref in refs[:blocks]], axis=0)
     unit, scale = unit_rows(rows)
     scaled = total * gain_ref[...]
@@ -197,27 +206,51 @@
     give(refs[blocks + 6 :], (scale * (scaled - unit * inner)).astype(jnp.bfloat16))
 
 
-def combine_forward(early_ref, own_ref, other_ref, out_ref):
-    width = out_ref.shape[2]
-    total = early_ref[:, :width].astype(jnp.float32)
-    table = early_ref[:, width:]
-    for e, part_ref in enumerate((own_ref, other_ref)):
-        pick = table[:, e * CAP : (e + 1) * CAP]
+def sent_out(out_hbm, held_ref, sem, columns):
+    width = held_ref.shape[1]
+    size = width // OUT_PIECES
+    copies = []
+    for piece in range(OUT_PIECES):
+        span = pl.ds(piece * size, size)
+        held_ref[:, span] = columns(span).astype(jnp.bfloat16)
+        copy = pltpu.make_async_copy(
+            held_ref.at[:, span], out_hbm.at[0, :, span], sem.at[piece]
+        )
+        copy.start()
+        copies.append(copy)
+    for copy in copies:
+        copy.wait()
+
+
+def combine_forward(early_ref, own_ref, other_ref, out_hbm, held_ref, sem):
+    table = early_ref[:, held_ref.shape[1] :]
+    picks = []
+    for e in range(EF):
         column = EF * CAP + 3 * e
         weight = jnp.sum(
             table[:, column : column + 3].astype(jnp.float32), axis=1, keepdims=True
         )
-        total = total + weight * jnp.dot(pick, part_ref[...], preferred_element_type=jnp.float32)
-    out_ref[0] = total.astype(jnp.bfloat16)
-
-
-def combine_backward(early_ref, own_ref, other_ref, out_ref):
-    width = out_ref.shape[2]
+        picks.append((table[:, e * CAP : (e + 1) * CAP], weight))
+
+    def columns(span):
+        total = early_ref[:, span].astype(jnp.float32)
+        for (pick, weight), part_ref in zip(picks, (own_ref, other_ref)):
+            total = total + weight * product(pick, part_ref.at[:, span])
+        return total
+
+    sent_out(out_hbm, held_ref, sem, columns)
+
+
+def combine_backward(early_ref, own_ref, other_ref, out_hbm, held_ref, sem):
+    width = held_ref.shape[1]
     pick = early_ref[:, width : width + EF * CAP]
-    parts = jnp.concatenate([own_ref[...], other_ref[...]], axis=0)
-    total = early_ref[:, :width].astype(jnp.float32)
-    total = total + jnp.dot(pick, parts, preferred_element_type=jnp.float32)
-    out_ref[0] = total.astype(jnp.bfloat16)
+
+    def columns(span):
+        parts = jnp.concatenate([own_ref[:, span], other_ref[:, span]], axis=0)
+        total = jnp.dot(pick, parts, preferred_element_type=jnp.float32)
+        return early_ref[:, span].astype(jnp.float32) + total
+
+    sent_out(out_hbm, held_ref, sem, columns)
 
 
 def on_device(
@@ -346,11 +379,12 @@
     parts_b = handed_back(*parts_b, -1)
     result = [bf16((1, tokens, width))]
     combine_flops = 2 * tokens * EF * CAP * width
+    scratch = [pltpu.VMEM((tokens, width), jnp.bfloat16), pltpu.SemaphoreType.DMA((OUT_PIECES,))]
     (next_input,) = call(
-        combine_forward, result, [VMEM] * 3, combine_flops, dispatch_bytes, 24
+        combine_forward, result, [VMEM] * 3, combine_flops, dispatch_bytes, 16, scratch, ANY
     )(early_f, *parts_f)
     (previous_gradient,) = call(
-        combine_backward, result, [VMEM] * 3, combine_flops, dispatch_bytes, 24
+        combine_backward, result, [VMEM] * 3, combine_flops, dispatch_bytes, 16, scratch, ANY
     )(early_b, *parts_b)
     return next_input, previous_gradient
 

time: 41 us -> 41 us (level)
  starting transfers between devices: 20.2 us -> 19.7 us
  waiting for transfers between devices: 7.47 us -> 7.91 us
    ppermute x4, starting transfers between devices: 8.17 us -> 7.73 us  [returned(): return lax.ppermute(block, ('section', 'expert'), route)]
where the time goes in v4:
time: 41 us; the launch traced here: 40.5 us
  starting transfers between devices  19.7 us (48%)
  Pallas kernels  12.1 us (30%)
  waiting for transfers between devices  7.91 us (19%)
  between operations  0.72 us (2%)
    ppermute x5, starting transfers between devices, swapped(): return lax.ppermute(block, 'expert', [(i, i ^ k) for i in range(devices)])  9.31 us
    ppermute x4, starting transfers between devices, returned(): return lax.ppermute(block, ('section', 'expert'), route)  7.73 us
    ppermute x5, waiting for transfers between devices, swapped(): return lax.ppermute(block, 'expert', [(i, i ^ k) for i in range(devices)])  7.18 us
    pallas_call x1, Pallas kernels, on_device(): call(functools.partial(load, pieces), [bf16((tokens, width + LANES))] * 2...  4.31 us
    ppermute x2, starting transfers between devices, moved(): return lax.ppermute(block, 'section', route)  2.69 us
    pallas_call x1, Pallas kernels, on_device(): call(functools.partial(expert_backward, devices), outs, [VMEM] * (devices...  1.98 us
    pallas_call x1, Pallas kernels, on_device(): call(dispatch, [bf16((3 * CAP, width))] * 2 + [bf16((tokens, LANES))] * 2...  1.92 us
    pallas_call x1, Pallas kernels, on_device(): call(functools.partial(expert_forward, devices), outs + [factor] * 2, [VM...  1.69 us
  transfers between devices with their start and end apart: 11, of which 5 were waited for; matrix products, arithmetic and copies ran while one was open for 0% of the time, Pallas kernels for 23%

profile of v4, /device:TPU:0, one launch (start us, length us, event | category | flops | bytes accessed | tf_op | source)
XLA Modules:
  0.0 40.5 jit_solution(18288474343559093520)
XLA Ops:
  0.6 1.9 %shard_map.122 = (bf16[48,2048]{1,0:T(8,128)(2,1)S(1)}, bf16[48,2048]{1,0:T(8,128)(2,1)S(1)}, bf16[128,128]{1,0:T(8,128)(2,1)S(1)}, bf16[128,128]{1,0:T(8,128)(2,1)S(1)}) custom-call(s32[1]{0:T(128)} %bitcast.owner_ref, s32[1,8,128]{2,1,0:T(8,128)} %bitcast.5, f32[1,8,128]{2,1,0:T(8,128)} %bitcast.6, s32[1,8,128]{2,1,0:T(8,128)} %bitcast.7, ...), custom_call_target="tpu_custom_call" | custom-call | flops 50331648 | bytes 1572864 | tf_op jit(solution)/shard_map/pallas_call | solution.py:306
  2.6 4.1 %collective-permute-start.1 = (bf16[48,2048]{1,0:T(8,128)(2,1)S(1)}, bf16[48,2048]{1,0:T(8,128)(2,1)S(1)}, u32[]{:S(2)}, u32[]{:S(2)}) collective-permute-start(bf16[48,2048]{1,0:T(8,128)(2,1)S(1)} %get-tuple-element.36), channel_id=1, source_target_pairs={{0,2},{1,3},{2,0},{3,1},{4,6},{5,7},{6,4},{7,5},{8,10},{9,11},{10,... | collective-permute-start | bytes 589832 | tf_op jit(solution)/shard_map/ppermute | solution.py:277
  6.7 1.6 %collective-permute-start.2 = (bf16[48,2048]{1,0:T(8,128)(2,1)S(1)}, bf16[48,2048]{1,0:T(8,128)(2,1)S(1)}, u32[]{:S(2)}, u32[]{:S(2)}) collective-permute-start(bf16[48,2048]{1,0:T(8,128)(2,1)S(1)} %get-tuple-element.44.refs_0_), channel_id=1, source_target_pairs={{0,1},{1,0},{2,3},{3,2},{4,5},{5,4},{6,7},{7,6},{8,9},{9,8},{10,11... | collective-permute-start | bytes 589832 | tf_op jit(solution)/shard_map/ppermute | solution.py:277
  8.2 0.0 copy-start
  8.2 4.3 %shard_map.123 = (bf16[128,2176]{1,0:T(8,128)(2,1)S(1)}, bf16[128,2176]{1,0:T(8,128)(2,1)S(1)}, bf16[1,768,2048]{2,1,0:T(8,128)(2,1)S(1)}, bf16[1,768,2048]{2,1,...) custom-call(bf16[1,128,2048]{2,1,0:T(8,128)(2,1)} %rows_f.1, ...), custom_call_target="tpu_custom_call" | custom-call | bytes 37748736 | tf_op jit(solution)/shard_map/pallas_call | solution.py:320
  12.6 0.1 collective-permute-start
  12.6 2.6 %collective-permute-start.7 = (bf16[128,2176]{1,0:T(8,128)(2,1)S(1)}, bf16[128,2176]{1,0:T(8,128)(2,1)S(1)}, u32[]{:S(2)}, u32[]{:S(2)}) collective-permute-start(bf16[128,2176]{1,0:T(8,128)(2,1)S(1)} %get-tuple-element.54), channel_id=1, source_target_pairs={{0,28},{4,0},{8,4},{12,8},{16,12},{20,16},{24,20},{28,24},{1,29},{... | collective-permute-start | bytes 1671176 | tf_op jit(solution)/shard_map/ppermute | solution.py:281
  15.3 0.6 %collective-permute-done.1.refs_2_ = bf16[48,2048]{1,0:T(8,128)(2,1)S(1)} collective-permute-done((bf16[48,2048]{1,0:T(8,128)(2,1)S(1)}, bf16[48,2048]{1,0:T(8,128)(2,1)S(1)}, u32[]{:S(2)}, u32[]{:S(2)}) %collective-permute-start.1) | collective-permute-done | bytes 196640 | tf_op jit(solution)/shard_map/ppermute | solution.py:277
  15.9 0.2 collective-permute-done.2.refs_1_
  16.1 1.5 %collective-permute-start.3 = (bf16[48,2048]{1,0:T(8,128)(2,1)S(1)}, bf16[48,2048]{1,0:T(8,128)(2,1)S(1)}, u32[]{:S(2)}, u32[]{:S(2)}) collective-permute-start(bf16[48,2048]{1,0:T(8,128)(2,1)S(1)} %collective-permute-done.1.refs_2_), channel_id=1, source_target_pairs={{0,1},{1,0},{2,3},{3,2},{4,5},{5,4},{6,7},{7,6},{8,9},{9,8},{10,11... | collective-permute-start | bytes 589832 | tf_op jit(solution)/shard_map/ppermute | solution.py:277
  17.6 4.3 %collective-permute-done.3.refs_3_ = bf16[48,2048]{1,0:T(8,128)(2,1)S(1)} collective-permute-done((bf16[48,2048]{1,0:T(8,128)(2,1)S(1)}, bf16[48,2048]{1,0:T(8,128)(2,1)S(1)}, u32[]{:S(2)}, u32[]{:S(2)}) %collective-permute-start.3) | collective-permute-done | bytes 196640 | tf_op jit(solution)/shard_map/ppermute | solution.py:277
  21.9 0.0 copy-done
  21.9 1.7 %shard_map.124 = (bf16[32,2048]{1,0:T(8,128)(2,1)S(1)}, bf16[32,2048]{1,0:T(8,128)(2,1)S(1)}, f32[64,768]{1,0:T(8,128)S(1)}, f32[64,768]{1,0:T(8,128)S(1)}) custom-call(bf16[48,2048]{1,0:T(8,128)(2,1)S(1)} %get-tuple-element.44.refs_0_, bf16[48,2048]{1,0:T(8,128)(2,1)S(1)} %collective-permute-done.2.refs_1_, ...), custom_call_target="tpu_custom_call" | custom-call | flops 1006632960 | bytes 9437184 | tf_op jit(solution)/shard_map/pallas_call | solution.py:346
  23.6 1.5 %collective-permute-start.4 = (bf16[32,2048]{1,0:T(8,128)(2,1)S(1)}, bf16[32,2048]{1,0:T(8,128)(2,1)S(1)}, u32[]{:S(2)}, u32[]{:S(2)}) collective-permute-start(bf16[32,2048]{1,0:T(8,128)(2,1)S(1)} %get-tuple-element.51), channel_id=1, source_target_pairs={{0,1},{1,0},{2,3},{3,2},{4,5},{5,4},{6,7},{7,6},{8,9},{9,8},{10,11... | collective-permute-start | bytes 393224 | tf_op jit(solution)/shard_map/ppermute | solution.py:277
  25.1 2.0 %shard_map.127 = (bf16[32,2048]{1,0:T(8,128)(2,1)S(1)}, bf16[32,2048]{1,0:T(8,128)(2,1)S(1)}) custom-call(bf16[48,2048]{1,0:T(8,128)(2,1)S(1)} %get-tuple-element.44.refs_0_, bf16[48,2048]{1,0:T(8,128)(2,1)S(1)} %collective-permute-done.2.refs_1_, bf16[48,2048]{1,0:T(8,128)(2,1)S(1)} %collective-permute-done.1.refs_2_, ...), custom_call_target="tpu_custom_call" | custom-call | flops 603979776 | bytes 9437184 | tf_op jit(solution)/shard_map/pallas_call | solution.py:354
  27.1 0.7 %collective-permute-start.8 = (bf16[32,2048]{1,0:T(8,128)(2,1)S(1)}, bf16[32,2048]{1,0:T(8,128)(2,1)S(1)}, u32[]{:S(2)}, u32[]{:S(2)}) collective-permute-start(bf16[32,2048]{1,0:T(8,128)(2,1)S(1)} %get-tuple-element.61), channel_id=1, source_target_pairs={{0,1},{1,0},{2,3},{3,2},{4,5},{5,4},{6,7},{7,6},{8,9},{9,8},{10,11... | collective-permute-start | bytes 393224 | tf_op jit(solution)/shard_map/ppermute | solution.py:277
  27.7 2.0 %collective-permute-done.4.received_ref = bf16[32,2048]{1,0:T(8,128)(2,1)S(1)} collective-permute-done((bf16[32,2048]{1,0:T(8,128)(2,1)S(1)}, bf16[32,2048]{1,0:T(8,128)(2,1)S(1)}, u32[]{:S(2)}, u32[]{:S(2)}) %collective-permute-start.4) | collective-permute-done | bytes 131104 | tf_op jit(solution)/shard_map/ppermute | solution.py:277
  29.8 0.1 collective-permute-start.5
  29.9 3.3 %collective-permute-start.6 = (bf16[16,2048]{1,0:T(8,128)(2,1)S(1)}, bf16[16,2048]{1,0:T(8,128)(2,1)S(1)}, u32[]{:S(2)}, u32[]{:S(2)}) collective-permute-start(bf16[16,2048]{1,0:T(8,128)(2,1)S(1)} %get-tuple-element.53), channel_id=1, source_target_pairs={{0,6},{1,7},{2,4},{3,5},{4,10},{5,11},{6,8},{7,9},{8,14},{9,15},{1... | collective-permute-start | bytes 196616 | tf_op jit(solution)/shard_map/ppermute | solution.py:289
  33.1 0.0 collective-permute-done.8.received_ref
  33.2 1.0 %collective-permute-start.9 = (bf16[16,2048]{1,0:T(8,128)(2,1)S(1)}, bf16[16,2048]{1,0:T(8,128)(2,1)S(1)}, u32[]{:S(2)}, u32[]{:S(2)}) collective-permute-start(bf16[16,2048]{1,0:T(8,128)(2,1)S(1)} %get-tuple-element.62), channel_id=1, source_target_pairs={{0,28},{1,29},{2,30},{3,31},{4,0},{5,1},{6,2},{7,3},{8,4},{9,5},{1... | collective-permute-start | bytes 196616 | tf_op jit(solution)/shard_map/ppermute | solution.py:289
  34.2 0.0 collective-permute-done.early_ref
  34.2 3.4 %collective-permute-start.10 = (bf16[16,2048]{1,0:T(8,128)(2,1)S(1)}, bf16[16,2048]{1,0:T(8,128)(2,1)S(1)}, u32[]{:S(2)}, u32[]{:S(2)}) collective-permute-start(bf16[16,2048]{1,0:T(8,128)(2,1)S(1)} %get-tuple-element.63), channel_id=1, source_target_pairs={{0,30},{1,31},{2,28},{3,29},{4,2},{5,3},{6,0},{7,1},{8,6},{9,7},{1... | collective-permute-start | bytes 196616 | tf_op jit(solution)/shard_map/ppermute | solution.py:289
  37.6 0.0 collective-permute-done.5.own_ref
  37.6 0.0 collective-permute-done.6.other_ref
  37.6 1.2 %shard_map.126 = bf16[1,128,2048]{2,1,0:T(8,128)(2,1)} custom-call(bf16[128,2176]{1,0:T(8,128)(2,1)S(1)} %collective-permute-done.early_ref, bf16[16,2048]{1,0:T(8,128)(2,1)S(1)} %collective-permute-done.5.own_ref, bf16[16,2048]{1,0:T(8,128)(2,1)S(1)} %collective-permute-done.6.other_ref), custom_call_target="tpu_custom_call" | custom-call | flops 16777216 | bytes 1572864 | tf_op jit(solution)/shard_map/pallas_call | solution.py:383
  38.8 0.0 collective-permute-done.7.early_ref
  38.8 0.0 collective-permute-done.9.own_ref
  38.8 0.7 %collective-permute-done.10.other_ref = bf16[16,2048]{1,0:T(8,128)(2,1)S(1)} collective-permute-done((bf16[16,2048]{1,0:T(8,128)(2,1)S(1)}, bf16[16,2048]{1,0:T(8,128)(2,1)S(1)}, u32[]{:S(2)}, u32[]{:S(2)}) %collective-permute-start.10) | collective-permute-done | bytes 65568 | tf_op jit(solution)/shard_map/ppermute | solution.py:289
  39.5 1.0 %shard_map.129 = bf16[1,128,2048]{2,1,0:T(8,128)(2,1)} custom-call(bf16[128,2176]{1,0:T(8,128)(2,1)S(1)} %collective-permute-done.7.early_ref, bf16[16,2048]{1,0:T(8,128)(2,1)S(1)} %collective-permute-done.9.own_ref, bf16[16,2048]{1,0:T(8,128)(2,1)S(1)} %collective-permute-done.10.other_ref), custom_call_target="tpu_custom_call" | custom-call | flops 16777216 | bytes 1572864 | tf_op jit(solution)/shard_map/pallas_call | solution.py:386
  (2 shorter events, 0.1 us)
Async XLA Ops:
  2.6 13.3 %collective-permute-start.1 = (bf16[48,2048]{1,0:T(8,128)(2,1)S(1)}, bf16[48,2048]{1,0:T(8,128)(2,1)S(1)}, u32[]{:S(2)}, u32[]{:S(2)}) collective-permute-start(bf16[48,2048]{1,0:T(8,128)(2,1)S(1)} %get-tuple-element.36), channel_id=1, source_target_pairs={{0,2},{1,3},{2,0},{3,1},{4,6},{5,7},{6,4},{7,5},{8,10},{9,11},{10,... | collective-permute-start | bytes 589832 | tf_op jit(solution)/shard_map/ppermute | solution.py:277
  6.7 9.4 %collective-permute-start.2 = (bf16[48,2048]{1,0:T(8,128)(2,1)S(1)}, bf16[48,2048]{1,0:T(8,128)(2,1)S(1)}, u32[]{:S(2)}, u32[]{:S(2)}) collective-permute-start(bf16[48,2048]{1,0:T(8,128)(2,1)S(1)} %get-tuple-element.44.refs_0_), channel_id=1, source_target_pairs={{0,1},{1,0},{2,3},{3,2},{4,5},{5,4},{6,7},{7,6},{8,9},{9,8},{10,11... | collective-permute-start | bytes 589832 | tf_op jit(solution)/shard_map/ppermute | solution.py:277
  8.2 13.7 %copy-start = (f32[1,2048]{1,0:T(1,128)S(1)}, f32[1,2048]{1,0:T(1,128)}, u32[]{:S(2)}) copy-start(f32[1,2048]{1,0:T(1,128)} %refs_4_.5) | copy-start | bytes 24580
  12.6 21.6 %collective-permute-start = (bf16[128,2176]{1,0:T(8,128)(2,1)S(1)}, bf16[128,2176]{1,0:T(8,128)(2,1)S(1)}, u32[]{:S(2)}, u32[]{:S(2)}) collective-permute-start(bf16[128,2176]{1,0:T(8,128)(2,1)S(1)} %get-tuple-element.35), channel_id=1, source_target_pairs={{0,4},{4,8},{8,12},{12,16},{16,20},{20,24},{24,28},{28,0},{1,5},{5... | collective-permute-start | bytes 1671176 | tf_op jit(solution)/shard_map/ppermute | solution.py:281
  12.6 26.1 %collective-permute-start.7 = (bf16[128,2176]{1,0:T(8,128)(2,1)S(1)}, bf16[128,2176]{1,0:T(8,128)(2,1)S(1)}, u32[]{:S(2)}, u32[]{:S(2)}) collective-permute-start(bf16[128,2176]{1,0:T(8,128)(2,1)S(1)} %get-tuple-element.54), channel_id=1, source_target_pairs={{0,28},{4,0},{8,4},{12,8},{16,12},{20,16},{24,20},{28,24},{1,29},{... | collective-permute-start | bytes 1671176 | tf_op jit(solution)/shard_map/ppermute | solution.py:281
  16.1 5.8 %collective-permute-start.3 = (bf16[48,2048]{1,0:T(8,128)(2,1)S(1)}, bf16[48,2048]{1,0:T(8,128)(2,1)S(1)}, u32[]{:S(2)}, u32[]{:S(2)}) collective-permute-start(bf16[48,2048]{1,0:T(8,128)(2,1)S(1)} %collective-permute-done.1.refs_2_), channel_id=1, source_target_pairs={{0,1},{1,0},{2,3},{3,2},{4,5},{5,4},{6,7},{7,6},{8,9},{9,8},{10,11... | collective-permute-start | bytes 589832 | tf_op jit(solution)/shard_map/ppermute | solution.py:277
  23.6 6.2 %collective-permute-start.4 = (bf16[32,2048]{1,0:T(8,128)(2,1)S(1)}, bf16[32,2048]{1,0:T(8,128)(2,1)S(1)}, u32[]{:S(2)}, u32[]{:S(2)}) collective-permute-start(bf16[32,2048]{1,0:T(8,128)(2,1)S(1)} %get-tuple-element.51), channel_id=1, source_target_pairs={{0,1},{1,0},{2,3},{3,2},{4,5},{5,4},{6,7},{7,6},{8,9},{9,8},{10,11... | collective-permute-start | bytes 393224 | tf_op jit(solution)/shard_map/ppermute | solution.py:277
  27.1 6.1 %collective-permute-start.8 = (bf16[32,2048]{1,0:T(8,128)(2,1)S(1)}, bf16[32,2048]{1,0:T(8,128)(2,1)S(1)}, u32[]{:S(2)}, u32[]{:S(2)}) collective-permute-start(bf16[32,2048]{1,0:T(8,128)(2,1)S(1)} %get-tuple-element.61), channel_id=1, source_target_pairs={{0,1},{1,0},{2,3},{3,2},{4,5},{5,4},{6,7},{7,6},{8,9},{9,8},{10,11... | collective-permute-start | bytes 393224 | tf_op jit(solution)/shard_map/ppermute | solution.py:277
  29.8 7.8 %collective-permute-start.5 = (bf16[16,2048]{1,0:T(8,128)(2,1)S(1)}, bf16[16,2048]{1,0:T(8,128)(2,1)S(1)}, u32[]{:S(2)}, u32[]{:S(2)}) collective-permute-start(bf16[16,2048]{1,0:T(8,128)(2,1)S(1)} %get-tuple-element.52), channel_id=1, source_target_pairs={{0,4},{1,5},{2,6},{3,7},{4,8},{5,9},{6,10},{7,11},{8,12},{9,13},{1... | collective-permute-start | bytes 196616 | tf_op jit(solution)/shard_map/ppermute | solution.py:289
  29.9 7.7 %collective-permute-start.6 = (bf16[16,2048]{1,0:T(8,128)(2,1)S(1)}, bf16[16,2048]{1,0:T(8,128)(2,1)S(1)}, u32[]{:S(2)}, u32[]{:S(2)}) collective-permute-start(bf16[16,2048]{1,0:T(8,128)(2,1)S(1)} %get-tuple-element.53), channel_id=1, source_target_pairs={{0,6},{1,7},{2,4},{3,5},{4,10},{5,11},{6,8},{7,9},{8,14},{9,15},{1... | collective-permute-start | bytes 196616 | tf_op jit(solution)/shard_map/ppermute | solution.py:289
  33.2 5.6 %collective-permute-start.9 = (bf16[16,2048]{1,0:T(8,128)(2,1)S(1)}, bf16[16,2048]{1,0:T(8,128)(2,1)S(1)}, u32[]{:S(2)}, u32[]{:S(2)}) collective-permute-start(bf16[16,2048]{1,0:T(8,128)(2,1)S(1)} %get-tuple-element.62), channel_id=1, source_target_pairs={{0,28},{1,29},{2,30},{3,31},{4,0},{5,1},{6,2},{7,3},{8,4},{9,5},{1... | collective-permute-start | bytes 196616 | tf_op jit(solution)/shard_map/ppermute | solution.py:289
  34.2 5.3 %collective-permute-start.10 = (bf16[16,2048]{1,0:T(8,128)(2,1)S(1)}, bf16[16,2048]{1,0:T(8,128)(2,1)S(1)}, u32[]{:S(2)}, u32[]{:S(2)}) collective-permute-start(bf16[16,2048]{1,0:T(8,128)(2,1)S(1)} %get-tuple-element.63), channel_id=1, source_target_pairs={{0,30},{1,31},{2,28},{3,29},{4,2},{5,3},{6,0},{7,1},{8,6},{9,7},{1... | collective-permute-start | bytes 196616 | tf_op jit(solution)/shard_map/ppermute | solution.py:289

commit v5 on v4

--- a/solution.py
+++ b/solution.py
@@ -41,24 +41,27 @@
     return pltpu.with_memory_space_constraint(array, pltpu.HBM)
 
 
-def slot_tables(owner, routes, shares):
-    tokens = routes.shape[1]
-    slot = lax.broadcasted_iota(jnp.int32, (EF * CAP, tokens), 0)
-    first = slot < CAP
-    weights = []
-    members = []
-    for expert in (owner, 1 - owner):
-        hit = routes == expert
-        members.append(jnp.sum(jnp.where(hit, 1.0, 0.0), axis=0, keepdims=True))
-        weights.append(jnp.sum(jnp.where(hit, shares, 0.0), axis=0, keepdims=True))
-    member = jnp.where(first, members[0], members[1])
+def slot_tables(owner, groups):
+    tokens = groups[0][0].shape[1]
+    rows = EF * CAP * len(groups)
+    members, weights = [], []
+    for routes, shares in groups:
+        for expert in (owner, 1 - owner):
+            hit = routes == expert
+            member = jnp.sum(jnp.where(hit, 1.0, 0.0), axis=0, keepdims=True)
+            members.append(jnp.broadcast_to(member, (CAP, tokens)))
+            weights.append(jnp.sum(jnp.where(hit, shares, 0.0), axis=0, keepdims=True))
+    member = jnp.concatenate(members, axis=0)
     row = lax.broadcasted_iota(jnp.int32, (tokens, tokens), 0)
     col = lax.broadcasted_iota(jnp.int32, (tokens, tokens), 1)
     earlier = jnp.where(row < col, 1.0, 0.0).astype(jnp.bfloat16)
     rank = jnp.dot(member.astype(jnp.bfloat16), earlier, preferred_element_type=jnp.float32)
-    place = (slot % CAP).astype(jnp.float32)
-    placed = jnp.where((member > 0.5) & (rank == place), 1.0, 0.0)
-    return placed, weights
+    place = lax.broadcasted_iota(jnp.int32, (rows, tokens), 0) % CAP
+    placed = jnp.where((member > 0.5) & (rank == place.astype(jnp.float32)), 1.0, 0.0)
+    return [
+        (placed[i * EF * CAP : (i + 1) * EF * CAP], weights[i * EF : (i + 1) * EF])
+        for i in range(len(groups))
+    ]
 
 
 def turned(table):
@@ -77,40 +80,22 @@
     loads = started(list(zip(refs[:7], refs[11:18])), refs[18])
     own_ref, other_ref, forward_ref, backward_ref = refs[7:11]
     routes_f, shares_f, routes_b, shares_b, rows_f, rows_b, grads = refs[11:18]
-    owner = owner_ref[0]
     for load in loads[:4]:
         load.wait()
-    placed, weights = slot_tables(owner, routes_f[0], shares_f[0])
-    pieces = []
-    for weight in weights:
-        left = weight
-        for _ in range(3):
-            part = left.astype(jnp.bfloat16).astype(jnp.float32)
-            left = left - part
-            pieces.append(part)
-    pieces.append(jnp.zeros((2, placed.shape[1]), jnp.float32))
-    table = jnp.concatenate([placed, *pieces], axis=0)
-    forward_ref[...] = turned(table).astype(jnp.bfloat16)
-    pick = placed.astype(jnp.bfloat16)
-    loads[4].wait()
-    slots = jnp.dot(pick, rows_f[0], preferred_element_type=jnp.float32)
-    own_ref[:CAP] = slots[:CAP].astype(jnp.bfloat16)
-    other_ref[:CAP] = slots[CAP:].astype(jnp.bfloat16)
-
-    placed, weights = slot_tables(owner, routes_b[0], shares_b[0])
-    backward_ref[...] = turned(placed).astype(jnp.bfloat16)
-    slot = lax.broadcasted_iota(jnp.int32, placed.shape, 0)
-    share = placed * jnp.where(slot < CAP, weights[0], weights[1])
+    groups = [(routes_f[0], shares_f[0]), (routes_b[0], shares_b[0])]
+    (placed_f, weights_f), (placed_b, weights_b) = slot_tables(owner_ref[0], groups)
+    slot = lax.broadcasted_iota(jnp.int32, placed_b.shape, 0)
+    share = placed_b * jnp.where(slot < CAP, weights_b[0], weights_b[1])
     share = jnp.sum(share, axis=1, keepdims=True)
-    pick = placed.astype(jnp.bfloat16)
-    loads[5].wait()
-    slots = jnp.dot(pick, rows_b[0], preferred_element_type=jnp.float32)
-    own_ref[CAP : 2 * CAP] = slots[:CAP].astype(jnp.bfloat16)
-    other_ref[CAP : 2 * CAP] = slots[CAP:].astype(jnp.bfloat16)
-    loads[6].wait()
-    slots = share * jnp.dot(pick, grads[0], preferred_element_type=jnp.float32)
-    own_ref[2 * CAP :] = slots[:CAP].astype(jnp.bfloat16)
-    other_ref[2 * CAP :] = slots[CAP:].astype(jnp.bfloat16)
+    for i, (placed, rows) in enumerate(((placed_f, rows_f), (placed_b, rows_b), (placed_b, grads))):
+        loads[4 + i].wait()
+        slots = product(placed.astype(jnp.bfloat16), rows.at[0])
+        slots = (slots if i < 2 else share * slots).astype(jnp.bfloat16)
+        own_ref[i * CAP : (i + 1) * CAP] = slots[:CAP]
+        other_ref[i * CAP : (i + 1) * CAP] = slots[CAP:]
+    unused = jnp.zeros((8 - EF, placed_f.shape[1]), jnp.float32)
+    forward_ref[...] = jnp.concatenate([placed_f, *weights_f, unused], axis=0)
+    backward_ref[...] = placed_b
 
 
 def load(pieces, rows_f, rows_b, table_f, table_b, *refs):
@@ -126,8 +111,15 @@
     early = started(
         [(rows_f.at[0], early_f.at[:, :width]), (rows_b.at[0], early_b.at[:, :width])], early_sem
     )
-    early_f[:, width:] = table_f[...]
-    early_b[:, width:] = table_b[...]
+    rows = [table_f[: EF * CAP]]
+    for e in range(EF):
+        left = table_f[EF * CAP + e : EF * CAP + e + 1]
+        for _ in range(3):
+            rows.append(left.astype(jnp.bfloat16).astype(jnp.float32))
+            left = left - rows[-1]
+    rows.append(jnp.zeros((2, left.shape[1]), jnp.float32))
+    early_f[:, width:] = turned(jnp.concatenate(rows, axis=0)).astype(jnp.bfloat16)
+    early_b[:, width:] = turned(table_b[...]).astype(jnp.bfloat16)
     for piece, span in enumerate(spans):
         for i in range(count):
             loads[piece * count + i].wait()
@@ -305,7 +297,8 @@
     layers = (forward_input, backward_input, output_grad)
     own, other, table_f, table_b = call(
         dispatch,
-        [bf16((3 * CAP, width))] * 2 + [bf16((tokens, LANES))] * 2,
+        [bf16((3 * CAP, width))] * 2
+        + [jax.ShapeDtypeStruct((n, tokens), jnp.float32) for n in (EF * CAP + 8, EF * CAP)],
         [SMEM] + [ANY] * 7,
         6 * EF * CAP * tokens * width,
         dispatch_bytes,

time: 41 us -> 40.9 us (level)
  transfers between devices with their start and end apart: 11 -> 11, of which waited for: 5 -> 5; matrix products, arithmetic and copies ran while one was open for 0% -> 0% of each run, Pallas kernels for 23% -> 24%
where the time goes in v5:
time: 40.9 us; the launch traced here: 40.4 us
  starting transfers between devices  19.7 us (48%)
  Pallas kernels  12.3 us (30%)
  waiting for transfers between devices  7.63 us (19%)
  between operations  0.73 us (2%)
    ppermute x5, starting transfers between devices, swapped(): return lax.ppermute(block, 'expert', [(i, i ^ k) for i in range(devices)])  9.32 us
    ppermute x4, starting transfers between devices, returned(): return lax.ppermute(block, ('section', 'expert'), route)  7.72 us
    ppermute x5, waiting for transfers between devices, swapped(): return lax.ppermute(block, 'expert', [(i, i ^ k) for i in range(devices)])  6.9 us
    pallas_call x1, Pallas kernels, on_device(): call(functools.partial(load, pieces), [bf16((tokens, width + LANES))] * 2...  4.6 us
    ppermute x2, starting transfers between devices, moved(): return lax.ppermute(block, 'section', route)  2.69 us
    pallas_call x1, Pallas kernels, on_device(): call(functools.partial(expert_backward, devices), outs, [VMEM] * (devices...  1.99 us
    pallas_call x1, Pallas kernels, on_device(): call(dispatch, [bf16((3 * CAP, width))] * 2 + [jax.ShapeDtypeStruct((n, t...  1.81 us
    pallas_call x1, Pallas kernels, on_device(): call(functools.partial(expert_forward, devices), outs + [factor] * 2, [VM...  1.69 us
  transfers between devices with their start and end apart: 11, of which 5 were waited for; matrix products, arithmetic and copies ran while one was open for 0% of the time, Pallas kernels for 24%

profile of v5, /device:TPU:0, one launch (start us, length us, event | category | flops | bytes accessed | tf_op | source)
XLA Modules:
  0.0 40.4 jit_solution(1630603063902216443)
XLA Ops:
  0.6 1.8 %shard_map.122 = (bf16[48,2048]{1,0:T(8,128)(2,1)S(1)}, bf16[48,2048]{1,0:T(8,128)(2,1)S(1)}, f32[40,128]{1,0:T(8,128)S(1)}, f32[32,128]{1,0:T(8,128)S(1)}) custom-call(s32[1]{0:T(128)} %bitcast.owner_ref, s32[1,8,128]{2,1,0:T(8,128)} %bitcast.5, f32[1,8,128]{2,1,0:T(8,128)} %bitcast.6, s32[1,8,128]{2,1,0:T(8,128)} %bitcast.7, f32[1,8,128]{2,1,0:T(8,128)} %bitcast.8, ...), custom_call_target="tpu_custom_call" | custom-call | flops 50331648 | bytes 1572864 | tf_op jit(solution)/shard_map/pallas_call | solution.py:298
  2.5 4.1 %collective-permute-start.1 = (bf16[48,2048]{1,0:T(8,128)(2,1)S(1)}, bf16[48,2048]{1,0:T(8,128)(2,1)S(1)}, u32[]{:S(2)}, u32[]{:S(2)}) collective-permute-start(bf16[48,2048]{1,0:T(8,128)(2,1)S(1)} %get-tuple-element.36), channel_id=1, source_target_pairs={{0,2},{1,3},{2,0},{3,1},{4,6},{5,7},{6,4},{7,5},{8,10},{9,11},{10,... | collective-permute-start | bytes 589832 | tf_op jit(solution)/shard_map/ppermute | solution.py:269
  6.6 1.6 %collective-permute-start.2 = (bf16[48,2048]{1,0:T(8,128)(2,1)S(1)}, bf16[48,2048]{1,0:T(8,128)(2,1)S(1)}, u32[]{:S(2)}, u32[]{:S(2)}) collective-permute-start(bf16[48,2048]{1,0:T(8,128)(2,1)S(1)} %get-tuple-element.44.refs_0_), channel_id=1, source_target_pairs={{0,1},{1,0},{2,3},{3,2},{4,5},{5,4},{6,7},{7,6},{8,9},{9,8},{10,11... | collective-permute-start | bytes 589832 | tf_op jit(solution)/shard_map/ppermute | solution.py:269
  8.1 0.0 copy-start
  8.1 4.6 %shard_map.123 = (bf16[128,2176]{1,0:T(8,128)(2,1)S(1)}, bf16[128,2176]{1,0:T(8,128)(2,1)S(1)}, bf16[1,768,2048]{2,1,0:T(8,128)(2,1)S(1)}, bf16[1,768,2048]{2,1,...) custom-call(bf16[1,128,2048]{2,1,0:T(8,128)(2,1)} %rows_f.1, ...), custom_call_target="tpu_custom_call" | custom-call | bytes 37748736 | tf_op jit(solution)/shard_map/pallas_call | solution.py:313
  12.8 0.1 collective-permute-start
  12.8 2.6 %collective-permute-start.7 = (bf16[128,2176]{1,0:T(8,128)(2,1)S(1)}, bf16[128,2176]{1,0:T(8,128)(2,1)S(1)}, u32[]{:S(2)}, u32[]{:S(2)}) collective-permute-start(bf16[128,2176]{1,0:T(8,128)(2,1)S(1)} %get-tuple-element.54), channel_id=1, source_target_pairs={{0,28},{4,0},{8,4},{12,8},{16,12},{20,16},{24,20},{28,24},{1,29},{... | collective-permute-start | bytes 1671176 | tf_op jit(solution)/shard_map/ppermute | solution.py:273
  15.4 0.3 collective-permute-done.1.refs_2_
  15.8 0.2 collective-permute-done.2.refs_1_
  16.0 1.5 %collective-permute-start.3 = (bf16[48,2048]{1,0:T(8,128)(2,1)S(1)}, bf16[48,2048]{1,0:T(8,128)(2,1)S(1)}, u32[]{:S(2)}, u32[]{:S(2)}) collective-permute-start(bf16[48,2048]{1,0:T(8,128)(2,1)S(1)} %collective-permute-done.1.refs_2_), channel_id=1, source_target_pairs={{0,1},{1,0},{2,3},{3,2},{4,5},{5,4},{6,7},{7,6},{8,9},{9,8},{10,11... | collective-permute-start | bytes 589832 | tf_op jit(solution)/shard_map/ppermute | solution.py:269
  17.5 4.4 %collective-permute-done.3.refs_3_ = bf16[48,2048]{1,0:T(8,128)(2,1)S(1)} collective-permute-done((bf16[48,2048]{1,0:T(8,128)(2,1)S(1)}, bf16[48,2048]{1,0:T(8,128)(2,1)S(1)}, u32[]{:S(2)}, u32[]{:S(2)}) %collective-permute-start.3) | collective-permute-done | bytes 196640 | tf_op jit(solution)/shard_map/ppermute | solution.py:269
  21.8 0.0 copy-done
  21.8 1.7 %shard_map.124 = (bf16[32,2048]{1,0:T(8,128)(2,1)S(1)}, bf16[32,2048]{1,0:T(8,128)(2,1)S(1)}, f32[64,768]{1,0:T(8,128)S(1)}, f32[64,768]{1,0:T(8,128)S(1)}) custom-call(bf16[48,2048]{1,0:T(8,128)(2,1)S(1)} %get-tuple-element.44.refs_0_, bf16[48,2048]{1,0:T(8,128)(2,1)S(1)} %collective-permute-done.2.refs_1_, ...), custom_call_target="tpu_custom_call" | custom-call | flops 1006632960 | bytes 9437184 | tf_op jit(solution)/shard_map/pallas_call | solution.py:339
  23.5 1.5 %collective-permute-start.4 = (bf16[32,2048]{1,0:T(8,128)(2,1)S(1)}, bf16[32,2048]{1,0:T(8,128)(2,1)S(1)}, u32[]{:S(2)}, u32[]{:S(2)}) collective-permute-start(bf16[32,2048]{1,0:T(8,128)(2,1)S(1)} %get-tuple-element.51), channel_id=1, source_target_pairs={{0,1},{1,0},{2,3},{3,2},{4,5},{5,4},{6,7},{7,6},{8,9},{9,8},{10,11... | collective-permute-start | bytes 393224 | tf_op jit(solution)/shard_map/ppermute | solution.py:269
  25.0 2.0 %shard_map.127 = (bf16[32,2048]{1,0:T(8,128)(2,1)S(1)}, bf16[32,2048]{1,0:T(8,128)(2,1)S(1)}) custom-call(bf16[48,2048]{1,0:T(8,128)(2,1)S(1)} %get-tuple-element.44.refs_0_, bf16[48,2048]{1,0:T(8,128)(2,1)S(1)} %collective-permute-done.2.refs_1_, bf16[48,2048]{1,0:T(8,128)(2,1)S(1)} %collective-permute-done.1.refs_2_, ...), custom_call_target="tpu_custom_call" | custom-call | flops 603979776 | bytes 9437184 | tf_op jit(solution)/shard_map/pallas_call | solution.py:347
  27.0 0.7 %collective-permute-start.8 = (bf16[32,2048]{1,0:T(8,128)(2,1)S(1)}, bf16[32,2048]{1,0:T(8,128)(2,1)S(1)}, u32[]{:S(2)}, u32[]{:S(2)}) collective-permute-start(bf16[32,2048]{1,0:T(8,128)(2,1)S(1)} %get-tuple-element.61), channel_id=1, source_target_pairs={{0,1},{1,0},{2,3},{3,2},{4,5},{5,4},{6,7},{7,6},{8,9},{9,8},{10,11... | collective-permute-start | bytes 393224 | tf_op jit(solution)/shard_map/ppermute | solution.py:269
  27.7 2.0 %collective-permute-done.4.received_ref = bf16[32,2048]{1,0:T(8,128)(2,1)S(1)} collective-permute-done((bf16[32,2048]{1,0:T(8,128)(2,1)S(1)}, bf16[32,2048]{1,0:T(8,128)(2,1)S(1)}, u32[]{:S(2)}, u32[]{:S(2)}) %collective-permute-start.4) | collective-permute-done | bytes 131104 | tf_op jit(solution)/shard_map/ppermute | solution.py:269
  29.7 0.1 collective-permute-start.5
  29.8 3.3 %collective-permute-start.6 = (bf16[16,2048]{1,0:T(8,128)(2,1)S(1)}, bf16[16,2048]{1,0:T(8,128)(2,1)S(1)}, u32[]{:S(2)}, u32[]{:S(2)}) collective-permute-start(bf16[16,2048]{1,0:T(8,128)(2,1)S(1)} %get-tuple-element.53), channel_id=1, source_target_pairs={{0,6},{1,7},{2,4},{3,5},{4,10},{5,11},{6,8},{7,9},{8,14},{9,15},{1... | collective-permute-start | bytes 196616 | tf_op jit(solution)/shard_map/ppermute | solution.py:281
  33.0 0.0 collective-permute-done.8.received_ref
  33.1 1.0 %collective-permute-start.9 = (bf16[16,2048]{1,0:T(8,128)(2,1)S(1)}, bf16[16,2048]{1,0:T(8,128)(2,1)S(1)}, u32[]{:S(2)}, u32[]{:S(2)}) collective-permute-start(bf16[16,2048]{1,0:T(8,128)(2,1)S(1)} %get-tuple-element.62), channel_id=1, source_target_pairs={{0,28},{1,29},{2,30},{3,31},{4,0},{5,1},{6,2},{7,3},{8,4},{9,5},{1... | collective-permute-start | bytes 196616 | tf_op jit(solution)/shard_map/ppermute | solution.py:281
  34.1 0.0 collective-permute-done.early_ref
  34.1 3.4 %collective-permute-start.10 = (bf16[16,2048]{1,0:T(8,128)(2,1)S(1)}, bf16[16,2048]{1,0:T(8,128)(2,1)S(1)}, u32[]{:S(2)}, u32[]{:S(2)}) collective-permute-start(bf16[16,2048]{1,0:T(8,128)(2,1)S(1)} %get-tuple-element.63), channel_id=1, source_target_pairs={{0,30},{1,31},{2,28},{3,29},{4,2},{5,3},{6,0},{7,1},{8,6},{9,7},{1... | collective-permute-start | bytes 196616 | tf_op jit(solution)/shard_map/ppermute | solution.py:281
  37.5 0.0 collective-permute-done.5.own_ref
  37.5 0.0 collective-permute-done.6.other_ref
  37.5 1.2 %shard_map.126 = bf16[1,128,2048]{2,1,0:T(8,128)(2,1)} custom-call(bf16[128,2176]{1,0:T(8,128)(2,1)S(1)} %collective-permute-done.early_ref, bf16[16,2048]{1,0:T(8,128)(2,1)S(1)} %collective-permute-done.5.own_ref, bf16[16,2048]{1,0:T(8,128)(2,1)S(1)} %collective-permute-done.6.other_ref), custom_call_target="tpu_custom_call" | custom-call | flops 16777216 | bytes 1572864 | tf_op jit(solution)/shard_map/pallas_call | solution.py:376
  38.7 0.0 collective-permute-done.7.early_ref
  38.7 0.0 collective-permute-done.9.own_ref
  38.7 0.7 %collective-permute-done.10.other_ref = bf16[16,2048]{1,0:T(8,128)(2,1)S(1)} collective-permute-done((bf16[16,2048]{1,0:T(8,128)(2,1)S(1)}, bf16[16,2048]{1,0:T(8,128)(2,1)S(1)}, u32[]{:S(2)}, u32[]{:S(2)}) %collective-permute-start.10) | collective-permute-done | bytes 65568 | tf_op jit(solution)/shard_map/ppermute | solution.py:281
  39.4 1.0 %shard_map.129 = bf16[1,128,2048]{2,1,0:T(8,128)(2,1)} custom-call(bf16[128,2176]{1,0:T(8,128)(2,1)S(1)} %collective-permute-done.7.early_ref, bf16[16,2048]{1,0:T(8,128)(2,1)S(1)} %collective-permute-done.9.own_ref, bf16[16,2048]{1,0:T(8,128)(2,1)S(1)} %collective-permute-done.10.other_ref), custom_call_target="tpu_custom_call" | custom-call | flops 16777216 | bytes 1572864 | tf_op jit(solution)/shard_map/pallas_call | solution.py:379
  (2 shorter events, 0.1 us)
Async XLA Ops:
  2.5 13.3 %collective-permute-start.1 = (bf16[48,2048]{1,0:T(8,128)(2,1)S(1)}, bf16[48,2048]{1,0:T(8,128)(2,1)S(1)}, u32[]{:S(2)}, u32[]{:S(2)}) collective-permute-start(bf16[48,2048]{1,0:T(8,128)(2,1)S(1)} %get-tuple-element.36), channel_id=1, source_target_pairs={{0,2},{1,3},{2,0},{3,1},{4,6},{5,7},{6,4},{7,5},{8,10},{9,11},{10,... | collective-permute-start | bytes 589832 | tf_op jit(solution)/shard_map/ppermute | solution.py:269
  6.6 9.4 %collective-permute-start.2 = (bf16[48,2048]{1,0:T(8,128)(2,1)S(1)}, bf16[48,2048]{1,0:T(8,128)(2,1)S(1)}, u32[]{:S(2)}, u32[]{:S(2)}) collective-permute-start(bf16[48,2048]{1,0:T(8,128)(2,1)S(1)} %get-tuple-element.44.refs_0_), channel_id=1, source_target_pairs={{0,1},{1,0},{2,3},{3,2},{4,5},{5,4},{6,7},{7,6},{8,9},{9,8},{10,11... | collective-permute-start | bytes 589832 | tf_op jit(solution)/shard_map/ppermute | solution.py:269
  8.1 13.7 %copy-start = (f32[1,2048]{1,0:T(1,128)S(1)}, f32[1,2048]{1,0:T(1,128)}, u32[]{:S(2)}) copy-start(f32[1,2048]{1,0:T(1,128)} %refs_4_.5) | copy-start | bytes 24580
  12.8 21.3 %collective-permute-start = (bf16[128,2176]{1,0:T(8,128)(2,1)S(1)}, bf16[128,2176]{1,0:T(8,128)(2,1)S(1)}, u32[]{:S(2)}, u32[]{:S(2)}) collective-permute-start(bf16[128,2176]{1,0:T(8,128)(2,1)S(1)} %get-tuple-element.35), channel_id=1, source_target_pairs={{0,4},{4,8},{8,12},{12,16},{16,20},{20,24},{24,28},{28,0},{1,5},{5... | collective-permute-start | bytes 1671176 | tf_op jit(solution)/shard_map/ppermute | solution.py:273
  12.8 25.9 %collective-permute-start.7 = (bf16[128,2176]{1,0:T(8,128)(2,1)S(1)}, bf16[128,2176]{1,0:T(8,128)(2,1)S(1)}, u32[]{:S(2)}, u32[]{:S(2)}) collective-permute-start(bf16[128,2176]{1,0:T(8,128)(2,1)S(1)} %get-tuple-element.54), channel_id=1, source_target_pairs={{0,28},{4,0},{8,4},{12,8},{16,12},{20,16},{24,20},{28,24},{1,29},{... | collective-permute-start | bytes 1671176 | tf_op jit(solution)/shard_map/ppermute | solution.py:273
  16.0 5.8 %collective-permute-start.3 = (bf16[48,2048]{1,0:T(8,128)(2,1)S(1)}, bf16[48,2048]{1,0:T(8,128)(2,1)S(1)}, u32[]{:S(2)}, u32[]{:S(2)}) collective-permute-start(bf16[48,2048]{1,0:T(8,128)(2,1)S(1)} %collective-permute-done.1.refs_2_), channel_id=1, source_target_pairs={{0,1},{1,0},{2,3},{3,2},{4,5},{5,4},{6,7},{7,6},{8,9},{9,8},{10,11... | collective-permute-start | bytes 589832 | tf_op jit(solution)/shard_map/ppermute | solution.py:269
  23.5 6.2 %collective-permute-start.4 = (bf16[32,2048]{1,0:T(8,128)(2,1)S(1)}, bf16[32,2048]{1,0:T(8,128)(2,1)S(1)}, u32[]{:S(2)}, u32[]{:S(2)}) collective-permute-start(bf16[32,2048]{1,0:T(8,128)(2,1)S(1)} %get-tuple-element.51), channel_id=1, source_target_pairs={{0,1},{1,0},{2,3},{3,2},{4,5},{5,4},{6,7},{7,6},{8,9},{9,8},{10,11... | collective-permute-start | bytes 393224 | tf_op jit(solution)/shard_map/ppermute | solution.py:269
  27.0 6.0 %collective-permute-start.8 = (bf16[32,2048]{1,0:T(8,128)(2,1)S(1)}, bf16[32,2048]{1,0:T(8,128)(2,1)S(1)}, u32[]{:S(2)}, u32[]{:S(2)}) collective-permute-start(bf16[32,2048]{1,0:T(8,128)(2,1)S(1)} %get-tuple-element.61), channel_id=1, source_target_pairs={{0,1},{1,0},{2,3},{3,2},{4,5},{5,4},{6,7},{7,6},{8,9},{9,8},{10,11... | collective-permute-start | bytes 393224 | tf_op jit(solution)/shard_map/ppermute | solution.py:269
  29.7 7.8 %collective-permute-start.5 = (bf16[16,2048]{1,0:T(8,128)(2,1)S(1)}, bf16[16,2048]{1,0:T(8,128)(2,1)S(1)}, u32[]{:S(2)}, u32[]{:S(2)}) collective-permute-start(bf16[16,2048]{1,0:T(8,128)(2,1)S(1)} %get-tuple-element.52), channel_id=1, source_target_pairs={{0,4},{1,5},{2,6},{3,7},{4,8},{5,9},{6,10},{7,11},{8,12},{9,13},{1... | collective-permute-start | bytes 196616 | tf_op jit(solution)/shard_map/ppermute | solution.py:281
  29.8 7.7 %collective-permute-start.6 = (bf16[16,2048]{1,0:T(8,128)(2,1)S(1)}, bf16[16,2048]{1,0:T(8,128)(2,1)S(1)}, u32[]{:S(2)}, u32[]{:S(2)}) collective-permute-start(bf16[16,2048]{1,0:T(8,128)(2,1)S(1)} %get-tuple-element.53), channel_id=1, source_target_pairs={{0,6},{1,7},{2,4},{3,5},{4,10},{5,11},{6,8},{7,9},{8,14},{9,15},{1... | collective-permute-start | bytes 196616 | tf_op jit(solution)/shard_map/ppermute | solution.py:281
  33.1 5.6 %collective-permute-start.9 = (bf16[16,2048]{1,0:T(8,128)(2,1)S(1)}, bf16[16,2048]{1,0:T(8,128)(2,1)S(1)}, u32[]{:S(2)}, u32[]{:S(2)}) collective-permute-start(bf16[16,2048]{1,0:T(8,128)(2,1)S(1)} %get-tuple-element.62), channel_id=1, source_target_pairs={{0,28},{1,29},{2,30},{3,31},{4,0},{5,1},{6,2},{7,3},{8,4},{9,5},{1... | collective-permute-start | bytes 196616 | tf_op jit(solution)/shard_map/ppermute | solution.py:281
  34.1 5.3 %collective-permute-start.10 = (bf16[16,2048]{1,0:T(8,128)(2,1)S(1)}, bf16[16,2048]{1,0:T(8,128)(2,1)S(1)}, u32[]{:S(2)}, u32[]{:S(2)}) collective-permute-start(bf16[16,2048]{1,0:T(8,128)(2,1)S(1)} %get-tuple-element.63), channel_id=1, source_target_pairs={{0,30},{1,31},{2,28},{3,29},{4,2},{5,3},{6,0},{7,1},{8,6},{9,7},{1... | collective-permute-start | bytes 196616 | tf_op jit(solution)/shard_map/ppermute | solution.py:281

commit v6 on v5

--- a/solution.py
+++ b/solution.py
@@ -167,29 +167,41 @@
     outs[1][...] = total[split:]
 
 
-def expert_forward(blocks, *refs):
-    gain_ref, gate_turned, up_turned, down_ref = refs[blocks : blocks + 4]
-    kept_ref, given_ref, to_gate_ref, to_up_ref = refs[blocks + 4 :]
-    rows = [ref[:CAP] for ref in refs[:blocks]] + [ref[CAP : 2 * CAP] for ref in refs[:blocks]]
-    unit, _ = unit_rows(jnp.concatenate(rows, axis=0))
-    normed = (unit * gain_ref[...]).astype(jnp.bfloat16)
+def normed_rows(rows, gain):
+    return (unit_rows(rows)[0] * gain).astype(jnp.bfloat16)
+
+
+def normalized(*refs):
+    gain_ref, out_ref = refs[-2:]
+    for k, ref in enumerate(refs[:-2]):
+        span = pl.ds(2 * CAP * k, 2 * CAP)
+        out_ref[span] = normed_rows(ref[: 2 * CAP], gain_ref[...])
+
+
+def expert_forward(blocks, last_ref, held_ref, *refs):
+    gain_ref, gate_turned, up_turned, down_ref = refs[:4]
+    kept_ref, given_ref, gate_ref, upper_ref = refs[4:]
+    ready = [held_ref[CAP * k : CAP * (k + 1)] for k in range(2 * blocks - 2)]
+    last = normed_rows(last_ref[: 2 * CAP], gain_ref[...])
+    normed = jnp.concatenate(ready[::2] + [last[:CAP]] + ready[1::2] + [last[CAP:]], axis=0)
     gate = product(normed, gate_turned)
     upper = product(normed, up_turned)
     split = blocks * CAP
-    sigma = jax.nn.sigmoid(gate)
-    passed = gate * sigma
-    hidden = (passed[:split] * upper[:split]).astype(jnp.bfloat16)
-    to_up_ref[...] = passed[split:]
-    to_gate_ref[...] = (upper * sigma * (1.0 + gate * (1.0 - sigma)))[split:]
-    give((kept_ref, given_ref), product(hidden, down_ref.at[0]).astype(jnp.bfloat16))
+    gate_ref[...] = gate[split:]
+    upper_ref[...] = upper[split:]
+    gate, upper = gate[:split], upper[:split]
+    hidden = (gate * jax.nn.sigmoid(gate) * upper).astype(jnp.bfloat16)
+    give((kept_ref, given_ref), wide_product(hidden, down_ref.at[0]).astype(jnp.bfloat16))
 
 
 def expert_backward(blocks, *refs):
-    gain_ref, to_gate_ref, to_up_ref, gate_ref, up_ref, down_turned = refs[blocks : blocks + 6]
+    gain_ref, held_gate, held_upper, gate_ref, up_ref, down_turned = refs[blocks : blocks + 6]
     grads = jnp.concatenate([ref[2 * CAP :] for ref in refs[:blocks]], axis=0)
     hidden_grad = wide_product(grads, down_turned)
-    gate_grad = (hidden_grad * to_gate_ref[...]).astype(jnp.bfloat16)
-    upper_grad = (hidden_grad * to_up_ref[...]).astype(jnp.bfloat16)
+    gate, upper = held_gate[...], held_upper[...]
+    sigma = jax.nn.sigmoid(gate)
+    gate_grad = (hidden_grad * upper * sigma * (1.0 + gate * (1.0 - sigma))).astype(jnp.bfloat16)
+    upper_grad = (hidden_grad * gate * sigma).astype(jnp.bfloat16)
     total = wide_product(gate_grad, gate_ref.at[0]) + wide_product(upper_grad, up_ref.at[0])
     rows = jnp.concatenate([ref[CAP : 2 * CAP] for ref in refs[:blocks]], axis=0)
     unit, scale = unit_rows(rows)
@@ -335,15 +347,23 @@
     rows = devices * CAP
     weight_bytes = 3 * hidden * width * 2
     outs = [bf16((rows // 2, width))] * 2
+    (held_rows,) = call(
+        normalized,
+        [bf16((2 * CAP * (devices - 1), width))],
+        [VMEM] * devices,
+        0,
+        8 * CAP * devices * width,
+        16,
+    )(*blocks[:-1], norm_gain)
     factor = jax.ShapeDtypeStruct((rows, hidden), jnp.float32)
-    *parts_f, to_gate, to_up = call(
+    *parts_f, gate_b, upper_b = call(
         functools.partial(expert_forward, devices),
         outs + [factor] * 2,
-        [VMEM] * (devices + 4),
+        [VMEM] * 6,
         10 * rows * hidden * width,
         weight_bytes,
         16,
-    )(*blocks, norm_gain, gate_turned, up_turned, down)
+    )(blocks[-1], held_rows, norm_gain, gate_turned, up_turned, down)
     parts_b = call(
         functools.partial(expert_backward, devices),
         outs,
@@ -351,7 +371,7 @@
         6 * rows * hidden * width,
         weight_bytes,
         16,
-    )(*blocks, norm_gain, to_gate, to_up, gate, up, down_turned)
+    )(*blocks, norm_gain, gate_b, upper_b, gate, up, down_turned)
 
     def handed_back(kept, given, distance):
         step = 1

time: 40.9 us -> 40.8 us (level)
  no operation moved by 1% of the time
where the time goes in v6:
time: 40.8 us; the launch traced here: 40.3 us
  starting transfers between devices  19.8 us (49%)
  Pallas kernels  12.4 us (30%)
  waiting for transfers between devices  7.41 us (18%)
  between operations  0.74 us (2%)
    ppermute x5, starting transfers between devices, swapped(): return lax.ppermute(block, 'expert', [(i, i ^ k) for i in range(devices)])  9.32 us
    ppermute x4, starting transfers between devices, returned(): return lax.ppermute(block, ('section', 'expert'), route)  7.74 us
    ppermute x5, waiting for transfers between devices, swapped(): return lax.ppermute(block, 'expert', [(i, i ^ k) for i in range(devices)])  6.69 us
    pallas_call x1, Pallas kernels, on_device(): call(functools.partial(load, pieces), [bf16((tokens, width + LANES))] * 2...  4.6 us
    ppermute x2, starting transfers between devices, moved(): return lax.ppermute(block, 'section', route)  2.69 us
    pallas_call x1, Pallas kernels, on_device(): call(functools.partial(expert_backward, devices), outs, [VMEM] * (devices...  1.99 us
    pallas_call x1, Pallas kernels, on_device(): call(dispatch, [bf16((3 * CAP, width))] * 2 + [jax.ShapeDtypeStruct((n, t...  1.81 us
    pallas_call x1, Pallas kernels, on_device(): call(functools.partial(expert_forward, devices), outs + [factor] * 2, [VM...  1.58 us
  transfers between devices with their start and end apart: 11, of which 5 were waited for; matrix products, arithmetic and copies ran while one was open for 0% of the time, Pallas kernels for 24%

profile of v6, /device:TPU:0, one launch (start us, length us, event | category | flops | bytes accessed | tf_op | source)
XLA Modules:
  0.0 40.3 jit_solution(12066975834939598705)
XLA Ops:
  0.6 1.8 %shard_map.122 = (bf16[48,2048]{1,0:T(8,128)(2,1)S(1)}, bf16[48,2048]{1,0:T(8,128)(2,1)S(1)}, f32[40,128]{1,0:T(8,128)S(1)}, f32[32,128]{1,0:T(8,128)S(1)}) custom-call(s32[1]{0:T(128)} %bitcast.owner_ref, s32[1,8,128]{2,1,0:T(8,128)} %bitcast.5, f32[1,8,128]{2,1,0:T(8,128)} %bitcast.6, s32[1,8,128]{2,1,0:T(8,128)} %bitcast.7, f32[1,8,128]{2,1,0:T(8,128)} %bitcast.8, ...), custom_call_target="tpu_custom_call" | custom-call | flops 50331648 | bytes 1572864 | tf_op jit(solution)/shard_map/pallas_call | solution.py:310
  2.5 4.1 %collective-permute-start.1 = (bf16[48,2048]{1,0:T(8,128)(2,1)S(1)}, bf16[48,2048]{1,0:T(8,128)(2,1)S(1)}, u32[]{:S(2)}, u32[]{:S(2)}) collective-permute-start(bf16[48,2048]{1,0:T(8,128)(2,1)S(1)} %get-tuple-element.36), channel_id=1, source_target_pairs={{0,2},{1,3},{2,0},{3,1},{4,6},{5,7},{6,4},{7,5},{8,10},{9,11},{10,... | collective-permute-start | bytes 589832 | tf_op jit(solution)/shard_map/ppermute | solution.py:281
  6.6 1.6 %collective-permute-start.2 = (bf16[48,2048]{1,0:T(8,128)(2,1)S(1)}, bf16[48,2048]{1,0:T(8,128)(2,1)S(1)}, u32[]{:S(2)}, u32[]{:S(2)}) collective-permute-start(bf16[48,2048]{1,0:T(8,128)(2,1)S(1)} %get-tuple-element.45.refs_0_), channel_id=1, source_target_pairs={{0,1},{1,0},{2,3},{3,2},{4,5},{5,4},{6,7},{7,6},{8,9},{9,8},{10,11... | collective-permute-start | bytes 589832 | tf_op jit(solution)/shard_map/ppermute | solution.py:281
  8.1 0.0 copy-start
  8.1 4.6 %shard_map.123 = (bf16[128,2176]{1,0:T(8,128)(2,1)S(1)}, bf16[128,2176]{1,0:T(8,128)(2,1)S(1)}, bf16[1,768,2048]{2,1,0:T(8,128)(2,1)S(1)}, bf16[1,768,2048]{2,1,...) custom-call(bf16[1,128,2048]{2,1,0:T(8,128)(2,1)} %rows_f.1, ...), custom_call_target="tpu_custom_call" | custom-call | bytes 37748736 | tf_op jit(solution)/shard_map/pallas_call | solution.py:325
  12.8 0.1 collective-permute-start
  12.8 2.6 %collective-permute-start.7 = (bf16[128,2176]{1,0:T(8,128)(2,1)S(1)}, bf16[128,2176]{1,0:T(8,128)(2,1)S(1)}, u32[]{:S(2)}, u32[]{:S(2)}) collective-permute-start(bf16[128,2176]{1,0:T(8,128)(2,1)S(1)} %get-tuple-element.54), channel_id=1, source_target_pairs={{0,28},{4,0},{8,4},{12,8},{16,12},{20,16},{24,20},{28,24},{1,29},{... | collective-permute-start | bytes 1671176 | tf_op jit(solution)/shard_map/ppermute | solution.py:285
  15.4 0.3 collective-permute-done.1.refs_2_
  15.8 0.2 collective-permute-done.2.refs_1_
  16.0 1.5 %collective-permute-start.3 = (bf16[48,2048]{1,0:T(8,128)(2,1)S(1)}, bf16[48,2048]{1,0:T(8,128)(2,1)S(1)}, u32[]{:S(2)}, u32[]{:S(2)}) collective-permute-start(bf16[48,2048]{1,0:T(8,128)(2,1)S(1)} %collective-permute-done.1.refs_2_), channel_id=1, source_target_pairs={{0,1},{1,0},{2,3},{3,2},{4,5},{5,4},{6,7},{7,6},{8,9},{9,8},{10,11... | collective-permute-start | bytes 589832 | tf_op jit(solution)/shard_map/ppermute | solution.py:281
  17.5 0.0 copy-done
  17.5 0.2 shard_map.124.held_ref
  17.7 4.2 %collective-permute-done.3.last_ref.refs_3_ = bf16[48,2048]{1,0:T(8,128)(2,1)S(1)} collective-permute-done((bf16[48,2048]{1,0:T(8,128)(2,1)S(1)}, bf16[48,2048]{1,0:T(8,128)(2,1)S(1)}, u32[]{:S(2)}, u32[]{:S(2)}) %collective-permute-start.3) | collective-permute-done | bytes 196640 | tf_op jit(solution)/shard_map/ppermute | solution.py:281
  21.8 1.6 %shard_map.125 = (bf16[32,2048]{1,0:T(8,128)(2,1)S(1)}, bf16[32,2048]{1,0:T(8,128)(2,1)S(1)}, f32[64,768]{1,0:T(8,128)S(1)}, f32[64,768]{1,0:T(8,128)S(1)}) custom-call(bf16[48,2048]{1,0:T(8,128)(2,1)S(1)} %collective-permute-done.3.last_ref.refs_3_, bf16[96,2048]{1,0:T(8,128)(2,1)S(1)} %shard_map.124.held_ref, f32[1,2048]{1,0:T(1,128)S(1)} %copy-done, ...), custom_call_target="tpu_custom_call" | custom-call | flops 1006632960 | bytes 9437184 | tf_op jit(solution)/shard_map/pallas_call | solution.py:359
  23.4 1.5 %collective-permute-start.4 = (bf16[32,2048]{1,0:T(8,128)(2,1)S(1)}, bf16[32,2048]{1,0:T(8,128)(2,1)S(1)}, u32[]{:S(2)}, u32[]{:S(2)}) collective-permute-start(bf16[32,2048]{1,0:T(8,128)(2,1)S(1)} %get-tuple-element.51), channel_id=1, source_target_pairs={{0,1},{1,0},{2,3},{3,2},{4,5},{5,4},{6,7},{7,6},{8,9},{9,8},{10,11... | collective-permute-start | bytes 393224 | tf_op jit(solution)/shard_map/ppermute | solution.py:281
  24.9 2.0 %shard_map.128 = (bf16[32,2048]{1,0:T(8,128)(2,1)S(1)}, bf16[32,2048]{1,0:T(8,128)(2,1)S(1)}) custom-call(bf16[48,2048]{1,0:T(8,128)(2,1)S(1)} %get-tuple-element.45.refs_0_, bf16[48,2048]{1,0:T(8,128)(2,1)S(1)} %collective-permute-done.2.refs_1_, bf16[48,2048]{1,0:T(8,128)(2,1)S(1)} %collective-permute-done.1.refs_2_, ...), custom_call_target="tpu_custom_call" | custom-call | flops 603979776 | bytes 9437184 | tf_op jit(solution)/shard_map/pallas_call | solution.py:367
  26.9 0.7 %collective-permute-start.8 = (bf16[32,2048]{1,0:T(8,128)(2,1)S(1)}, bf16[32,2048]{1,0:T(8,128)(2,1)S(1)}, u32[]{:S(2)}, u32[]{:S(2)}) collective-permute-start(bf16[32,2048]{1,0:T(8,128)(2,1)S(1)} %get-tuple-element.61), channel_id=1, source_target_pairs={{0,1},{1,0},{2,3},{3,2},{4,5},{5,4},{6,7},{7,6},{8,9},{9,8},{10,11... | collective-permute-start | bytes 393224 | tf_op jit(solution)/shard_map/ppermute | solution.py:281
  27.6 2.0 %collective-permute-done.4.received_ref = bf16[32,2048]{1,0:T(8,128)(2,1)S(1)} collective-permute-done((bf16[32,2048]{1,0:T(8,128)(2,1)S(1)}, bf16[32,2048]{1,0:T(8,128)(2,1)S(1)}, u32[]{:S(2)}, u32[]{:S(2)}) %collective-permute-start.4) | collective-permute-done | bytes 131104 | tf_op jit(solution)/shard_map/ppermute | solution.py:281
  29.6 0.1 collective-permute-start.5
  29.7 3.2 %collective-permute-start.6 = (bf16[16,2048]{1,0:T(8,128)(2,1)S(1)}, bf16[16,2048]{1,0:T(8,128)(2,1)S(1)}, u32[]{:S(2)}, u32[]{:S(2)}) collective-permute-start(bf16[16,2048]{1,0:T(8,128)(2,1)S(1)} %get-tuple-element.53), channel_id=1, source_target_pairs={{0,6},{1,7},{2,4},{3,5},{4,10},{5,11},{6,8},{7,9},{8,14},{9,15},{1... | collective-permute-start | bytes 196616 | tf_op jit(solution)/shard_map/ppermute | solution.py:293
  32.9 0.0 collective-permute-done.8.received_ref
  33.0 1.0 %collective-permute-start.9 = (bf16[16,2048]{1,0:T(8,128)(2,1)S(1)}, bf16[16,2048]{1,0:T(8,128)(2,1)S(1)}, u32[]{:S(2)}, u32[]{:S(2)}) collective-permute-start(bf16[16,2048]{1,0:T(8,128)(2,1)S(1)} %get-tuple-element.62), channel_id=1, source_target_pairs={{0,28},{1,29},{2,30},{3,31},{4,0},{5,1},{6,2},{7,3},{8,4},{9,5},{1... | collective-permute-start | bytes 196616 | tf_op jit(solution)/shard_map/ppermute | solution.py:293
  33.9 0.0 collective-permute-done.early_ref
  33.9 3.4 %collective-permute-start.10 = (bf16[16,2048]{1,0:T(8,128)(2,1)S(1)}, bf16[16,2048]{1,0:T(8,128)(2,1)S(1)}, u32[]{:S(2)}, u32[]{:S(2)}) collective-permute-start(bf16[16,2048]{1,0:T(8,128)(2,1)S(1)} %get-tuple-element.63), channel_id=1, source_target_pairs={{0,30},{1,31},{2,28},{3,29},{4,2},{5,3},{6,0},{7,1},{8,6},{9,7},{1... | collective-permute-start | bytes 196616 | tf_op jit(solution)/shard_map/ppermute | solution.py:293
  37.4 0.0 collective-permute-done.5.own_ref
  37.4 0.0 collective-permute-done.6.other_ref
  37.4 1.2 %shard_map.127 = bf16[1,128,2048]{2,1,0:T(8,128)(2,1)} custom-call(bf16[128,2176]{1,0:T(8,128)(2,1)S(1)} %collective-permute-done.early_ref, bf16[16,2048]{1,0:T(8,128)(2,1)S(1)} %collective-permute-done.5.own_ref, bf16[16,2048]{1,0:T(8,128)(2,1)S(1)} %collective-permute-done.6.other_ref), custom_call_target="tpu_custom_call" | custom-call | flops 16777216 | bytes 1572864 | tf_op jit(solution)/shard_map/pallas_call | solution.py:396
  38.6 0.0 collective-permute-done.7.early_ref
  38.6 0.0 collective-permute-done.9.own_ref
  38.6 0.7 %collective-permute-done.10.other_ref = bf16[16,2048]{1,0:T(8,128)(2,1)S(1)} collective-permute-done((bf16[16,2048]{1,0:T(8,128)(2,1)S(1)}, bf16[16,2048]{1,0:T(8,128)(2,1)S(1)}, u32[]{:S(2)}, u32[]{:S(2)}) %collective-permute-start.10) | collective-permute-done | bytes 65568 | tf_op jit(solution)/shard_map/ppermute | solution.py:293
  39.3 1.0 %shard_map.130 = bf16[1,128,2048]{2,1,0:T(8,128)(2,1)} custom-call(bf16[128,2176]{1,0:T(8,128)(2,1)S(1)} %collective-permute-done.7.early_ref, bf16[16,2048]{1,0:T(8,128)(2,1)S(1)} %collective-permute-done.9.own_ref, bf16[16,2048]{1,0:T(8,128)(2,1)S(1)} %collective-permute-done.10.other_ref), custom_call_target="tpu_custom_call" | custom-call | flops 16777216 | bytes 1572864 | tf_op jit(solution)/shard_map/pallas_call | solution.py:399
  (2 shorter events, 0.1 us)
Async XLA Ops:
  2.5 13.3 %collective-permute-start.1 = (bf16[48,2048]{1,0:T(8,128)(2,1)S(1)}, bf16[48,2048]{1,0:T(8,128)(2,1)S(1)}, u32[]{:S(2)}, u32[]{:S(2)}) collective-permute-start(bf16[48,2048]{1,0:T(8,128)(2,1)S(1)} %get-tuple-element.36), channel_id=1, source_target_pairs={{0,2},{1,3},{2,0},{3,1},{4,6},{5,7},{6,4},{7,5},{8,10},{9,11},{10,... | collective-permute-start | bytes 589832 | tf_op jit(solution)/shard_map/ppermute | solution.py:281
  6.6 9.4 %collective-permute-start.2 = (bf16[48,2048]{1,0:T(8,128)(2,1)S(1)}, bf16[48,2048]{1,0:T(8,128)(2,1)S(1)}, u32[]{:S(2)}, u32[]{:S(2)}) collective-permute-start(bf16[48,2048]{1,0:T(8,128)(2,1)S(1)} %get-tuple-element.45.refs_0_), channel_id=1, source_target_pairs={{0,1},{1,0},{2,3},{3,2},{4,5},{5,4},{6,7},{7,6},{8,9},{9,8},{10,11... | collective-permute-start | bytes 589832 | tf_op jit(solution)/shard_map/ppermute | solution.py:281
  8.1 9.3 %copy-start = (f32[1,2048]{1,0:T(1,128)S(1)}, f32[1,2048]{1,0:T(1,128)}, u32[]{:S(2)}) copy-start(f32[1,2048]{1,0:T(1,128)} %refs_4_.3) | copy-start | bytes 24580
  12.8 21.2 %collective-permute-start = (bf16[128,2176]{1,0:T(8,128)(2,1)S(1)}, bf16[128,2176]{1,0:T(8,128)(2,1)S(1)}, u32[]{:S(2)}, u32[]{:S(2)}) collective-permute-start(bf16[128,2176]{1,0:T(8,128)(2,1)S(1)} %get-tuple-element.35), channel_id=1, source_target_pairs={{0,4},{4,8},{8,12},{12,16},{16,20},{20,24},{24,28},{28,0},{1,5},{5... | collective-permute-start | bytes 1671176 | tf_op jit(solution)/shard_map/ppermute | solution.py:285
  12.8 25.8 %collective-permute-start.7 = (bf16[128,2176]{1,0:T(8,128)(2,1)S(1)}, bf16[128,2176]{1,0:T(8,128)(2,1)S(1)}, u32[]{:S(2)}, u32[]{:S(2)}) collective-permute-start(bf16[128,2176]{1,0:T(8,128)(2,1)S(1)} %get-tuple-element.54), channel_id=1, source_target_pairs={{0,28},{4,0},{8,4},{12,8},{16,12},{20,16},{24,20},{28,24},{1,29},{... | collective-permute-start | bytes 1671176 | tf_op jit(solution)/shard_map/ppermute | solution.py:285
  16.0 5.8 %collective-permute-start.3 = (bf16[48,2048]{1,0:T(8,128)(2,1)S(1)}, bf16[48,2048]{1,0:T(8,128)(2,1)S(1)}, u32[]{:S(2)}, u32[]{:S(2)}) collective-permute-start(bf16[48,2048]{1,0:T(8,128)(2,1)S(1)} %collective-permute-done.1.refs_2_), channel_id=1, source_target_pairs={{0,1},{1,0},{2,3},{3,2},{4,5},{5,4},{6,7},{7,6},{8,9},{9,8},{10,11... | collective-permute-start | bytes 589832 | tf_op jit(solution)/shard_map/ppermute | solution.py:281
  23.4 6.2 %collective-permute-start.4 = (bf16[32,2048]{1,0:T(8,128)(2,1)S(1)}, bf16[32,2048]{1,0:T(8,128)(2,1)S(1)}, u32[]{:S(2)}, u32[]{:S(2)}) collective-permute-start(bf16[32,2048]{1,0:T(8,128)(2,1)S(1)} %get-tuple-element.51), channel_id=1, source_target_pairs={{0,1},{1,0},{2,3},{3,2},{4,5},{5,4},{6,7},{7,6},{8,9},{9,8},{10,11... | collective-permute-start | bytes 393224 | tf_op jit(solution)/shard_map/ppermute | solution.py:281
  26.9 6.0 %collective-permute-start.8 = (bf16[32,2048]{1,0:T(8,128)(2,1)S(1)}, bf16[32,2048]{1,0:T(8,128)(2,1)S(1)}, u32[]{:S(2)}, u32[]{:S(2)}) collective-permute-start(bf16[32,2048]{1,0:T(8,128)(2,1)S(1)} %get-tuple-element.61), channel_id=1, source_target_pairs={{0,1},{1,0},{2,3},{3,2},{4,5},{5,4},{6,7},{7,6},{8,9},{9,8},{10,11... | collective-permute-start | bytes 393224 | tf_op jit(solution)/shard_map/ppermute | solution.py:281
  29.6 7.8 %collective-permute-start.5 = (bf16[16,2048]{1,0:T(8,128)(2,1)S(1)}, bf16[16,2048]{1,0:T(8,128)(2,1)S(1)}, u32[]{:S(2)}, u32[]{:S(2)}) collective-permute-start(bf16[16,2048]{1,0:T(8,128)(2,1)S(1)} %get-tuple-element.52), channel_id=1, source_target_pairs={{0,4},{1,5},{2,6},{3,7},{4,8},{5,9},{6,10},{7,11},{8,12},{9,13},{1... | collective-permute-start | bytes 196616 | tf_op jit(solution)/shard_map/ppermute | solution.py:293
  29.7 7.7 %collective-permute-start.6 = (bf16[16,2048]{1,0:T(8,128)(2,1)S(1)}, bf16[16,2048]{1,0:T(8,128)(2,1)S(1)}, u32[]{:S(2)}, u32[]{:S(2)}) collective-permute-start(bf16[16,2048]{1,0:T(8,128)(2,1)S(1)} %get-tuple-element.53), channel_id=1, source_target_pairs={{0,6},{1,7},{2,4},{3,5},{4,10},{5,11},{6,8},{7,9},{8,14},{9,15},{1... | collective-permute-start | bytes 196616 | tf_op jit(solution)/shard_map/ppermute | solution.py:293
  33.0 5.6 %collective-permute-start.9 = (bf16[16,2048]{1,0:T(8,128)(2,1)S(1)}, bf16[16,2048]{1,0:T(8,128)(2,1)S(1)}, u32[]{:S(2)}, u32[]{:S(2)}) collective-permute-start(bf16[16,2048]{1,0:T(8,128)(2,1)S(1)} %get-tuple-element.62), channel_id=1, source_target_pairs={{0,28},{1,29},{2,30},{3,31},{4,0},{5,1},{6,2},{7,3},{8,4},{9,5},{1... | collective-permute-start | bytes 196616 | tf_op jit(solution)/shard_map/ppermute | solution.py:293
  33.9 5.3 %collective-permute-start.10 = (bf16[16,2048]{1,0:T(8,128)(2,1)S(1)}, bf16[16,2048]{1,0:T(8,128)(2,1)S(1)}, u32[]{:S(2)}, u32[]{:S(2)}) collective-permute-start(bf16[16,2048]{1,0:T(8,128)(2,1)S(1)} %get-tuple-element.63), channel_id=1, source_target_pairs={{0,30},{1,31},{2,28},{3,29},{4,2},{5,3},{6,0},{7,1},{8,6},{9,7},{1... | collective-permute-start | bytes 196616 | tf_op jit(solution)/shard_map/ppermute | solution.py:293

commit v7 on v6

--- a/solution.py
+++ b/solution.py
@@ -191,7 +191,7 @@
     upper_ref[...] = upper[split:]
     gate, upper = gate[:split], upper[:split]
     hidden = (gate * jax.nn.sigmoid(gate) * upper).astype(jnp.bfloat16)
-    give((kept_ref, given_ref), wide_product(hidden, down_ref.at[0]).astype(jnp.bfloat16))
+    give((kept_ref, given_ref), product(hidden, down_ref.at[0]).astype(jnp.bfloat16))
 
 
 def expert_backward(blocks, *refs):

time: 40.8 us -> 40.9 us (level)
  no operation moved by 1% of the time
where the time goes in v7:
time: 40.9 us; the launch traced here: 40.4 us
  starting transfers between devices  19.7 us (48%)
  Pallas kernels  12.5 us (31%)
  waiting for transfers between devices  7.41 us (18%)
  between operations  0.73 us (2%)
    ppermute x5, starting transfers between devices, swapped(): return lax.ppermute(block, 'expert', [(i, i ^ k) for i in range(devices)])  9.32 us
    ppermute x4, starting transfers between devices, returned(): return lax.ppermute(block, ('section', 'expert'), route)  7.74 us
    ppermute x5, waiting for transfers between devices, swapped(): return lax.ppermute(block, 'expert', [(i, i ^ k) for i in range(devices)])  6.69 us
    pallas_call x1, Pallas kernels, on_device(): call(functools.partial(load, pieces), [bf16((tokens, width + LANES))] * 2...  4.6 us
    ppermute x2, starting transfers between devices, moved(): return lax.ppermute(block, 'section', route)  2.69 us
    pallas_call x1, Pallas kernels, on_device(): call(functools.partial(expert_backward, devices), outs, [VMEM] * (devices...  1.99 us
    pallas_call x1, Pallas kernels, on_device(): call(dispatch, [bf16((3 * CAP, width))] * 2 + [jax.ShapeDtypeStruct((n, t...  1.81 us
    pallas_call x1, Pallas kernels, on_device(): call(functools.partial(expert_forward, devices), outs + [factor] * 2, [VM...  1.67 us
  transfers between devices with their start and end apart: 11, of which 5 were waited for; matrix products, arithmetic and copies ran while one was open for 0% of the time, Pallas kernels for 24%

profile of v7, /device:TPU:0, one launch (start us, length us, event | category | flops | bytes accessed | tf_op | source)
XLA Modules:
  0.0 40.4 jit_solution(6713160161009727333)
XLA Ops:
  0.6 1.8 %shard_map.122 = (bf16[48,2048]{1,0:T(8,128)(2,1)S(1)}, bf16[48,2048]{1,0:T(8,128)(2,1)S(1)}, f32[40,128]{1,0:T(8,128)S(1)}, f32[32,128]{1,0:T(8,128)S(1)}) custom-call(s32[1]{0:T(128)} %bitcast.owner_ref, s32[1,8,128]{2,1,0:T(8,128)} %bitcast.5, f32[1,8,128]{2,1,0:T(8,128)} %bitcast.6, s32[1,8,128]{2,1,0:T(8,128)} %bitcast.7, f32[1,8,128]{2,1,0:T(8,128)} %bitcast.8, ...), custom_call_target="tpu_custom_call" | custom-call | flops 50331648 | bytes 1572864 | tf_op jit(solution)/shard_map/pallas_call | solution.py:310
  2.5 4.1 %collective-permute-start.1 = (bf16[48,2048]{1,0:T(8,128)(2,1)S(1)}, bf16[48,2048]{1,0:T(8,128)(2,1)S(1)}, u32[]{:S(2)}, u32[]{:S(2)}) collective-permute-start(bf16[48,2048]{1,0:T(8,128)(2,1)S(1)} %get-tuple-element.36), channel_id=1, source_target_pairs={{0,2},{1,3},{2,0},{3,1},{4,6},{5,7},{6,4},{7,5},{8,10},{9,11},{10,... | collective-permute-start | bytes 589832 | tf_op jit(solution)/shard_map/ppermute | solution.py:281
  6.6 1.6 %collective-permute-start.2 = (bf16[48,2048]{1,0:T(8,128)(2,1)S(1)}, bf16[48,2048]{1,0:T(8,128)(2,1)S(1)}, u32[]{:S(2)}, u32[]{:S(2)}) collective-permute-start(bf16[48,2048]{1,0:T(8,128)(2,1)S(1)} %get-tuple-element.45.refs_0_), channel_id=1, source_target_pairs={{0,1},{1,0},{2,3},{3,2},{4,5},{5,4},{6,7},{7,6},{8,9},{9,8},{10,11... | collective-permute-start | bytes 589832 | tf_op jit(solution)/shard_map/ppermute | solution.py:281
  8.1 0.0 copy-start
  8.1 4.6 %shard_map.123 = (bf16[128,2176]{1,0:T(8,128)(2,1)S(1)}, bf16[128,2176]{1,0:T(8,128)(2,1)S(1)}, bf16[1,768,2048]{2,1,0:T(8,128)(2,1)S(1)}, bf16[1,768,2048]{2,1,...) custom-call(bf16[1,128,2048]{2,1,0:T(8,128)(2,1)} %rows_f.1, ...), custom_call_target="tpu_custom_call" | custom-call | bytes 37748736 | tf_op jit(solution)/shard_map/pallas_call | solution.py:325
  12.8 0.1 collective-permute-start
  12.8 2.6 %collective-permute-start.7 = (bf16[128,2176]{1,0:T(8,128)(2,1)S(1)}, bf16[128,2176]{1,0:T(8,128)(2,1)S(1)}, u32[]{:S(2)}, u32[]{:S(2)}) collective-permute-start(bf16[128,2176]{1,0:T(8,128)(2,1)S(1)} %get-tuple-element.54), channel_id=1, source_target_pairs={{0,28},{4,0},{8,4},{12,8},{16,12},{20,16},{24,20},{28,24},{1,29},{... | collective-permute-start | bytes 1671176 | tf_op jit(solution)/shard_map/ppermute | solution.py:285
  15.4 0.3 collective-permute-done.1.refs_2_
  15.8 0.2 collective-permute-done.2.refs_1_
  16.0 1.5 %collective-permute-start.3 = (bf16[48,2048]{1,0:T(8,128)(2,1)S(1)}, bf16[48,2048]{1,0:T(8,128)(2,1)S(1)}, u32[]{:S(2)}, u32[]{:S(2)}) collective-permute-start(bf16[48,2048]{1,0:T(8,128)(2,1)S(1)} %collective-permute-done.1.refs_2_), channel_id=1, source_target_pairs={{0,1},{1,0},{2,3},{3,2},{4,5},{5,4},{6,7},{7,6},{8,9},{9,8},{10,11... | collective-permute-start | bytes 589832 | tf_op jit(solution)/shard_map/ppermute | solution.py:281
  17.5 0.0 copy-done
  17.5 0.2 shard_map.124.held_ref
  17.7 4.2 %collective-permute-done.3.last_ref.refs_3_ = bf16[48,2048]{1,0:T(8,128)(2,1)S(1)} collective-permute-done((bf16[48,2048]{1,0:T(8,128)(2,1)S(1)}, bf16[48,2048]{1,0:T(8,128)(2,1)S(1)}, u32[]{:S(2)}, u32[]{:S(2)}) %collective-permute-start.3) | collective-permute-done | bytes 196640 | tf_op jit(solution)/shard_map/ppermute | solution.py:281
  21.8 1.7 %shard_map.125 = (bf16[32,2048]{1,0:T(8,128)(2,1)S(1)}, bf16[32,2048]{1,0:T(8,128)(2,1)S(1)}, f32[64,768]{1,0:T(8,128)S(1)}, f32[64,768]{1,0:T(8,128)S(1)}) custom-call(bf16[48,2048]{1,0:T(8,128)(2,1)S(1)} %collective-permute-done.3.last_ref.refs_3_, bf16[96,2048]{1,0:T(8,128)(2,1)S(1)} %shard_map.124.held_ref, f32[1,2048]{1,0:T(1,128)S(1)} %copy-done, ...), custom_call_target="tpu_custom_call" | custom-call | flops 1006632960 | bytes 9437184 | tf_op jit(solution)/shard_map/pallas_call | solution.py:359
  23.5 1.5 %collective-permute-start.4 = (bf16[32,2048]{1,0:T(8,128)(2,1)S(1)}, bf16[32,2048]{1,0:T(8,128)(2,1)S(1)}, u32[]{:S(2)}, u32[]{:S(2)}) collective-permute-start(bf16[32,2048]{1,0:T(8,128)(2,1)S(1)} %get-tuple-element.51), channel_id=1, source_target_pairs={{0,1},{1,0},{2,3},{3,2},{4,5},{5,4},{6,7},{7,6},{8,9},{9,8},{10,11... | collective-permute-start | bytes 393224 | tf_op jit(solution)/shard_map/ppermute | solution.py:281
  25.0 2.0 %shard_map.128 = (bf16[32,2048]{1,0:T(8,128)(2,1)S(1)}, bf16[32,2048]{1,0:T(8,128)(2,1)S(1)}) custom-call(bf16[48,2048]{1,0:T(8,128)(2,1)S(1)} %get-tuple-element.45.refs_0_, bf16[48,2048]{1,0:T(8,128)(2,1)S(1)} %collective-permute-done.2.refs_1_, bf16[48,2048]{1,0:T(8,128)(2,1)S(1)} %collective-permute-done.1.refs_2_, ...), custom_call_target="tpu_custom_call" | custom-call | flops 603979776 | bytes 9437184 | tf_op jit(solution)/shard_map/pallas_call | solution.py:367
  27.0 0.7 %collective-permute-start.8 = (bf16[32,2048]{1,0:T(8,128)(2,1)S(1)}, bf16[32,2048]{1,0:T(8,128)(2,1)S(1)}, u32[]{:S(2)}, u32[]{:S(2)}) collective-permute-start(bf16[32,2048]{1,0:T(8,128)(2,1)S(1)} %get-tuple-element.61), channel_id=1, source_target_pairs={{0,1},{1,0},{2,3},{3,2},{4,5},{5,4},{6,7},{7,6},{8,9},{9,8},{10,11... | collective-permute-start | bytes 393224 | tf_op jit(solution)/shard_map/ppermute | solution.py:281
  27.6 2.0 %collective-permute-done.4.received_ref = bf16[32,2048]{1,0:T(8,128)(2,1)S(1)} collective-permute-done((bf16[32,2048]{1,0:T(8,128)(2,1)S(1)}, bf16[32,2048]{1,0:T(8,128)(2,1)S(1)}, u32[]{:S(2)}, u32[]{:S(2)}) %collective-permute-start.4) | collective-permute-done | bytes 131104 | tf_op jit(solution)/shard_map/ppermute | solution.py:281
  29.7 0.1 collective-permute-start.5
  29.7 3.3 %collective-permute-start.6 = (bf16[16,2048]{1,0:T(8,128)(2,1)S(1)}, bf16[16,2048]{1,0:T(8,128)(2,1)S(1)}, u32[]{:S(2)}, u32[]{:S(2)}) collective-permute-start(bf16[16,2048]{1,0:T(8,128)(2,1)S(1)} %get-tuple-element.53), channel_id=1, source_target_pairs={{0,6},{1,7},{2,4},{3,5},{4,10},{5,11},{6,8},{7,9},{8,14},{9,15},{1... | collective-permute-start | bytes 196616 | tf_op jit(solution)/shard_map/ppermute | solution.py:293
  33.0 0.0 collective-permute-done.8.received_ref
  33.0 1.0 %collective-permute-start.9 = (bf16[16,2048]{1,0:T(8,128)(2,1)S(1)}, bf16[16,2048]{1,0:T(8,128)(2,1)S(1)}, u32[]{:S(2)}, u32[]{:S(2)}) collective-permute-start(bf16[16,2048]{1,0:T(8,128)(2,1)S(1)} %get-tuple-element.62), channel_id=1, source_target_pairs={{0,28},{1,29},{2,30},{3,31},{4,0},{5,1},{6,2},{7,3},{8,4},{9,5},{1... | collective-permute-start | bytes 196616 | tf_op jit(solution)/shard_map/ppermute | solution.py:293
  34.0 0.0 collective-permute-done.early_ref
  34.0 3.4 %collective-permute-start.10 = (bf16[16,2048]{1,0:T(8,128)(2,1)S(1)}, bf16[16,2048]{1,0:T(8,128)(2,1)S(1)}, u32[]{:S(2)}, u32[]{:S(2)}) collective-permute-start(bf16[16,2048]{1,0:T(8,128)(2,1)S(1)} %get-tuple-element.63), channel_id=1, source_target_pairs={{0,30},{1,31},{2,28},{3,29},{4,2},{5,3},{6,0},{7,1},{8,6},{9,7},{1... | collective-permute-start | bytes 196616 | tf_op jit(solution)/shard_map/ppermute | solution.py:293
  37.5 0.0 collective-permute-done.5.own_ref
  37.5 0.0 collective-permute-done.6.other_ref
  37.5 1.2 %shard_map.127 = bf16[1,128,2048]{2,1,0:T(8,128)(2,1)} custom-call(bf16[128,2176]{1,0:T(8,128)(2,1)S(1)} %collective-permute-done.early_ref, bf16[16,2048]{1,0:T(8,128)(2,1)S(1)} %collective-permute-done.5.own_ref, bf16[16,2048]{1,0:T(8,128)(2,1)S(1)} %collective-permute-done.6.other_ref), custom_call_target="tpu_custom_call" | custom-call | flops 16777216 | bytes 1572864 | tf_op jit(solution)/shard_map/pallas_call | solution.py:396
  38.6 0.0 collective-permute-done.7.early_ref
  38.6 0.0 collective-permute-done.9.own_ref
  38.7 0.7 %collective-permute-done.10.other_ref = bf16[16,2048]{1,0:T(8,128)(2,1)S(1)} collective-permute-done((bf16[16,2048]{1,0:T(8,128)(2,1)S(1)}, bf16[16,2048]{1,0:T(8,128)(2,1)S(1)}, u32[]{:S(2)}, u32[]{:S(2)}) %collective-permute-start.10) | collective-permute-done | bytes 65568 | tf_op jit(solution)/shard_map/ppermute | solution.py:293
  39.4 1.0 %shard_map.130 = bf16[1,128,2048]{2,1,0:T(8,128)(2,1)} custom-call(bf16[128,2176]{1,0:T(8,128)(2,1)S(1)} %collective-permute-done.7.early_ref, bf16[16,2048]{1,0:T(8,128)(2,1)S(1)} %collective-permute-done.9.own_ref, bf16[16,2048]{1,0:T(8,128)(2,1)S(1)} %collective-permute-done.10.other_ref), custom_call_target="tpu_custom_call" | custom-call | flops 16777216 | bytes 1572864 | tf_op jit(solution)/shard_map/pallas_call | solution.py:399
  (2 shorter events, 0.1 us)
Async XLA Ops:
  2.5 13.3 %collective-permute-start.1 = (bf16[48,2048]{1,0:T(8,128)(2,1)S(1)}, bf16[48,2048]{1,0:T(8,128)(2,1)S(1)}, u32[]{:S(2)}, u32[]{:S(2)}) collective-permute-start(bf16[48,2048]{1,0:T(8,128)(2,1)S(1)} %get-tuple-element.36), channel_id=1, source_target_pairs={{0,2},{1,3},{2,0},{3,1},{4,6},{5,7},{6,4},{7,5},{8,10},{9,11},{10,... | collective-permute-start | bytes 589832 | tf_op jit(solution)/shard_map/ppermute | solution.py:281
  6.6 9.4 %collective-permute-start.2 = (bf16[48,2048]{1,0:T(8,128)(2,1)S(1)}, bf16[48,2048]{1,0:T(8,128)(2,1)S(1)}, u32[]{:S(2)}, u32[]{:S(2)}) collective-permute-start(bf16[48,2048]{1,0:T(8,128)(2,1)S(1)} %get-tuple-element.45.refs_0_), channel_id=1, source_target_pairs={{0,1},{1,0},{2,3},{3,2},{4,5},{5,4},{6,7},{7,6},{8,9},{9,8},{10,11... | collective-permute-start | bytes 589832 | tf_op jit(solution)/shard_map/ppermute | solution.py:281
  8.1 9.3 %copy-start = (f32[1,2048]{1,0:T(1,128)S(1)}, f32[1,2048]{1,0:T(1,128)}, u32[]{:S(2)}) copy-start(f32[1,2048]{1,0:T(1,128)} %refs_4_.3) | copy-start | bytes 24580
  12.8 21.3 %collective-permute-start = (bf16[128,2176]{1,0:T(8,128)(2,1)S(1)}, bf16[128,2176]{1,0:T(8,128)(2,1)S(1)}, u32[]{:S(2)}, u32[]{:S(2)}) collective-permute-start(bf16[128,2176]{1,0:T(8,128)(2,1)S(1)} %get-tuple-element.35), channel_id=1, source_target_pairs={{0,4},{4,8},{8,12},{12,16},{16,20},{20,24},{24,28},{28,0},{1,5},{5... | collective-permute-start | bytes 1671176 | tf_op jit(solution)/shard_map/ppermute | solution.py:285
  12.8 25.8 %collective-permute-start.7 = (bf16[128,2176]{1,0:T(8,128)(2,1)S(1)}, bf16[128,2176]{1,0:T(8,128)(2,1)S(1)}, u32[]{:S(2)}, u32[]{:S(2)}) collective-permute-start(bf16[128,2176]{1,0:T(8,128)(2,1)S(1)} %get-tuple-element.54), channel_id=1, source_target_pairs={{0,28},{4,0},{8,4},{12,8},{16,12},{20,16},{24,20},{28,24},{1,29},{... | collective-permute-start | bytes 1671176 | tf_op jit(solution)/shard_map/ppermute | solution.py:285
  16.0 5.8 %collective-permute-start.3 = (bf16[48,2048]{1,0:T(8,128)(2,1)S(1)}, bf16[48,2048]{1,0:T(8,128)(2,1)S(1)}, u32[]{:S(2)}, u32[]{:S(2)}) collective-permute-start(bf16[48,2048]{1,0:T(8,128)(2,1)S(1)} %collective-permute-done.1.refs_2_), channel_id=1, source_target_pairs={{0,1},{1,0},{2,3},{3,2},{4,5},{5,4},{6,7},{7,6},{8,9},{9,8},{10,11... | collective-permute-start | bytes 589832 | tf_op jit(solution)/shard_map/ppermute | solution.py:281
  23.5 6.2 %collective-permute-start.4 = (bf16[32,2048]{1,0:T(8,128)(2,1)S(1)}, bf16[32,2048]{1,0:T(8,128)(2,1)S(1)}, u32[]{:S(2)}, u32[]{:S(2)}) collective-permute-start(bf16[32,2048]{1,0:T(8,128)(2,1)S(1)} %get-tuple-element.51), channel_id=1, source_target_pairs={{0,1},{1,0},{2,3},{3,2},{4,5},{5,4},{6,7},{7,6},{8,9},{9,8},{10,11... | collective-permute-start | bytes 393224 | tf_op jit(solution)/shard_map/ppermute | solution.py:281
  27.0 6.0 %collective-permute-start.8 = (bf16[32,2048]{1,0:T(8,128)(2,1)S(1)}, bf16[32,2048]{1,0:T(8,128)(2,1)S(1)}, u32[]{:S(2)}, u32[]{:S(2)}) collective-permute-start(bf16[32,2048]{1,0:T(8,128)(2,1)S(1)} %get-tuple-element.61), channel_id=1, source_target_pairs={{0,1},{1,0},{2,3},{3,2},{4,5},{5,4},{6,7},{7,6},{8,9},{9,8},{10,11... | collective-permute-start | bytes 393224 | tf_op jit(solution)/shard_map/ppermute | solution.py:281
  29.7 7.8 %collective-permute-start.5 = (bf16[16,2048]{1,0:T(8,128)(2,1)S(1)}, bf16[16,2048]{1,0:T(8,128)(2,1)S(1)}, u32[]{:S(2)}, u32[]{:S(2)}) collective-permute-start(bf16[16,2048]{1,0:T(8,128)(2,1)S(1)} %get-tuple-element.52), channel_id=1, source_target_pairs={{0,4},{1,5},{2,6},{3,7},{4,8},{5,9},{6,10},{7,11},{8,12},{9,13},{1... | collective-permute-start | bytes 196616 | tf_op jit(solution)/shard_map/ppermute | solution.py:293
  29.7 7.7 %collective-permute-start.6 = (bf16[16,2048]{1,0:T(8,128)(2,1)S(1)}, bf16[16,2048]{1,0:T(8,128)(2,1)S(1)}, u32[]{:S(2)}, u32[]{:S(2)}) collective-permute-start(bf16[16,2048]{1,0:T(8,128)(2,1)S(1)} %get-tuple-element.53), channel_id=1, source_target_pairs={{0,6},{1,7},{2,4},{3,5},{4,10},{5,11},{6,8},{7,9},{8,14},{9,15},{1... | collective-permute-start | bytes 196616 | tf_op jit(solution)/shard_map/ppermute | solution.py:293
  33.0 5.6 %collective-permute-start.9 = (bf16[16,2048]{1,0:T(8,128)(2,1)S(1)}, bf16[16,2048]{1,0:T(8,128)(2,1)S(1)}, u32[]{:S(2)}, u32[]{:S(2)}) collective-permute-start(bf16[16,2048]{1,0:T(8,128)(2,1)S(1)} %get-tuple-element.62), channel_id=1, source_target_pairs={{0,28},{1,29},{2,30},{3,31},{4,0},{5,1},{6,2},{7,3},{8,4},{9,5},{1... | collective-permute-start | bytes 196616 | tf_op jit(solution)/shard_map/ppermute | solution.py:293
  34.0 5.3 %collective-permute-start.10 = (bf16[16,2048]{1,0:T(8,128)(2,1)S(1)}, bf16[16,2048]{1,0:T(8,128)(2,1)S(1)}, u32[]{:S(2)}, u32[]{:S(2)}) collective-permute-start(bf16[16,2048]{1,0:T(8,128)(2,1)S(1)} %get-tuple-element.63), channel_id=1, source_target_pairs={{0,30},{1,31},{2,28},{3,29},{4,2},{5,3},{6,0},{7,1},{8,6},{9,7},{1... | collective-permute-start | bytes 196616 | tf_op jit(solution)/shard_map/ppermute | solution.py:293

commit v8 on v5

--- a/solution.py
+++ b/solution.py
@@ -10,7 +10,7 @@
 EF = 2
 CAP = 16
 EPSILON = 1e-06
-OUT_PIECES = 4
+OUT_PIECES = 2
 LANES = 128
 MIB = 1 << 20
 

time: 40.9 us -> 40.9 us (level)
  no operation moved by 1% of the time
where the time goes in v8:
time: 40.9 us; the launch traced here: 40.4 us
  starting transfers between devices  19.7 us (48%)
  Pallas kernels  12.3 us (30%)
  waiting for transfers between devices  7.62 us (19%)
  between operations  0.73 us (2%)
    ppermute x5, starting transfers between devices, swapped(): return lax.ppermute(block, 'expert', [(i, i ^ k) for i in range(devices)])  9.32 us
    ppermute x4, starting transfers between devices, returned(): return lax.ppermute(block, ('section', 'expert'), route)  7.72 us
    ppermute x5, waiting for transfers between devices, swapped(): return lax.ppermute(block, 'expert', [(i, i ^ k) for i in range(devices)])  6.9 us
    pallas_call x1, Pallas kernels, on_device(): call(functools.partial(load, pieces), [bf16((tokens, width + LANES))] * 2...  4.6 us
    ppermute x2, starting transfers between devices, moved(): return lax.ppermute(block, 'section', route)  2.69 us
    pallas_call x1, Pallas kernels, on_device(): call(functools.partial(expert_backward, devices), outs, [VMEM] * (devices...  1.99 us
    pallas_call x1, Pallas kernels, on_device(): call(dispatch, [bf16((3 * CAP, width))] * 2 + [jax.ShapeDtypeStruct((n, t...  1.81 us
    pallas_call x1, Pallas kernels, on_device(): call(functools.partial(expert_forward, devices), outs + [factor] * 2, [VM...  1.69 us
  transfers between devices with their start and end apart: 11, of which 5 were waited for; matrix products, arithmetic and copies ran while one was open for 0% of the time, Pallas kernels for 24%

profile of v8, /device:TPU:0, one launch (start us, length us, event | category | flops | bytes accessed | tf_op | source)
XLA Modules:
  0.0 40.4 jit_solution(7850365021123104376)
XLA Ops:
  0.6 1.8 %shard_map.122 = (bf16[48,2048]{1,0:T(8,128)(2,1)S(1)}, bf16[48,2048]{1,0:T(8,128)(2,1)S(1)}, f32[40,128]{1,0:T(8,128)S(1)}, f32[32,128]{1,0:T(8,128)S(1)}) custom-call(s32[1]{0:T(128)} %bitcast.owner_ref, s32[1,8,128]{2,1,0:T(8,128)} %bitcast.5, f32[1,8,128]{2,1,0:T(8,128)} %bitcast.6, s32[1,8,128]{2,1,0:T(8,128)} %bitcast.7, f32[1,8,128]{2,1,0:T(8,128)} %bitcast.8, ...), custom_call_target="tpu_custom_call" | custom-call | flops 50331648 | bytes 1572864 | tf_op jit(solution)/shard_map/pallas_call | solution.py:298
  2.5 4.1 %collective-permute-start.1 = (bf16[48,2048]{1,0:T(8,128)(2,1)S(1)}, bf16[48,2048]{1,0:T(8,128)(2,1)S(1)}, u32[]{:S(2)}, u32[]{:S(2)}) collective-permute-start(bf16[48,2048]{1,0:T(8,128)(2,1)S(1)} %get-tuple-element.36), channel_id=1, source_target_pairs={{0,2},{1,3},{2,0},{3,1},{4,6},{5,7},{6,4},{7,5},{8,10},{9,11},{10,... | collective-permute-start | bytes 589832 | tf_op jit(solution)/shard_map/ppermute | solution.py:269
  6.6 1.6 %collective-permute-start.2 = (bf16[48,2048]{1,0:T(8,128)(2,1)S(1)}, bf16[48,2048]{1,0:T(8,128)(2,1)S(1)}, u32[]{:S(2)}, u32[]{:S(2)}) collective-permute-start(bf16[48,2048]{1,0:T(8,128)(2,1)S(1)} %get-tuple-element.44.refs_0_), channel_id=1, source_target_pairs={{0,1},{1,0},{2,3},{3,2},{4,5},{5,4},{6,7},{7,6},{8,9},{9,8},{10,11... | collective-permute-start | bytes 589832 | tf_op jit(solution)/shard_map/ppermute | solution.py:269
  8.1 0.0 copy-start
  8.1 4.6 %shard_map.123 = (bf16[128,2176]{1,0:T(8,128)(2,1)S(1)}, bf16[128,2176]{1,0:T(8,128)(2,1)S(1)}, bf16[1,768,2048]{2,1,0:T(8,128)(2,1)S(1)}, bf16[1,768,2048]{2,1,...) custom-call(bf16[1,128,2048]{2,1,0:T(8,128)(2,1)} %rows_f.1, ...), custom_call_target="tpu_custom_call" | custom-call | bytes 37748736 | tf_op jit(solution)/shard_map/pallas_call | solution.py:313
  12.8 0.1 collective-permute-start
  12.8 2.6 %collective-permute-start.7 = (bf16[128,2176]{1,0:T(8,128)(2,1)S(1)}, bf16[128,2176]{1,0:T(8,128)(2,1)S(1)}, u32[]{:S(2)}, u32[]{:S(2)}) collective-permute-start(bf16[128,2176]{1,0:T(8,128)(2,1)S(1)} %get-tuple-element.54), channel_id=1, source_target_pairs={{0,28},{4,0},{8,4},{12,8},{16,12},{20,16},{24,20},{28,24},{1,29},{... | collective-permute-start | bytes 1671176 | tf_op jit(solution)/shard_map/ppermute | solution.py:273
  15.4 0.3 collective-permute-done.1.refs_2_
  15.8 0.2 collective-permute-done.2.refs_1_
  16.0 1.5 %collective-permute-start.3 = (bf16[48,2048]{1,0:T(8,128)(2,1)S(1)}, bf16[48,2048]{1,0:T(8,128)(2,1)S(1)}, u32[]{:S(2)}, u32[]{:S(2)}) collective-permute-start(bf16[48,2048]{1,0:T(8,128)(2,1)S(1)} %collective-permute-done.1.refs_2_), channel_id=1, source_target_pairs={{0,1},{1,0},{2,3},{3,2},{4,5},{5,4},{6,7},{7,6},{8,9},{9,8},{10,11... | collective-permute-start | bytes 589832 | tf_op jit(solution)/shard_map/ppermute | solution.py:269
  17.5 4.4 %collective-permute-done.3.refs_3_ = bf16[48,2048]{1,0:T(8,128)(2,1)S(1)} collective-permute-done((bf16[48,2048]{1,0:T(8,128)(2,1)S(1)}, bf16[48,2048]{1,0:T(8,128)(2,1)S(1)}, u32[]{:S(2)}, u32[]{:S(2)}) %collective-permute-start.3) | collective-permute-done | bytes 196640 | tf_op jit(solution)/shard_map/ppermute | solution.py:269
  21.8 0.0 copy-done
  21.8 1.7 %shard_map.124 = (bf16[32,2048]{1,0:T(8,128)(2,1)S(1)}, bf16[32,2048]{1,0:T(8,128)(2,1)S(1)}, f32[64,768]{1,0:T(8,128)S(1)}, f32[64,768]{1,0:T(8,128)S(1)}) custom-call(bf16[48,2048]{1,0:T(8,128)(2,1)S(1)} %get-tuple-element.44.refs_0_, bf16[48,2048]{1,0:T(8,128)(2,1)S(1)} %collective-permute-done.2.refs_1_, ...), custom_call_target="tpu_custom_call" | custom-call | flops 1006632960 | bytes 9437184 | tf_op jit(solution)/shard_map/pallas_call | solution.py:339
  23.5 1.5 %collective-permute-start.4 = (bf16[32,2048]{1,0:T(8,128)(2,1)S(1)}, bf16[32,2048]{1,0:T(8,128)(2,1)S(1)}, u32[]{:S(2)}, u32[]{:S(2)}) collective-permute-start(bf16[32,2048]{1,0:T(8,128)(2,1)S(1)} %get-tuple-element.51), channel_id=1, source_target_pairs={{0,1},{1,0},{2,3},{3,2},{4,5},{5,4},{6,7},{7,6},{8,9},{9,8},{10,11... | collective-permute-start | bytes 393224 | tf_op jit(solution)/shard_map/ppermute | solution.py:269
  25.0 2.0 %shard_map.127 = (bf16[32,2048]{1,0:T(8,128)(2,1)S(1)}, bf16[32,2048]{1,0:T(8,128)(2,1)S(1)}) custom-call(bf16[48,2048]{1,0:T(8,128)(2,1)S(1)} %get-tuple-element.44.refs_0_, bf16[48,2048]{1,0:T(8,128)(2,1)S(1)} %collective-permute-done.2.refs_1_, bf16[48,2048]{1,0:T(8,128)(2,1)S(1)} %collective-permute-done.1.refs_2_, ...), custom_call_target="tpu_custom_call" | custom-call | flops 603979776 | bytes 9437184 | tf_op jit(solution)/shard_map/pallas_call | solution.py:347
  27.0 0.7 %collective-permute-start.8 = (bf16[32,2048]{1,0:T(8,128)(2,1)S(1)}, bf16[32,2048]{1,0:T(8,128)(2,1)S(1)}, u32[]{:S(2)}, u32[]{:S(2)}) collective-permute-start(bf16[32,2048]{1,0:T(8,128)(2,1)S(1)} %get-tuple-element.61), channel_id=1, source_target_pairs={{0,1},{1,0},{2,3},{3,2},{4,5},{5,4},{6,7},{7,6},{8,9},{9,8},{10,11... | collective-permute-start | bytes 393224 | tf_op jit(solution)/shard_map/ppermute | solution.py:269
  27.7 2.0 %collective-permute-done.4.received_ref = bf16[32,2048]{1,0:T(8,128)(2,1)S(1)} collective-permute-done((bf16[32,2048]{1,0:T(8,128)(2,1)S(1)}, bf16[32,2048]{1,0:T(8,128)(2,1)S(1)}, u32[]{:S(2)}, u32[]{:S(2)}) %collective-permute-start.4) | collective-permute-done | bytes 131104 | tf_op jit(solution)/shard_map/ppermute | solution.py:269
  29.7 0.1 collective-permute-start.5
  29.8 3.3 %collective-permute-start.6 = (bf16[16,2048]{1,0:T(8,128)(2,1)S(1)}, bf16[16,2048]{1,0:T(8,128)(2,1)S(1)}, u32[]{:S(2)}, u32[]{:S(2)}) collective-permute-start(bf16[16,2048]{1,0:T(8,128)(2,1)S(1)} %get-tuple-element.53), channel_id=1, source_target_pairs={{0,6},{1,7},{2,4},{3,5},{4,10},{5,11},{6,8},{7,9},{8,14},{9,15},{1... | collective-permute-start | bytes 196616 | tf_op jit(solution)/shard_map/ppermute | solution.py:281
  33.0 0.0 collective-permute-done.8.received_ref
  33.1 1.0 %collective-permute-start.9 = (bf16[16,2048]{1,0:T(8,128)(2,1)S(1)}, bf16[16,2048]{1,0:T(8,128)(2,1)S(1)}, u32[]{:S(2)}, u32[]{:S(2)}) collective-permute-start(bf16[16,2048]{1,0:T(8,128)(2,1)S(1)} %get-tuple-element.62), channel_id=1, source_target_pairs={{0,28},{1,29},{2,30},{3,31},{4,0},{5,1},{6,2},{7,3},{8,4},{9,5},{1... | collective-permute-start | bytes 196616 | tf_op jit(solution)/shard_map/ppermute | solution.py:281
  34.1 0.0 collective-permute-done.early_ref
  34.1 3.4 %collective-permute-start.10 = (bf16[16,2048]{1,0:T(8,128)(2,1)S(1)}, bf16[16,2048]{1,0:T(8,128)(2,1)S(1)}, u32[]{:S(2)}, u32[]{:S(2)}) collective-permute-start(bf16[16,2048]{1,0:T(8,128)(2,1)S(1)} %get-tuple-element.63), channel_id=1, source_target_pairs={{0,30},{1,31},{2,28},{3,29},{4,2},{5,3},{6,0},{7,1},{8,6},{9,7},{1... | collective-permute-start | bytes 196616 | tf_op jit(solution)/shard_map/ppermute | solution.py:281
  37.5 0.0 collective-permute-done.5.own_ref
  37.5 0.0 collective-permute-done.6.other_ref
  37.5 1.2 %shard_map.126 = bf16[1,128,2048]{2,1,0:T(8,128)(2,1)} custom-call(bf16[128,2176]{1,0:T(8,128)(2,1)S(1)} %collective-permute-done.early_ref, bf16[16,2048]{1,0:T(8,128)(2,1)S(1)} %collective-permute-done.5.own_ref, bf16[16,2048]{1,0:T(8,128)(2,1)S(1)} %collective-permute-done.6.other_ref), custom_call_target="tpu_custom_call" | custom-call | flops 16777216 | bytes 1572864 | tf_op jit(solution)/shard_map/pallas_call | solution.py:376
  38.7 0.0 collective-permute-done.7.early_ref
  38.7 0.0 collective-permute-done.9.own_ref
  38.7 0.7 %collective-permute-done.10.other_ref = bf16[16,2048]{1,0:T(8,128)(2,1)S(1)} collective-permute-done((bf16[16,2048]{1,0:T(8,128)(2,1)S(1)}, bf16[16,2048]{1,0:T(8,128)(2,1)S(1)}, u32[]{:S(2)}, u32[]{:S(2)}) %collective-permute-start.10) | collective-permute-done | bytes 65568 | tf_op jit(solution)/shard_map/ppermute | solution.py:281
  39.4 1.0 %shard_map.129 = bf16[1,128,2048]{2,1,0:T(8,128)(2,1)} custom-call(bf16[128,2176]{1,0:T(8,128)(2,1)S(1)} %collective-permute-done.7.early_ref, bf16[16,2048]{1,0:T(8,128)(2,1)S(1)} %collective-permute-done.9.own_ref, bf16[16,2048]{1,0:T(8,128)(2,1)S(1)} %collective-permute-done.10.other_ref), custom_call_target="tpu_custom_call" | custom-call | flops 16777216 | bytes 1572864 | tf_op jit(solution)/shard_map/pallas_call | solution.py:379
  (2 shorter events, 0.1 us)
Async XLA Ops:
  2.5 13.3 %collective-permute-start.1 = (bf16[48,2048]{1,0:T(8,128)(2,1)S(1)}, bf16[48,2048]{1,0:T(8,128)(2,1)S(1)}, u32[]{:S(2)}, u32[]{:S(2)}) collective-permute-start(bf16[48,2048]{1,0:T(8,128)(2,1)S(1)} %get-tuple-element.36), channel_id=1, source_target_pairs={{0,2},{1,3},{2,0},{3,1},{4,6},{5,7},{6,4},{7,5},{8,10},{9,11},{10,... | collective-permute-start | bytes 589832 | tf_op jit(solution)/shard_map/ppermute | solution.py:269
  6.6 9.4 %collective-permute-start.2 = (bf16[48,2048]{1,0:T(8,128)(2,1)S(1)}, bf16[48,2048]{1,0:T(8,128)(2,1)S(1)}, u32[]{:S(2)}, u32[]{:S(2)}) collective-permute-start(bf16[48,2048]{1,0:T(8,128)(2,1)S(1)} %get-tuple-element.44.refs_0_), channel_id=1, source_target_pairs={{0,1},{1,0},{2,3},{3,2},{4,5},{5,4},{6,7},{7,6},{8,9},{9,8},{10,11... | collective-permute-start | bytes 589832 | tf_op jit(solution)/shard_map/ppermute | solution.py:269
  8.1 13.7 %copy-start = (f32[1,2048]{1,0:T(1,128)S(1)}, f32[1,2048]{1,0:T(1,128)}, u32[]{:S(2)}) copy-start(f32[1,2048]{1,0:T(1,128)} %refs_4_.5) | copy-start | bytes 24580
  12.8 21.3 %collective-permute-start = (bf16[128,2176]{1,0:T(8,128)(2,1)S(1)}, bf16[128,2176]{1,0:T(8,128)(2,1)S(1)}, u32[]{:S(2)}, u32[]{:S(2)}) collective-permute-start(bf16[128,2176]{1,0:T(8,128)(2,1)S(1)} %get-tuple-element.35), channel_id=1, source_target_pairs={{0,4},{4,8},{8,12},{12,16},{16,20},{20,24},{24,28},{28,0},{1,5},{5... | collective-permute-start | bytes 1671176 | tf_op jit(solution)/shard_map/ppermute | solution.py:273
  12.8 25.9 %collective-permute-start.7 = (bf16[128,2176]{1,0:T(8,128)(2,1)S(1)}, bf16[128,2176]{1,0:T(8,128)(2,1)S(1)}, u32[]{:S(2)}, u32[]{:S(2)}) collective-permute-start(bf16[128,2176]{1,0:T(8,128)(2,1)S(1)} %get-tuple-element.54), channel_id=1, source_target_pairs={{0,28},{4,0},{8,4},{12,8},{16,12},{20,16},{24,20},{28,24},{1,29},{... | collective-permute-start | bytes 1671176 | tf_op jit(solution)/shard_map/ppermute | solution.py:273
  16.0 5.8 %collective-permute-start.3 = (bf16[48,2048]{1,0:T(8,128)(2,1)S(1)}, bf16[48,2048]{1,0:T(8,128)(2,1)S(1)}, u32[]{:S(2)}, u32[]{:S(2)}) collective-permute-start(bf16[48,2048]{1,0:T(8,128)(2,1)S(1)} %collective-permute-done.1.refs_2_), channel_id=1, source_target_pairs={{0,1},{1,0},{2,3},{3,2},{4,5},{5,4},{6,7},{7,6},{8,9},{9,8},{10,11... | collective-permute-start | bytes 589832 | tf_op jit(solution)/shard_map/ppermute | solution.py:269
  23.5 6.2 %collective-permute-start.4 = (bf16[32,2048]{1,0:T(8,128)(2,1)S(1)}, bf16[32,2048]{1,0:T(8,128)(2,1)S(1)}, u32[]{:S(2)}, u32[]{:S(2)}) collective-permute-start(bf16[32,2048]{1,0:T(8,128)(2,1)S(1)} %get-tuple-element.51), channel_id=1, source_target_pairs={{0,1},{1,0},{2,3},{3,2},{4,5},{5,4},{6,7},{7,6},{8,9},{9,8},{10,11... | collective-permute-start | bytes 393224 | tf_op jit(solution)/shard_map/ppermute | solution.py:269
  27.0 6.0 %collective-permute-start.8 = (bf16[32,2048]{1,0:T(8,128)(2,1)S(1)}, bf16[32,2048]{1,0:T(8,128)(2,1)S(1)}, u32[]{:S(2)}, u32[]{:S(2)}) collective-permute-start(bf16[32,2048]{1,0:T(8,128)(2,1)S(1)} %get-tuple-element.61), channel_id=1, source_target_pairs={{0,1},{1,0},{2,3},{3,2},{4,5},{5,4},{6,7},{7,6},{8,9},{9,8},{10,11... | collective-permute-start | bytes 393224 | tf_op jit(solution)/shard_map/ppermute | solution.py:269
  29.7 7.8 %collective-permute-start.5 = (bf16[16,2048]{1,0:T(8,128)(2,1)S(1)}, bf16[16,2048]{1,0:T(8,128)(2,1)S(1)}, u32[]{:S(2)}, u32[]{:S(2)}) collective-permute-start(bf16[16,2048]{1,0:T(8,128)(2,1)S(1)} %get-tuple-element.52), channel_id=1, source_target_pairs={{0,4},{1,5},{2,6},{3,7},{4,8},{5,9},{6,10},{7,11},{8,12},{9,13},{1... | collective-permute-start | bytes 196616 | tf_op jit(solution)/shard_map/ppermute | solution.py:281
  29.8 7.7 %collective-permute-start.6 = (bf16[16,2048]{1,0:T(8,128)(2,1)S(1)}, bf16[16,2048]{1,0:T(8,128)(2,1)S(1)}, u32[]{:S(2)}, u32[]{:S(2)}) collective-permute-start(bf16[16,2048]{1,0:T(8,128)(2,1)S(1)} %get-tuple-element.53), channel_id=1, source_target_pairs={{0,6},{1,7},{2,4},{3,5},{4,10},{5,11},{6,8},{7,9},{8,14},{9,15},{1... | collective-permute-start | bytes 196616 | tf_op jit(solution)/shard_map/ppermute | solution.py:281
  33.1 5.6 %collective-permute-start.9 = (bf16[16,2048]{1,0:T(8,128)(2,1)S(1)}, bf16[16,2048]{1,0:T(8,128)(2,1)S(1)}, u32[]{:S(2)}, u32[]{:S(2)}) collective-permute-start(bf16[16,2048]{1,0:T(8,128)(2,1)S(1)} %get-tuple-element.62), channel_id=1, source_target_pairs={{0,28},{1,29},{2,30},{3,31},{4,0},{5,1},{6,2},{7,3},{8,4},{9,5},{1... | collective-permute-start | bytes 196616 | tf_op jit(solution)/shard_map/ppermute | solution.py:281
  34.1 5.3 %collective-permute-start.10 = (bf16[16,2048]{1,0:T(8,128)(2,1)S(1)}, bf16[16,2048]{1,0:T(8,128)(2,1)S(1)}, u32[]{:S(2)}, u32[]{:S(2)}) collective-permute-start(bf16[16,2048]{1,0:T(8,128)(2,1)S(1)} %get-tuple-element.63), channel_id=1, source_target_pairs={{0,30},{1,31},{2,28},{3,29},{4,2},{5,3},{6,0},{7,1},{8,6},{9,7},{1... | collective-permute-start | bytes 196616 | tf_op jit(solution)/shard_map/ppermute | solution.py:281
